TPU v7x, 32 devices: a whole 2x2x4 slice. The times are simulated.
32 devices in a mesh: head: 4 (over x, core), tensor: 4 (over z), dp: 2 (over y).
Axes of the slice: x: 2, y: 2, z: 4, core: 2. Of those that a mesh axis runs over, the one named last changes fastest.
Arguments:
- trunk_hidden: bfloat16 [96, 5120], P('dp', 'tensor'), may hold values from -60 to 60
- next_embeds: bfloat16 [4, 96, 5120], P('head', 'dp', 'tensor'), may hold values from -6 to 6
- combine_weight: bfloat16 [4, 10240, 5120], P('head', 'dp', 'tensor'), may hold values from -0.0625 to 0.0625
- final_gain: float32 [5120], P('tensor'), may hold values from 0.5 to 1.5
- unembed_weight: bfloat16 [16384, 5120], P('dp', 'tensor'), may hold values from -32 to 32
- target_ids: int32 [4, 96], P('head'), may hold values from 0 to 16383
- loss_scale: float32 [4, 96], P('head'), may hold values from 2 to 32
Outputs:
- trunk_grad: float32 [96, 5120], P('dp', 'tensor')
- embed_grad: float32 [4, 96, 5120], P('head', 'dp', 'tensor')
- combine_grad: float32 [4, 10240, 5120], P('head', 'dp', 'tensor')
- unembed_grad: float32 [2, 4, 2048, 5120], P('dp', 'head', None, 'tensor')
All inputs are finite; a program needn't handle non-finite values.
Results may differ from a plain program's by a relative error of at most 0.02.
Values may be sent and summed in bfloat16 or wider, within the bound.
No kernel may reach another device: no remote copies, remote signals or barrier semaphores. Data moves between devices by JAX's collectives and lax.ppermute only.
A program may use at most 192 MiB of HBM per device.

v0:
```python
import jax
import jax.numpy as jnp
from jax import lax
from jax.sharding import PartitionSpec as P

D = 5120


epsilon = 1e-05


def contract_rows(left, right):
    return lax.dot_general(
        left, right, (((0,), (0,)), ((), ())), preferred_element_type=jnp.float32
    )


def contract_cols(left, right):
    return lax.dot_general(
        left, right, (((1,), (1,)), ((), ())), preferred_element_type=jnp.float32
    )


def local(
    trunk_hidden, next_embeds, combine_weight, final_gain, unembed_weight, target_ids, loss_scale
):
    rows, part_width = trunk_hidden.shape
    vocab_part = unembed_weight.shape[0]
    weight_block = combine_weight[0]
    trunk_whole, embed_whole = (
        lax.all_gather(trunk_hidden, "tensor", axis=1, tiled=True),
        lax.all_gather(next_embeds[0], "tensor", axis=1, tiled=True),
    )
    trunk_float = trunk_whole.astype(jnp.float32)
    embed_float = embed_whole.astype(jnp.float32)
    trunk_scale = lax.rsqrt(jnp.sum(trunk_float * trunk_float, axis=1) / D + epsilon)
    embed_scale = lax.rsqrt(jnp.sum(embed_float * embed_float, axis=1) / D + epsilon)
    trunk_normed = trunk_float * trunk_scale[:, None]
    embed_normed = embed_float * embed_scale[:, None]
    joined = jnp.concatenate(
        [trunk_normed.astype(jnp.bfloat16), embed_normed.astype(jnp.bfloat16)], axis=1
    )
    feature_start = lax.axis_index("tensor") * part_width
    trunk_local = lax.dynamic_slice_in_dim(trunk_normed, feature_start, part_width, 1)
    embed_local = lax.dynamic_slice_in_dim(embed_normed, feature_start, part_width, 1)
    blocks = lax.all_to_all(joined, "dp", split_axis=1, concat_axis=0, tiled=True)
    projected = lax.psum_scatter(
        jnp.dot(blocks, weight_block, preferred_element_type=jnp.float32).astype(jnp.bfloat16),
        "dp",
        scatter_dimension=0,
        tiled=True,
    ).astype(jnp.float32)
    mixed = trunk_hidden.astype(jnp.float32) + projected
    mixed_sums = lax.psum(jnp.sum(mixed * mixed, axis=1), "tensor")
    mixed_scale = lax.rsqrt(mixed_sums / D + epsilon)
    mixed_normed = mixed * mixed_scale[:, None]
    normed_out = (mixed_normed * final_gain[None, :]).astype(jnp.bfloat16)
    normed_all = lax.all_gather(normed_out, "dp", axis=0, tiled=True)
    partial_logits = contract_cols(normed_all, unembed_weight)
    logits = lax.psum(partial_logits, "tensor")
    row_targets = target_ids[0]
    row_weights = loss_scale[0]
    largest = lax.pmax(jnp.max(logits, axis=1), "dp")
    shifted = jnp.exp(logits - largest[:, None])
    summed = lax.psum(jnp.sum(shifted, axis=1), "dp")
    probs = shifted / summed[:, None]
    vocab_ids = (
        lax.broadcasted_iota(jnp.int32, (1, vocab_part), 1) + lax.axis_index("dp") * vocab_part
    )
    hits = (vocab_ids == row_targets[:, None]).astype(jnp.float32)
    grad_local = (row_weights[:, None] * (probs - hits)).astype(jnp.bfloat16)
    grad_normed = lax.psum_scatter(
        jnp.dot(grad_local, unembed_weight, preferred_element_type=jnp.float32).astype(
            jnp.bfloat16
        ),
        "dp",
        scatter_dimension=0,
        tiled=True,
    ).astype(jnp.float32)
    vocab_term = contract_rows(grad_local, normed_all).astype(jnp.bfloat16)
    vocab_total = lax.psum_scatter(vocab_term, "head", scatter_dimension=0, tiled=True).astype(
        jnp.float32
    )
    unembed_grad = vocab_total.reshape(1, 1, vocab_total.shape[0], part_width)
    scaled_grad = grad_normed * final_gain[None, :]
    grad_dots = lax.psum(jnp.sum(scaled_grad * mixed_normed, axis=1), "tensor")
    grad_mixed = mixed_scale[:, None] * (scaled_grad - mixed_normed * (grad_dots / D)[:, None])
    grad_mixed_low = grad_mixed.astype(jnp.bfloat16)
    grad_all = lax.all_gather(grad_mixed_low, "dp", axis=0, tiled=True)
    combine_grad = contract_rows(blocks, grad_all)[None]
    joined_part = lax.all_to_all(
        contract_cols(grad_all, weight_block).astype(jnp.bfloat16),
        "dp",
        split_axis=0,
        concat_axis=1,
        tiled=True,
    ).astype(jnp.float32)
    joined_grad = lax.psum_scatter(
        joined_part.reshape(rows, 2, D).astype(jnp.bfloat16),
        "tensor",
        scatter_dimension=2,
        tiled=True,
    ).astype(jnp.float32)
    trunk_side = joined_grad[:, 0]
    embed_side = joined_grad[:, 1]
    trunk_dots, embed_dots = lax.psum(
        (jnp.sum(trunk_side * trunk_local, axis=1), jnp.sum(embed_side * embed_local, axis=1)),
        "tensor",
    )
    trunk_term = trunk_scale[:, None] * (trunk_side - trunk_local * (trunk_dots / D)[:, None])
    embed_grad = (embed_scale[:, None] * (embed_side - embed_local * (embed_dots / D)[:, None]))[
        None
    ]
    trunk_grad = lax.psum((grad_mixed + trunk_term).astype(jnp.bfloat16), "head").astype(
        jnp.float32
    )
    return (trunk_grad, embed_grad, combine_grad, unembed_grad)


def solution(mesh):
    in_specs = (
        P("dp", "tensor"),
        P("head", "dp", "tensor"),
        P("head", "dp", "tensor"),
        P("tensor"),
        P("dp", "tensor"),
        P("head", None),
        P("head", None),
    )
    out_specs = (
        P("dp", "tensor"),
        P("head", "dp", "tensor"),
        P("head", "dp", "tensor"),
        P("dp", "head", None, "tensor"),
    )
    return jax.shard_map(local, mesh=mesh, in_specs=in_specs, out_specs=out_specs, check_vma=False)
```

profile of v0, /device:TPU:0, one launch (start us, length us, event | category | flops | bytes accessed | tf_op | source)
XLA Modules:
  0.0 543.3 jit_solution(3018210545732555088)
XLA Ops:
  7.2 0.0 reduce-scatter.5.cloned.1.call-start
  7.2 17.2 %all-gather = bf16[1,48,5120]{2,1,0:T(8,128)(2,1)S(1)} all-gather(bf16[1,48,1280]{2,1,0:T(8,128)(2,1)} %param.8), channel_id=2, replica_groups=mesh['head'=4,'tensor'=4,'dp'=2] {'tensor'}, dimensions={2}, use_global_device_ids=true | all-gather | bytes 614400 | tf_op jit(solution)/shard_map/all_gather | solution.py:32
  24.4 0.2 fusion.12
  24.6 16.1 %all_gather.12 = bf16[48,5120]{1,0:T(8,128)(2,1)S(1)} all-gather(bf16[48,1280]{1,0:T(8,128)(2,1)} %param.7), channel_id=1, replica_groups=mesh['head'=4,'tensor'=4,'dp'=2] {'tensor'}, dimensions={1}, use_global_device_ids=true | all-gather | bytes 614400 | tf_op jit(solution)/shard_map/all_gather | solution.py:31
  40.7 0.2 fusion.11
  41.0 1.1 convert_multiply_fusion.2
  42.1 1.1 convert_multiply_fusion
  43.2 0.1 pad_maximum_fusion
  43.3 0.1 copy.14
  43.4 11.6 %all_to_all.35 = bf16[48,2,5120]{2,0,1:T(8,128)(2,1)S(1)} all-to-all(bf16[48,2,5120]{2,0,1:T(8,128)(2,1)S(1)} %bitcast.57), channel_id=1, replica_groups=mesh['head'=4,'tensor'=4,'dp'=2] {'dp'}, dimensions={1} | all-to-all | bytes 1966080 | tf_op jit(solution)/shard_map/all_to_all | solution.py:46
  55.0 0.9 copy-done.1
  55.9 7.6 %fusion.8 = bf16[96,1280]{1,0:T(8,128)(2,1)} fusion(bf16[96,5120]{1,0:T(8,128)(2,1)S(1)} %bitcast.53, bf16[1,5120,1280]{2,1,0:T(8,128)(2,1)} %param.9), kind=kOutput, calls=%fused_computation.11 | convolution fusion | flops 1258414080 | bytes 14336000 | tf_op jit(solution)/shard_map/dot_general | solution.py:48
  63.6 0.0 reduce-scatter.5.cloned.1.call-update
  63.6 0.0 all-reduce.4.cloned.1.call-start
  63.7 12.1 %reduce-scatter.5.cloned.1.call-done = bf16[48,1280]{1,0:T(8,128)(2,1)} async-done(((bf16[96,1280]{1,0:T(8,128)(2,1)}), bf16[48,1280]{1,0:T(8,128)(2,1)}) %reduce-scatter.5.cloned.1.call-update) | async-done | bytes 122896 | tf_op jit(solution)/shard_map/reduce_scatter | solution.py:47
  75.8 1.0 multiply_reduce_fusion.3
  76.8 11.7 %psum.49 = f32[48]{0:T(128)S(1)} all-reduce(f32[48]{0:T(128)S(1)} %multiply_reduce_fusion.3), channel_id=1, replica_groups=mesh['head'=4,'tensor'=4,'dp'=2] {'tensor'}, use_global_device_ids=true, to_apply=%region_4.0 | all-reduce | flops 48 | bytes 384 | tf_op jit(solution)/shard_map/psum | solution.py:54
  88.6 1.0 multiply_convert_fusion.1
  89.6 5.6 %all_gather.14 = bf16[96,1280]{1,0:T(8,128)(2,1)S(1)} all-gather(bf16[48,1280]{1,0:T(8,128)(2,1)S(1)} %multiply_convert_fusion.1), channel_id=1, replica_groups=mesh['head'=4,'tensor'=4,'dp'=2] {'dp'}, dimensions={0}, use_global_device_ids=true | all-gather | bytes 368640 | tf_op jit(solution)/shard_map/all_gather | solution.py:58
  95.1 0.7 copy-done.8
  95.8 12.4 %fusion.17 = f32[96,8192]{1,0:T(8,128)} fusion(bf16[96,1280]{1,0:T(8,128)(2,1)S(1)} %all_gather.14, bf16[8192,1280]{1,0:T(8,128)(2,1)} %param.11), kind=kOutput, calls=%fused_computation.44 | convolution fusion | flops 2013265920 | bytes 24363008 | tf_op jit(solution)/shard_map/dot_general | solution.py:19
  108.2 0.0 all-reduce.4.cloned.1.call-update
  108.2 0.0 reduce-scatter.7.cloned.1.call-start
  108.3 0.0 copy-start.13
  108.3 0.0 copy-start.14
  108.3 118.4 %all-reduce.4.cloned.1.call-done = f32[96,8192]{1,0:T(8,128)} async-done(((f32[96,8192]{1,0:T(8,128)}), f32[96,8192]{1,0:T(8,128)}) %all-reduce.4.cloned.1.call-update) | async-done | bytes 3145744 | tf_op jit(solution)/shard_map/psum | solution.py:60
  226.7 2.3 reduce_max.9
  229.0 4.9 pmax.7
  234.0 0.6 fusion.7
  234.6 4.9 psum.51
  239.5 0.0 copy-done.14
  239.5 11.4 %convolution_convert_fusion.1 = bf16[96,1280]{1,0:T(8,128)(2,1)} fusion(bf16[8192,1280]{1,0:T(8,128)(2,1)} %param.11, f32[96,8192]{1,0:T(8,128)S(1)} %copy-done, s32[8192]{0:T(1024)S(1)} %iota_add_fusion, f32[96]{0:T(128)S(1)} %psum.51, f32[96]{0:T(128)S(1)} %pmax.7, f32[96]{0:T(128)S(1)} %bitcast.60, s32[96]{0:T(128)S(1)} %bitcast.62), kind=kOutput, calls=%fused_computation.12 | convolution fusion | flops 2018893824 | bytes 24397312 | tf_op jit(solution)/shard_map/dot_general | solution.py:73
  250.9 0.0 copy-done.11
  250.9 0.0 reduce-scatter.7.cloned.1.call-update
  251.0 0.0 reduce-scatter.9.cloned.1.call-start
  251.0 10.6 %reduce-scatter.7.cloned.1.call-done = bf16[48,1280]{1,0:T(8,128)(2,1)} async-done(((bf16[96,1280]{1,0:T(8,128)(2,1)}), bf16[48,1280]{1,0:T(8,128)(2,1)}) %reduce-scatter.7.cloned.1.call-update) | async-done | bytes 122896 | tf_op jit(solution)/shard_map/reduce_scatter | solution.py:72
  261.6 0.0 copy-done.5
  261.6 1.1 multiply_reduce_fusion.2
  262.7 11.7 %psum.52 = f32[48]{0:T(128)S(1)} all-reduce(f32[48]{0:T(128)S(1)} %multiply_reduce_fusion.2), channel_id=1, replica_groups=mesh['head'=4,'tensor'=4,'dp'=2] {'tensor'}, use_global_device_ids=true, to_apply=%region_12.0 | all-reduce | flops 48 | bytes 384 | tf_op jit(solution)/shard_map/psum | solution.py:86
  274.4 1.0 fusion.14
  275.4 5.7 %all_gather.15 = bf16[96,1280]{1,0:T(8,128)(2,1)S(1)} all-gather(bf16[48,1280]{1,0:T(8,128)(2,1)S(1)} %fusion.14), channel_id=1, replica_groups=mesh['head'=4,'tensor'=4,'dp'=2] {'dp'}, dimensions={0}, use_global_device_ids=true | all-gather | bytes 368640 | tf_op jit(solution)/shard_map/all_gather | solution.py:89
  281.2 8.9 %fusion.4 = bf16[96,5120]{1,0:T(8,128)(2,1)S(1)} fusion(bf16[96,1280]{1,0:T(8,128)(2,1)S(1)} %all_gather.15, bf16[1,5120,1280]{2,1,0:T(8,128)(2,1)} %param.9), kind=kOutput, calls=%fused_computation.6 | convolution fusion | flops 1258782720 | bytes 14336000 | tf_op jit(solution)/shard_map/dot_general | solution.py:19
  290.1 13.3 %all_to_all.36 = bf16[2,48,5120]{2,1,0:T(8,128)(2,1)} all-to-all(bf16[2,48,5120]{2,1,0:T(8,128)(2,1)S(1)} %bitcast.58), channel_id=1, replica_groups=mesh['head'=4,'tensor'=4,'dp'=2] {'dp'}, dimensions={0} | all-to-all | bytes 1966080 | tf_op jit(solution)/shard_map/all_to_all | solution.py:91
  303.4 0.0 reduce-scatter.9.cloned.1.call-update
  303.4 0.0 all-reduce.6.cloned.1.call-start
  303.5 23.4 %reduce-scatter.9.cloned.1.call-done = bf16[48,2,1280]{2,0,1:T(8,128)(2,1)} async-done(((bf16[48,2,5120]{2,0,1:T(8,128)(2,1)}), bf16[48,2,1280]{2,0,1:T(8,128)(2,1)}) %reduce-scatter.9.cloned.1.call-update) | async-done | bytes 245776 | tf_op jit(solution)/shard_map/reduce_scatter | solution.py:98
  326.9 1.0 convert_element_type.72
  327.9 0.0 copy-start.3
  327.9 0.8 copy-done.3
  328.7 1.8 multiply_reduce_fusion
  330.5 10.0 %all-reduce = (f32[48]{0:T(128)}, f32[48]{0:T(128)}) all-reduce(f32[48]{0:T(128)} %get-tuple-element.5, f32[48]{0:T(128)} %get-tuple-element.4), channel_id=1, replica_groups=mesh['head'=4,'tensor'=4,'dp'=2] {'tensor'}, use_global_device_ids=true, to_apply=%region_15.0 | all-reduce | flops 96 | bytes 768 | tf_op jit(solution)/shard_map/psum | solution.py:106
  340.5 0.7 broadcast_multiply_fusion
  341.1 2.3 multiply_bitcast_fusion
  343.4 0.0 all-reduce.6.cloned.1.call-update
  343.4 0.0 reduce-scatter.11.cloned.1.call-start
  343.5 11.2 %convolution_convert_fusion = bf16[8192,1280]{1,0:T(8,128)(2,1)} fusion(bf16[96,1280]{1,0:T(8,128)(2,1)} %copy-done.8, f32[96,8192]{1,0:T(8,128)S(1)} %copy-done, s32[8192]{0:T(1024)S(1)} %iota_add_fusion, f32[96]{0:T(128)} %copy-done.15, f32[96]{0:T(128)} %copy-done.11, f32[96]{0:T(128)} %bitcast.59, s32[96]{0:T(128)} %bitcast.61), kind=kOutput, calls=%fused_computation | convolution fusion | flops 2029256704 | bytes 24397312 | tf_op jit(solution)/shard_map/dot_general | solution.py:13
  354.7 0.0 reduce-scatter.11.cloned.1.call-update
  354.7 1.2 copy-done.2
  355.9 0.0 copy-done.7
  355.9 11.2 %convolution_bitcast_fusion = f32[1,5120,1280]{2,1,0:T(8,128)} fusion(bf16[96,5120]{1,0:T(8,128)(2,1)S(1)} %bitcast.54, bf16[96,1280]{1,0:T(8,128)(2,1)S(1)} %copy-done.7), kind=kOutput, calls=%fused_computation.1 | convolution fusion | flops 1258291200 | bytes 27443200 | tf_op jit(solution)/shard_map/dot_general | solution.py:13
  367.1 5.7 %all-reduce.6.cloned.1.call-done = bf16[48,1280]{1,0:T(8,128)(2,1)} async-done(((bf16[48,1280]{1,0:T(8,128)(2,1)}), bf16[48,1280]{1,0:T(8,128)(2,1)}) %all-reduce.6.cloned.1.call-update) | async-done | bytes 122896 | tf_op jit(solution)/shard_map/psum | solution.py:114
  372.8 1.6 convert_element_type.74
  374.4 154.6 %reduce-scatter.11.cloned.1.call-done = bf16[2048,1280]{1,0:T(8,128)(2,1)} async-done(((bf16[8192,1280]{1,0:T(8,128)(2,1)}), bf16[2048,1280]{1,0:T(8,128)(2,1)}) %reduce-scatter.11.cloned.1.call-update) | async-done | bytes 5242896 | tf_op jit(solution)/shard_map/reduce_scatter | solution.py:81
  529.1 7.4 %bitcast_convert_fusion = f32[1,1,2048,1280]{3,2,1,0:T(8,128)} fusion(bf16[2048,1280]{1,0:T(8,128)(2,1)} %reduce-scatter.11.cloned.1.call-done), kind=kLoop, calls=%fused_computation.7 | loop fusion | flops 2621440 | bytes 15728640 | tf_op jit(solution)/shard_map/reshape | solution.py:84
  (32 shorter events, 0.1 us)
Async XLA Ops:
  7.2 68.6 %reduce-scatter.5.cloned.1.call-start = ((), (), s32[]{:S(2)}) async-start(), calls=%async_computation.6 | async-start | bytes 368640 | tf_op jit(solution)/shard_map/reduce_scatter | solution.py:47
  24.6 18.6 %copy-start.16 = (f32[48]{0:T(128)}, f32[48]{0:T(128)S(1)}, u32[]{:S(2)}) copy-start(f32[48]{0:T(128)S(1)} %add_rsqrt_fusion.1) | copy-start | bytes 580
  41.0 2.3 copy-start.17
  55.0 0.9 copy-start.1
  55.9 19.8 %copy-start.4 = (bf16[48,1280]{1,0:T(8,128)(2,1)S(1)}, bf16[48,1280]{1,0:T(8,128)(2,1)}, u32[]{:S(2)}) copy-start(bf16[48,1280]{1,0:T(8,128)(2,1)} %param.7) | copy-start | bytes 368644
  55.9 32.6 %copy-start.10 = (f32[1280]{0:T(1024)S(1)}, f32[1280]{0:T(1024)}, u32[]{:S(2)}) copy-start(f32[1280]{0:T(1024)} %param.10) | copy-start | bytes 15364
  63.6 163.1 %all-reduce.4.cloned.1.call-start = ((), (), s32[]{:S(2)}) async-start(), calls=%async_computation.7 | async-start | bytes 6291456 | tf_op jit(solution)/shard_map/psum | solution.py:60
  88.6 185.9 %copy-start.12 = (f32[48]{0:T(128)}, f32[48]{0:T(128)S(1)}, u32[]{:S(2)}) copy-start(f32[48]{0:T(128)S(1)} %add_rsqrt_fusion) | copy-start | bytes 580
  95.1 0.7 copy-start.8
  108.2 153.4 %reduce-scatter.7.cloned.1.call-start = ((), (), s32[]{:S(2)}) async-start(), calls=%async_computation.8 | async-start | bytes 368640 | tf_op jit(solution)/shard_map/reduce_scatter | solution.py:72
  108.3 131.2 %copy-start.13 = (f32[1,96]{1,0:T(1,128)S(1)}, f32[1,96]{1,0:T(1,128)}, u32[]{:S(2)}) copy-start(f32[1,96]{1,0:T(1,128)} %param.13) | copy-start | bytes 1156
  108.3 131.2 %copy-start.14 = (s32[1,96]{1,0:T(1,128)S(1)}, s32[1,96]{1,0:T(1,128)}, u32[]{:S(2)}) copy-start(s32[1,96]{1,0:T(1,128)} %param.12) | copy-start | bytes 1156
  226.7 7.2 %copy-start = (f32[96,8192]{1,0:T(8,128)S(1)}, f32[96,8192]{1,0:T(8,128)}, u32[]{:S(2)}) copy-start(f32[96,8192]{1,0:T(8,128)} %all-reduce.4.cloned.1.call-done) | copy-start | bytes 9437188
  234.0 17.0 %copy-start.11 = (f32[96]{0:T(128)}, f32[96]{0:T(128)S(1)}, u32[]{:S(2)}) copy-start(f32[96]{0:T(128)S(1)} %pmax.7) | copy-start | bytes 1156
  239.5 11.4 %copy-start.15 = (f32[96]{0:T(128)}, f32[96]{0:T(128)S(1)}, u32[]{:S(2)}) copy-start(f32[96]{0:T(128)S(1)} %psum.51) | copy-start | bytes 1156
  239.5 22.1 %copy-start.5 = (bf16[48,1280]{1,0:T(8,128)(2,1)S(1)}, bf16[48,1280]{1,0:T(8,128)(2,1)}, u32[]{:S(2)}) copy-start(bf16[48,1280]{1,0:T(8,128)(2,1)} %reduce-scatter.5.cloned.1.call-done) | copy-start | bytes 368644
  251.0 76.0 %reduce-scatter.9.cloned.1.call-start = ((), (), s32[]{:S(2)}) async-start(), calls=%async_computation.9 | async-start | bytes 1228800 | tf_op jit(solution)/shard_map/reduce_scatter | solution.py:98
  274.4 6.8 %copy-start.18 = (f32[48]{0:T(128)}, f32[48]{0:T(128)S(1)}, u32[]{:S(2)}) copy-start(f32[48]{0:T(128)S(1)} %broadcast_multiply_fusion.2) | copy-start | bytes 580
  281.2 8.9 %copy-start.6 = (bf16[96,1280]{1,0:T(8,128)(2,1)}, bf16[96,1280]{1,0:T(8,128)(2,1)S(1)}, u32[]{:S(2)}) copy-start(bf16[96,1280]{1,0:T(8,128)(2,1)S(1)} %all_gather.15) | copy-start | bytes 737284
  290.1 51.1 %copy-start.9 = (bf16[48,1280]{1,0:T(8,128)(2,1)S(1)}, bf16[48,1280]{1,0:T(8,128)(2,1)}, u32[]{:S(2)}) copy-start(bf16[48,1280]{1,0:T(8,128)(2,1)} %reduce-scatter.7.cloned.1.call-done) | copy-start | bytes 368644
  303.4 69.4 %all-reduce.6.cloned.1.call-start = ((), (), s32[]{:S(2)}) async-start(), calls=%async_computation.10 | async-start | bytes 245760 | tf_op jit(solution)/shard_map/psum | solution.py:114
  327.9 0.8 copy-start.3
  343.4 185.6 %reduce-scatter.11.cloned.1.call-start = ((), (), s32[]{:S(2)}) async-start(), calls=%async_computation.11 | async-start | bytes 26214400 | tf_op jit(solution)/shard_map/reduce_scatter | solution.py:81
  354.7 1.2 copy-start.2
  354.7 1.2 copy-start.7
Sparse Core Ops, SparseCore 0:
  63.7 11.9 reduce-scatter.4
  108.4 118.3 all-reduce.3
  251.1 10.4 reduce-scatter.6
  303.5 23.3 reduce-scatter.8
  343.6 29.2 all-reduce.5
  375.3 153.7 reduce-scatter.10
where the time goes:
time: 544 us; the launch traced here: 543 us
  waiting for transfers between devices  325 us (60%)
  blocking collectives  113 us (21%)
  matrix products  62.7 us (12%)
  other arithmetic  24.5 us (5%)
  between operations  14.2 us (3%)
    reduce_scatter x1, waiting for transfers between devices, local(): lax.psum_scatter(vocab_term, 'head', scatter_dimension=0, tiled=True)  155 us
    psum x1, waiting for transfers between devices, local(): logits = lax.psum(partial_logits, 'tensor')  118 us
    reduce_scatter x1, waiting for transfers between devices, local(): lax.psum_scatter(joined_part.reshape(rows, 2, D).astype(jnp.bfloat16), 't...  23.4 us
    dot_general x2, matrix products, contract_rows(): lax.dot_general(left, right, (((0,), (0,)), ((), ())), preferred_element_...  22.4 us
    dot_general x2, matrix products, contract_cols(): lax.dot_general(left, right, (((1,), (1,)), ((), ())), preferred_element_...  21.3 us
    all_gather x1, blocking collectives, local(): lax.all_gather(next_embeds[0], 'tensor', axis=1, tiled=True)  17.2 us
    all_gather x1, blocking collectives, local(): lax.all_gather(trunk_hidden, 'tensor', axis=1, tiled=True)  16.1 us
    all_to_all x1, blocking collectives, local(): lax.all_to_all(contract_cols(grad_all, weight_block).astype(jnp.bfloat16)...  13.3 us
  transfers between devices with their start and end apart: 6, of which 6 were waited for; matrix products, arithmetic and copies ran while one was open for 4% of the time, Pallas kernels for 0%

commit v1 on v0

v1 whole, which is shorter than its diff:
```python
import jax
import jax.numpy as jnp
from jax import lax
from jax.sharding import PartitionSpec as P

epsilon = 1e-05
f32 = jnp.float32
bf16 = jnp.bfloat16


def contract_rows(left, right):
    return lax.dot_general(
        left, right, (((0,), (0,)), ((), ())), preferred_element_type=f32
    )


def contract_cols(left, right):
    return lax.dot_general(
        left, right, (((1,), (1,)), ((), ())), preferred_element_type=f32
    )


def plain_dot(left, right):
    return jnp.dot(left, right, preferred_element_type=f32)


def shift(value, axis, size, by):
    return lax.ppermute(value, axis, [(i, (i + by) % size) for i in range(size)])


def flip(value, axis, size, mask):
    return lax.ppermute(value, axis, [(i, i ^ mask) for i in range(size)])


def swap(value):
    return lax.ppermute(value, "dp", [(0, 1), (1, 0)])


def fast_local(
    n_head,
    n_tensor,
    trunk_hidden,
    next_embeds,
    combine_weight,
    final_gain,
    unembed_weight,
    target_ids,
    loss_scale,
):
    half, width = trunk_hidden.shape
    rows = 2 * half
    features = width * n_tensor
    weight_block = combine_weight[0]
    vocab_part = unembed_weight.shape[0]
    piece = vocab_part // n_tensor
    d = lax.axis_index("dp")
    t = lax.axis_index("tensor")
    h = lax.axis_index("head")
    first = d == 0
    targets = target_ids[0]
    row_weights = loss_scale[0]

    def combine_rows(which):
        return lax.dynamic_slice_in_dim(weight_block, which * width, width, 0)

    def vocab_rows(which):
        return lax.dynamic_slice_in_dim(unembed_weight, which * piece, piece, 0)

    def around(by):
        return lax.rem(t + by + n_tensor, n_tensor)

    def spread(value):
        return [value] + [shift(value, "tensor", n_tensor, r) for r in range(1, n_tensor)]

    with jax.named_scope("inputs"):
        embeds = next_embeds[0]
        other = swap(jnp.where(first, embeds, trunk_hidden))
        kept = jnp.where(first, trunk_hidden, embeds)
        trunk_other = swap(trunk_hidden)
        trunk_rows = jnp.concatenate(
            [jnp.where(first, trunk_hidden, trunk_other), jnp.where(first, trunk_other, trunk_hidden)], axis=0
        ).astype(f32)
        own = jnp.concatenate(
            [jnp.where(first, kept, other), jnp.where(first, other, kept)], axis=0
        )
        parts = spread(own)
    with jax.named_scope("projection"):
        square_sum = sum(jnp.sum(jnp.square(p.astype(f32)), axis=1) for p in parts)
        in_scale = lax.rsqrt(square_sum / features + epsilon)
        raw = sum(plain_dot(p, combine_rows(around(-r))) for r, p in enumerate(parts))
        projected = raw * in_scale[:, None]
        mixed = trunk_rows + (projected + swap(projected.astype(bf16)).astype(f32))
        gained = mixed * final_gain[None, :]
        low = gained.astype(bf16)
    with jax.named_scope("mixed_scale"):
        mixed_sums = sum(spread(jnp.sum(mixed * mixed, axis=1)))
        mixed_scale = lax.rsqrt(mixed_sums / features + epsilon)
        normed_out = (gained * mixed_scale[:, None]).astype(bf16)
        normed_heads = [normed_out] + [
            flip(normed_out, "head", n_head, m) for m in range(1, n_head)
        ]
    with jax.named_scope("logits"):
        table = jnp.array([[3, 2, 1, 0], [3, 2, 0, 1], [0, 1, 3, 2], [0, 1, 2, 3]], jnp.int32)
        order = table[t]
        slots = [contract_cols(low, vocab_rows(order[j])) for j in range(4)]
        one = lax.ppermute(slots[0], "tensor", [(0, 1), (3, 2)])
        two = jnp.where((t == 0) | (t == 3), slots[1], slots[0] + one)
        right = lax.ppermute(two, "tensor", [(0, 1), (1, 2)])
        left = lax.ppermute(two, "tensor", [(3, 2), (2, 1)])
        right = jnp.where(t == 1, slots[1], slots[2]) + right
        left = jnp.where(t == 2, slots[1], slots[2]) + left
        right = lax.ppermute(right, "tensor", [(0, 1), (1, 2), (2, 3)])
        left = lax.ppermute(left, "tensor", [(3, 2), (2, 1), (1, 0)])
        logits = (slots[3] + right + left) * mixed_scale[:, None]
    with jax.named_scope("softmax"):
        ids = lax.broadcasted_iota(jnp.int32, (1, piece), 1) + d * vocab_part
        hits = (ids + t * piece) == targets[:, None]
        top = jnp.max(logits, axis=1)
        shifted = jnp.exp(logits - top[:, None])
        total = jnp.sum(shifted, axis=1)
        at_target = jnp.sum(jnp.where(hits, logits, 0.0), axis=1)
        stats = spread(jnp.stack([top, total, at_target]))
        shifted_low = shifted.astype(bf16)
        shifted_parts = spread(shifted_low)
        tops = [s[0] for s in stats]
        part_top = jnp.max(jnp.stack(tops), axis=0)
        part_sum = sum(s[1] * jnp.exp(s[0] - part_top) for s in stats)
        part_hit = sum(s[2] for s in stats)
        there = swap(jnp.stack([part_top, part_sum, part_hit]))
        largest = jnp.maximum(part_top, there[0])
        summed = part_sum * jnp.exp(part_top - largest) + there[1] * jnp.exp(there[0] - largest)
        hit_grad = row_weights * (jnp.exp(part_hit + there[2] - largest) / summed - 1.0)
        grads = []
        for r, e in enumerate(shifted_parts):
            factor = row_weights * jnp.exp(tops[r] - largest) / summed
            mine = (ids + around(-r) * piece) == targets[:, None]
            grads.append(
                jnp.where(mine, hit_grad[:, None], e.astype(f32) * factor[:, None]).astype(bf16)
            )
        dots_part = sum(spread(jnp.sum(grads[0].astype(f32) * logits, axis=1)))
        grad_dots = dots_part + swap(dots_part)
    with jax.named_scope("grad_normed"):
        grad_part = sum(plain_dot(g, vocab_rows(around(-r))) for r, g in enumerate(grads))
        grad_normed = grad_part + swap(grad_part.astype(bf16)).astype(f32)
        mixed_normed = mixed * mixed_scale[:, None]
        grad_mixed = mixed_scale[:, None] * (
            grad_normed * final_gain[None, :] - mixed_normed * (grad_dots / features)[:, None]
        )
        grad_low = grad_mixed.astype(bf16)
    with jax.named_scope("joined_grad"):
        dots = sum(spread(jnp.sum(grad_low.astype(f32) * projected, axis=1)))
        side = [
            shift(contract_cols(grad_low, combine_rows(around(r))).astype(bf16), "tensor", n_tensor, r)
            for r in range(1, n_tensor)
        ]
        side = contract_cols(grad_low, combine_rows(t)) + sum(s.astype(f32) for s in side)
        own_normed = own.astype(f32) * in_scale[:, None]
        term = in_scale[:, None] * (side - own_normed * (dots / features)[:, None])
        term = jnp.where(first, term + grad_mixed, term)
        theirs = swap(jnp.where(first, term[half:], term[:half]).astype(bf16)).astype(f32)
        embed_grad = jnp.where(first, theirs, term[half:])[None]
        trunk_sum = jnp.where(first, term[:half], theirs)
        mask = 1
        while mask < n_head:
            trunk_low = trunk_sum.astype(bf16)
            trunk_sum = trunk_low.astype(f32) + flip(trunk_low, "head", n_head, mask).astype(f32)
            mask *= 2
        trunk_grad = trunk_sum
    with jax.named_scope("combine_grad"):
        stacked = jnp.stack(parts)
        ordered = jnp.concatenate(
            [
                lax.dynamic_index_in_dim(stacked, around(-c), 0, keepdims=False)
                for c in range(n_tensor)
            ],
            axis=1,
        )
        combine_grad = contract_rows(ordered, (in_scale[:, None] * grad_mixed).astype(bf16))[None]
    with jax.named_scope("unembed_grad"):
        grad_stack = jnp.stack(grads)
        grad_heads = []
        for m in range(n_head):
            piece_of = lax.dynamic_index_in_dim(
                grad_stack, around(-(h ^ m)), 0, keepdims=False
            )
            grad_heads.append(flip(piece_of, "head", n_head, m) if m else piece_of)
        unembed_grad = contract_rows(
            jnp.concatenate(grad_heads, axis=0), jnp.concatenate(normed_heads, axis=0)
        )
        unembed_grad = unembed_grad.reshape(1, 1, piece, width)
    return (trunk_grad, embed_grad, combine_grad, unembed_grad)


def general_local(
    n_tensor,
    trunk_hidden,
    next_embeds,
    combine_weight,
    final_gain,
    unembed_weight,
    target_ids,
    loss_scale,
):
    rows, part_width = trunk_hidden.shape
    features = part_width * n_tensor
    vocab_part = unembed_weight.shape[0]
    weight_block = combine_weight[0]
    trunk_whole, embed_whole = (
        lax.all_gather(trunk_hidden, "tensor", axis=1, tiled=True),
        lax.all_gather(next_embeds[0], "tensor", axis=1, tiled=True),
    )
    trunk_float = trunk_whole.astype(f32)
    embed_float = embed_whole.astype(f32)
    trunk_scale = lax.rsqrt(jnp.sum(trunk_float * trunk_float, axis=1) / features + epsilon)
    embed_scale = lax.rsqrt(jnp.sum(embed_float * embed_float, axis=1) / features + epsilon)
    trunk_normed = trunk_float * trunk_scale[:, None]
    embed_normed = embed_float * embed_scale[:, None]
    joined = jnp.concatenate([trunk_normed.astype(bf16), embed_normed.astype(bf16)], axis=1)
    feature_start = lax.axis_index("tensor") * part_width
    trunk_local = lax.dynamic_slice_in_dim(trunk_normed, feature_start, part_width, 1)
    embed_local = lax.dynamic_slice_in_dim(embed_normed, feature_start, part_width, 1)
    blocks = lax.all_to_all(joined, "dp", split_axis=1, concat_axis=0, tiled=True)
    projected = lax.psum_scatter(
        plain_dot(blocks, weight_block).astype(bf16), "dp", scatter_dimension=0, tiled=True
    ).astype(f32)
    mixed = trunk_hidden.astype(f32) + projected
    mixed_sums = lax.psum(jnp.sum(mixed * mixed, axis=1), "tensor")
    mixed_scale = lax.rsqrt(mixed_sums / features + epsilon)
    mixed_normed = mixed * mixed_scale[:, None]
    normed_out = (mixed_normed * final_gain[None, :]).astype(bf16)
    normed_all = lax.all_gather(normed_out, "dp", axis=0, tiled=True)
    logits = lax.psum(contract_cols(normed_all, unembed_weight), "tensor")
    largest = lax.pmax(jnp.max(logits, axis=1), "dp")
    shifted = jnp.exp(logits - largest[:, None])
    summed = lax.psum(jnp.sum(shifted, axis=1), "dp")
    probs = shifted / summed[:, None]
    vocab_ids = (
        lax.broadcasted_iota(jnp.int32, (1, vocab_part), 1) + lax.axis_index("dp") * vocab_part
    )
    hits = (vocab_ids == target_ids[0][:, None]).astype(f32)
    grad_local = (loss_scale[0][:, None] * (probs - hits)).astype(bf16)
    grad_normed = lax.psum_scatter(
        plain_dot(grad_local, unembed_weight).astype(bf16), "dp", scatter_dimension=0, tiled=True
    ).astype(f32)
    vocab_term = contract_rows(grad_local, normed_all).astype(bf16)
    vocab_total = lax.psum_scatter(vocab_term, "head", scatter_dimension=0, tiled=True).astype(f32)
    unembed_grad = vocab_total.reshape(1, 1, vocab_total.shape[0], part_width)
    scaled_grad = grad_normed * final_gain[None, :]
    grad_dots = lax.psum(jnp.sum(scaled_grad * mixed_normed, axis=1), "tensor")
    grad_mixed = mixed_scale[:, None] * (
        scaled_grad - mixed_normed * (grad_dots / features)[:, None]
    )
    grad_all = lax.all_gather(grad_mixed.astype(bf16), "dp", axis=0, tiled=True)
    combine_grad = contract_rows(blocks, grad_all)[None]
    joined_part = lax.all_to_all(
        contract_cols(grad_all, weight_block).astype(bf16),
        "dp",
        split_axis=0,
        concat_axis=1,
        tiled=True,
    )
    joined_grad = lax.psum_scatter(
        joined_part.reshape(rows, 2, features), "tensor", scatter_dimension=2, tiled=True
    ).astype(f32)
    trunk_side = joined_grad[:, 0]
    embed_side = joined_grad[:, 1]
    trunk_dots, embed_dots = lax.psum(
        (jnp.sum(trunk_side * trunk_local, axis=1), jnp.sum(embed_side * embed_local, axis=1)),
        "tensor",
    )
    trunk_term = trunk_scale[:, None] * (
        trunk_side - trunk_local * (trunk_dots / features)[:, None]
    )
    embed_grad = (
        embed_scale[:, None] * (embed_side - embed_local * (embed_dots / features)[:, None])
    )[None]
    trunk_grad = lax.psum((grad_mixed + trunk_term).astype(bf16), "head").astype(f32)
    return (trunk_grad, embed_grad, combine_grad, unembed_grad)


def solution(mesh):
    n_head, n_tensor, n_dp = mesh.shape["head"], mesh.shape["tensor"], mesh.shape["dp"]
    in_specs = (
        P("dp", "tensor"),
        P("head", "dp", "tensor"),
        P("head", "dp", "tensor"),
        P("tensor"),
        P("dp", "tensor"),
        P("head", None),
        P("head", None),
    )
    out_specs = (
        P("dp", "tensor"),
        P("head", "dp", "tensor"),
        P("head", "dp", "tensor"),
        P("dp", "head", None, "tensor"),
    )
    if n_dp == 2 and n_tensor == 4 and n_head == 4:

        def local(*args):
            return fast_local(n_head, n_tensor, *args)

    else:

        def local(*args):
            return general_local(n_tensor, *args)

    return jax.shard_map(local, mesh=mesh, in_specs=in_specs, out_specs=out_specs, check_vma=False)
```

time: 544 us -> 245 us (0.45)
  waiting for transfers between devices: 325 us -> 94.9 us
  blocking collectives: 113 us -> 0 us
  starting transfers between devices: 0.25 us -> 69.7 us
  other arithmetic: 24.5 us -> 11.6 us
  between operations: 14.2 us -> 3.72 us
    reduce_scatter x4 -> x0, waiting for transfers between devices: 201 us -> none  [the longest x1 155 us: local(): lax.psum_scatter(vocab_term, 'head', scatter_dimension=0, tiled=True)]
    psum x2 -> x0, waiting for transfers between devices: 124 us -> none  [the longest x1 118 us: local(): logits = lax.psum(partial_logits, 'tensor')]
    ppermute x0 -> x41, waiting for transfers between devices: none -> 94.9 us  [the longest x21 51.5 us: shift(): lax.ppermute(value, axis, [(i, (i + by) % size) for i in range(size)])]
    ppermute x0 -> x41, starting transfers between devices: none -> 69.7 us  [the longest x21 30.7 us: shift(): lax.ppermute(value, axis, [(i, (i + by) % size) for i in range(size)])]
    all_gather x4 -> x0, blocking collectives: 44.6 us -> none  [the longest x1 17.2 us: local(): lax.all_gather(next_embeds[0], 'tensor', axis=1, tiled=True)]
    psum x4 -> x0, blocking collectives: 38.4 us -> none  [the longest x1 11.7 us: local(): mixed_sums = lax.psum(jnp.sum(mixed * mixed, axis=1), 'tensor')]
    all_to_all x2 -> x0, blocking collectives: 24.9 us -> none  [the longest x1 13.3 us: local(): lax.all_to_all(contract_cols(grad_all, weight_block).astype(jnp.bfloat16)...]
    reshape x1 -> x0, other arithmetic: 7.38 us -> none  [local(): unembed_grad = vocab_total.reshape(1, 1, vocab_total.shape[0], part_width)]
  transfers between devices with their start and end apart: 6 -> 41, of which waited for: 6 -> 20; matrix products, arithmetic and copies ran while one was open for 4% -> 20% of each run, Pallas kernels for 0% -> 0%
where the time goes in v1:
time: 245 us
  waiting for transfers between devices  94.9 us (39%)
  starting transfers between devices  69.7 us (28%)
  matrix products  63.2 us (26%)
  other arithmetic  11.6 us (5%)
  between operations  3.72 us (2%)
    ppermute x21, waiting for transfers between devices, shift(): lax.ppermute(value, axis, [(i, (i + by) % size) for i in range(size)])  51.5 us
    ppermute x21, starting transfers between devices, shift(): lax.ppermute(value, axis, [(i, (i + by) % size) for i in range(size)])  30.7 us
    dot_general x8, matrix products, plain_dot(): return jnp.dot(left, right, preferred_element_type=f32)  25 us
    dot_general x8, matrix products, contract_cols(): lax.dot_general(left, right, (((1,), (1,)), ((), ())), preferred_element_...  21.3 us
    dot_general x2, matrix products, contract_rows(): lax.dot_general(left, right, (((0,), (0,)), ((), ())), preferred_element_...  16.9 us
    ppermute x7, waiting for transfers between devices, swap(): return lax.ppermute(value, 'dp', [(0, 1), (1, 0)])  15.4 us
    ppermute x7, starting transfers between devices, swap(): return lax.ppermute(value, 'dp', [(0, 1), (1, 0)])  12.5 us
    ppermute x8, waiting for transfers between devices, flip(): return lax.ppermute(value, axis, [(i, i ^ mask) for i in range(size)])  9.83 us
  transfers between devices with their start and end apart: 41, of which 20 were waited for; matrix products, arithmetic and copies ran while one was open for 20% of the time, Pallas kernels for 0%

profile of v1, /device:TPU:0, one launch (start us, length us, event | category | flops | bytes accessed | tf_op | source)
XLA Modules:
  0.0 244.8 jit_solution(4573038691568785599)
XLA Ops:
  0.6 3.0 %collective-permute-start.4 = (bf16[48,1280]{1,0:T(8,128)(2,1)}, bf16[48,1280]{1,0:T(8,128)(2,1)S(1)}, u32[]{:S(2)}, u32[]{:S(2)}) collective-permute-start(bf16[48,1280]{1,0:T(8,128)(2,1)} %param.8), channel_id=1, source_target_pairs={{0,1},{1,0},{2,3},{3,2},{4,5},{5,4},{6,7},{7,6},{8,9},{9,8},{10,11... | collective-permute-start | bytes 368648 | tf_op jit(solution)/shard_map/inputs/ppermute | solution.py:36
  3.7 3.5 %collective-permute-done.4 = bf16[48,1280]{1,0:T(8,128)(2,1)S(1)} collective-permute-done((bf16[48,1280]{1,0:T(8,128)(2,1)}, bf16[48,1280]{1,0:T(8,128)(2,1)S(1)}, u32[]{:S(2)}, u32[]{:S(2)}) %collective-permute-start.4) | collective-permute-done | bytes 122912 | tf_op jit(solution)/shard_map/inputs/ppermute | solution.py:36
  8.2 1.8 collective-permute-start
  10.0 3.1 %collective-permute-done = bf16[48,1280]{1,0:T(8,128)(2,1)S(1)} collective-permute-done((bf16[48,1280]{1,0:T(8,128)(2,1)S(1)}, bf16[48,1280]{1,0:T(8,128)(2,1)S(1)}, u32[]{:S(2)}, u32[]{:S(2)}) %collective-permute-start) | collective-permute-done | bytes 122912 | tf_op jit(solution)/shard_map/inputs/ppermute | solution.py:36
  14.8 2.8 %collective-permute-start.2 = (bf16[96,1280]{1,0:T(8,128)(2,1)S(1)}, bf16[96,1280]{1,0:T(8,128)(2,1)S(1)}, u32[]{:S(2)}, u32[]{:S(2)}) collective-permute-start(bf16[96,1280]{1,0:T(8,128)(2,1)S(1)} %get-tuple-element.34), channel_id=1, source_target_pairs={{0,4},{2,6},{4,0},{6,2},{1,5},{3,7},{5,1},{7,3},{8,12},{10,14},{12... | collective-permute-start | bytes 737288 | tf_op jit(solution)/shard_map/inputs/ppermute | solution.py:28
  17.7 1.6 collective-permute-start.1
  19.2 2.2 collective-permute-start.3
  21.6 11.7 %collective-permute-done.2 = bf16[96,1280]{1,0:T(8,128)(2,1)S(1)} collective-permute-done((bf16[96,1280]{1,0:T(8,128)(2,1)S(1)}, bf16[96,1280]{1,0:T(8,128)(2,1)S(1)}, u32[]{:S(2)}, u32[]{:S(2)}) %collective-permute-start.2) | collective-permute-done | bytes 245792 | tf_op jit(solution)/shard_map/inputs/ppermute | solution.py:28
  34.0 2.6 %fusion.24 = f32[96,1280]{1,0:T(8,128)S(1)} fusion(bf16[96,1280]{1,0:T(8,128)(2,1)S(1)} %collective-permute-done.3, bf16[1,5120,1280]{2,1,0:T(8,128)(2,1)} %param.10, s32[]{:T(128)S(6)} %select_n.175), kind=kOutput, calls=%fused_computation.26 | convolution fusion | flops 314572800 | bytes 4014084 | tf_op jit(solution)/shard_map/projection/dot_general | solution.py:24
  36.6 2.6 %fusion.28 = f32[96,1280]{1,0:T(8,128)S(1)} fusion(bf16[96,1280]{1,0:T(8,128)(2,1)S(1)} %collective-permute-done.1, bf16[1,5120,1280]{2,1,0:T(8,128)(2,1)} %param.10, s32[]{:T(128)S(6)} %select_n.173), kind=kOutput, calls=%fused_computation.30 | convolution fusion | flops 314572800 | bytes 4014084 | tf_op jit(solution)/shard_map/projection/dot_general | solution.py:24
  39.3 2.6 %fusion.26 = f32[96,1280]{1,0:T(8,128)S(1)} fusion(bf16[96,1280]{1,0:T(8,128)(2,1)S(1)} %collective-permute-done.2, bf16[1,5120,1280]{2,1,0:T(8,128)(2,1)} %param.10, s32[]{:T(128)S(6)} %select_n.174), kind=kOutput, calls=%fused_computation.28 | convolution fusion | flops 314572800 | bytes 4014084 | tf_op jit(solution)/shard_map/projection/dot_general | solution.py:24
  41.9 2.6 %fusion.156 = (bf16[96,1280]{1,0:T(8,128)(2,1)S(1)}, f32[96,1280]{1,0:T(8,128)S(1)}) fusion(f32[96]{0:T(128)S(1)} %add_rsqrt_fusion.1, f32[96,1280]{1,0:T(8,128)S(1)} %fusion.24, f32[96,1280]{1,0:T(8,128)S(1)} %fusion.26, f32[96,1280]{1,0:T(8,128)S(1)} %fusion.28, bf16[1,5120,1280]{2,1,0:T(8,128)(2,1)} %param.10, s32[]{:T(128)S(6)} %select_n.172, ...), kind=kOutput, calls=%fused_computation.213 | convolution fusion | flops 315678720 | bytes 5734788 | tf_op jit(solution)/shard_map/projection/dot_general | solution.py:24
  44.5 1.4 collective-permute-start.5
  47.9 2.8 %collective-permute-done.5 = bf16[96,1280]{1,0:T(8,128)(2,1)S(1)} collective-permute-done((bf16[96,1280]{1,0:T(8,128)(2,1)S(1)}, bf16[96,1280]{1,0:T(8,128)(2,1)S(1)}, u32[]{:S(2)}, u32[]{:S(2)}) %collective-permute-start.5) | collective-permute-done | bytes 245792 | tf_op jit(solution)/shard_map/projection/ppermute | solution.py:36
  51.5 4.2 %fusion.8 = f32[96,2048]{1,0:T(8,128)S(1)} fusion(bf16[96,1280]{1,0:T(8,128)(2,1)S(1)} %multiply_convert_fusion.2, bf16[8192,1280]{1,0:T(8,128)(2,1)} %param.12, s32[]{:T(128)S(6)} %select_n.183), kind=kOutput, calls=%fused_computation.10 | convolution fusion | flops 503316480 | bytes 6275076 | tf_op jit(solution)/shard_map/logits/dot_general | solution.py:18
  55.7 8.3 %collective-permute-start.9 = (f32[96,2048]{1,0:T(8,128)S(1)}, f32[96,2048]{1,0:T(8,128)}, u32[]{:S(2)}, u32[]{:S(2)}) collective-permute-start(f32[96,2048]{1,0:T(8,128)S(1)} %fusion.8), channel_id=1, source_target_pairs={{0,2},{6,4},{1,3},{7,5},{8,10},{14,12},{9,11},{15,13},{16,18},{22,... | collective-permute-start | bytes 2359304 | tf_op jit(solution)/shard_map/logits/ppermute | solution.py:106
  64.7 4.2 %fusion.12 = f32[96,2048]{1,0:T(8,128)S(1)} fusion(bf16[96,1280]{1,0:T(8,128)(2,1)S(1)} %multiply_convert_fusion.2, bf16[8192,1280]{1,0:T(8,128)(2,1)} %param.12, s32[]{:T(128)S(6)} %select_n.179), kind=kOutput, calls=%fused_computation.14 | convolution fusion | flops 503316480 | bytes 6275076 | tf_op jit(solution)/shard_map/logits/dot_general | solution.py:18
  68.8 9.7 %collective-permute-done.9 = f32[96,2048]{1,0:T(8,128)} collective-permute-done((f32[96,2048]{1,0:T(8,128)S(1)}, f32[96,2048]{1,0:T(8,128)}, u32[]{:S(2)}, u32[]{:S(2)}) %collective-permute-start.9) | collective-permute-done | bytes 786464 | tf_op jit(solution)/shard_map/logits/ppermute | solution.py:106
  78.6 2.1 add_select_fusion
  81.4 6.0 %collective-permute-start.10 = (f32[96,2048]{1,0:T(8,128)}, f32[96,2048]{1,0:T(8,128)}, u32[]{:S(2)}, u32[]{:S(2)}) collective-permute-start(f32[96,2048]{1,0:T(8,128)} %add_select_fusion), channel_id=1, source_target_pairs={{0,2},{2,4},{1,3},{3,5},{8,10},{10,12},{9,11},{11,13},{16,18},{18,... | collective-permute-start | bytes 2359304 | tf_op jit(solution)/shard_map/logits/ppermute | solution.py:108
  88.7 4.2 %fusion.10 = f32[96,2048]{1,0:T(8,128)S(1)} fusion(bf16[96,1280]{1,0:T(8,128)(2,1)S(1)} %multiply_convert_fusion.2, bf16[8192,1280]{1,0:T(8,128)(2,1)} %param.12, s32[]{:T(128)S(6)} %select_n.180), kind=kOutput, calls=%fused_computation.12 | convolution fusion | flops 503316480 | bytes 6275076 | tf_op jit(solution)/shard_map/logits/dot_general | solution.py:18
  92.9 8.4 %collective-permute-done.10 = f32[96,2048]{1,0:T(8,128)} collective-permute-done((f32[96,2048]{1,0:T(8,128)}, f32[96,2048]{1,0:T(8,128)}, u32[]{:S(2)}, u32[]{:S(2)}) %collective-permute-start.10) | collective-permute-done | bytes 786464 | tf_op jit(solution)/shard_map/logits/ppermute | solution.py:108
  101.3 1.3 select_add_fusion.1
  102.7 5.2 %collective-permute-start.11 = (f32[96,2048]{1,0:T(8,128)S(1)}, f32[96,2048]{1,0:T(8,128)S(1)}, u32[]{:S(2)}, u32[]{:S(2)}) collective-permute-start(f32[96,2048]{1,0:T(8,128)S(1)} %get-tuple-element.24), channel_id=1, source_target_pairs={{0,2},{2,4},{4,6},{1,3},{3,5},{5,7},{8,10},{10,12},{12,14},{9,11},... | collective-permute-start | bytes 2359304 | tf_op jit(solution)/shard_map/logits/ppermute | solution.py:112
  107.9 1.3 collective-permute-start.13
  109.3 4.1 %collective-permute-start.8 = (f32[96]{0:T(128)S(1)}, f32[96]{0:T(128)S(1)}, u32[]{:S(2)}, u32[]{:S(2)}) collective-permute-start(f32[96]{0:T(128)S(1)} %copy-done.8), channel_id=1, source_target_pairs={{0,6},{2,0},{4,2},{6,4},{1,7},{3,1},{5,3},{7,5},{8,14},{10,8},{12,... | collective-permute-start | bytes 1160 | tf_op jit(solution)/shard_map/mixed_scale/ppermute | solution.py:28
  113.9 1.9 collective-permute-start.6
  115.8 4.2 %fusion.14 = f32[96,2048]{1,0:T(8,128)S(1)} fusion(bf16[96,1280]{1,0:T(8,128)(2,1)S(1)} %multiply_convert_fusion.2, bf16[8192,1280]{1,0:T(8,128)(2,1)} %param.12, s32[]{:T(128)S(6)} %select_n.177), kind=kOutput, calls=%fused_computation.16 | convolution fusion | flops 503316480 | bytes 6275076 | tf_op jit(solution)/shard_map/logits/dot_general | solution.py:18
  120.0 6.4 %collective-permute-done.8 = f32[96]{0:T(128)S(1)} collective-permute-done((f32[96]{0:T(128)S(1)}, f32[96]{0:T(128)S(1)}, u32[]{:S(2)}, u32[]{:S(2)}) %collective-permute-start.8) | collective-permute-done | bytes 416 | tf_op jit(solution)/shard_map/mixed_scale/ppermute | solution.py:28
  126.4 1.1 collective-permute-done.7
  128.3 2.1 collective-permute-start.15
  130.6 1.2 collective-permute-done.16
  132.8 2.9 %collective-permute-done.14 = f32[3,96]{1,0:T(4,128)S(1)} collective-permute-done((f32[3,96]{1,0:T(4,128)S(1)}, f32[3,96]{1,0:T(4,128)S(1)}, u32[]{:S(2)}, u32[]{:S(2)}) %collective-permute-start.14) | collective-permute-done | bytes 1184 | tf_op jit(solution)/shard_map/softmax/ppermute | solution.py:28
  135.8 1.6 collective-permute-start.17
  137.5 2.0 collective-permute-done.17
  140.7 1.5 collective-permute-start.22
  142.3 2.4 collective-permute-start.20
  145.8 1.5 collective-permute-start.18
  147.3 1.4 collective-permute-done.23
  148.7 1.6 collective-permute-start.25
  150.3 3.7 %fusion.6 = f32[96,1280]{1,0:T(8,128)S(1)} fusion(bf16[8192,1280]{1,0:T(8,128)(2,1)} %param.12, s32[]{:T(128)S(6)} %select_n.189, bf16[96,2048]{1,0:T(8,128)(2,1)S(1)} %get-tuple-element.7, f32[96]{0:T(128)S(1)} %get-tuple-element.41, bf16[96]{0:T(256)(128)(2,1)S(1)} %bitcast_multiply_fusion.5, s32[2048]{0:T(1024)S(1)} %fusion.104, s32[96]{0:T(128)S(1)} %bitcast.253), kind=kOutput, calls=%fused_computation.8 | convolution fusion | flops 504102912 | bytes 6136772 | tf_op jit(solution)/shard_map/grad_normed/dot_general | solution.py:24
  154.0 17.7 %collective-permute-done.19 = bf16[96,2048]{1,0:T(8,128)(2,1)S(1)} collective-permute-done((bf16[96,2048]{1,0:T(8,128)(2,1)S(1)}, bf16[96,2048]{1,0:T(8,128)(2,1)S(1)}, u32[]{:S(2)}, u32[]{:S(2)}) %collective-permute-start.19) | collective-permute-done | bytes 393248 | tf_op jit(solution)/shard_map/softmax/ppermute | solution.py:28
  171.7 3.7 %fusion.2 = f32[96,1280]{1,0:T(8,128)S(1)} fusion(bf16[8192,1280]{1,0:T(8,128)(2,1)} %param.12, s32[]{:T(128)S(6)} %select_n.193, bf16[96,2048]{1,0:T(8,128)(2,1)S(1)} %collective-permute-done.19, f32[96]{0:T(128)S(1)} %get-tuple-element.39, s32[2048]{0:T(1024)S(1)} %get-tuple-element.54, bf16[96]{0:T(256)(128)(2,1)S(1)} %bitcast_multiply_fusion.5, ...), kind=kOutput, calls=%fused_computation.4 | convolution fusion | flops 504102912 | bytes 6136772 | tf_op jit(solution)/shard_map/grad_normed/dot_general | solution.py:24
  175.4 3.7 %fusion = f32[96,1280]{1,0:T(8,128)S(1)} fusion(bf16[8192,1280]{1,0:T(8,128)(2,1)} %param.12, s32[]{:T(128)S(6)} %select_n.195, bf16[96,2048]{1,0:T(8,128)(2,1)S(1)} %collective-permute-done.20, f32[96]{0:T(128)S(1)} %get-tuple-element.40, s32[2048]{0:T(1024)S(1)} %get-tuple-element.53, bf16[96]{0:T(256)(128)(2,1)S(1)} %bitcast_multiply_fusion.5, ...), kind=kOutput, calls=%fused_computation.2 | convolution fusion | flops 504102912 | bytes 6136772 | tf_op jit(solution)/shard_map/grad_normed/dot_general | solution.py:24
  179.1 3.6 %fusion.157 = (bf16[96,1280]{1,0:T(8,128)(2,1)S(1)}, f32[96,1280]{1,0:T(8,128)S(1)}) fusion(f32[96,1280]{1,0:T(8,128)S(1)} %fusion, f32[96,1280]{1,0:T(8,128)S(1)} %fusion.2, f32[96,1280]{1,0:T(8,128)S(1)} %fusion.6, bf16[8192,1280]{1,0:T(8,128)(2,1)} %param.12, s32[]{:T(128)S(6)} %select_n.191, bf16[96,2048]{1,0:T(8,128)(2,1)S(1)} %collective-permute-done.18, ...), kind=kOutput, calls=%fused_computation.214 | convolution fusion | flops 504594432 | bytes 7857092 | tf_op jit(solution)/shard_map/grad_normed/dot_general | solution.py:24
  182.7 1.6 collective-permute-start.21
  185.0 4.0 %collective-permute-done.21 = bf16[96,1280]{1,0:T(8,128)(2,1)S(1)} collective-permute-done((bf16[96,1280]{1,0:T(8,128)(2,1)S(1)}, bf16[96,1280]{1,0:T(8,128)(2,1)S(1)}, u32[]{:S(2)}, u32[]{:S(2)}) %collective-permute-start.21) | collective-permute-done | bytes 245792 | tf_op jit(solution)/shard_map/grad_normed/ppermute | solution.py:36
  189.4 1.9 collective-permute-start.29
  191.4 1.1 fusion.67
  192.5 1.1 fusion.64
  193.7 1.1 fusion.61
  194.8 1.6 collective-permute-start.26
  196.4 1.5 collective-permute-start.27
  197.9 2.8 %collective-permute-start.28 = (bf16[96,1280]{1,0:T(8,128)(2,1)S(1)}, bf16[96,1280]{1,0:T(8,128)(2,1)S(1)}, u32[]{:S(2)}, u32[]{:S(2)}) collective-permute-start(bf16[96,1280]{1,0:T(8,128)(2,1)S(1)} %fusion.67), channel_id=1, source_target_pairs={{0,6},{2,0},{4,2},{6,4},{1,7},{3,1},{5,3},{7,5},{8,14},{10,8},{12,... | collective-permute-start | bytes 737288 | tf_op jit(solution)/shard_map/joined_grad/ppermute | solution.py:28
  201.0 1.6 collective-permute-start.36
  203.1 7.3 %collective-permute-done.27 = bf16[96,1280]{1,0:T(8,128)(2,1)S(1)} collective-permute-done((bf16[96,1280]{1,0:T(8,128)(2,1)S(1)}, bf16[96,1280]{1,0:T(8,128)(2,1)S(1)}, u32[]{:S(2)}, u32[]{:S(2)}) %collective-permute-start.27) | collective-permute-done | bytes 245792 | tf_op jit(solution)/shard_map/joined_grad/ppermute | solution.py:28
  210.4 1.2 add_select_fusion.1
  211.6 1.6 collective-permute-start.32
  213.2 11.2 %convolution_bitcast_fusion = f32[1,5120,1280]{2,1,0:T(8,128)} fusion(bf16[96,1280]{1,0:T(8,128)(2,1)S(1)} %get-tuple-element.27, bf16[96,1280]{1,0:T(8,128)(2,1)S(1)} %get-tuple-element.28, bf16[96,1280]{1,0:T(8,128)(2,1)S(1)} %get-tuple-element.29, bf16[96,1280]{1,0:T(8,128)(2,1)S(1)} %get-tuple-element.26, f32[96,1280]{1,0:T(8,128)S(1)} %get-tuple-element.10, ...), kind=kOutput, calls=%fused_computation | convolution fusion | flops 1262469120 | bytes 27689344 | tf_op jit(solution)/shard_map/combine_grad/dot_general | solution.py:12
  224.4 1.5 collective-permute-start.39
  226.5 6.4 %collective-permute-done.39 = bf16[96,1280]{1,0:T(8,128)(2,1)S(1)} collective-permute-done((bf16[96,1280]{1,0:T(8,128)(2,1)S(1)}, bf16[96,1280]{1,0:T(8,128)(2,1)S(1)}, u32[]{:S(2)}, u32[]{:S(2)}) %collective-permute-start.39) | collective-permute-done | bytes 245792 | tf_op jit(solution)/shard_map/mixed_scale/ppermute | solution.py:32
  232.9 5.7 %convolution_bitcast_fusion.1 = f32[1,1,2048,1280]{3,2,1,0:T(8,128)} fusion(bf16[96,2048]{1,0:T(8,128)(2,1)S(1)} %collective-permute-done.37, bf16[96,2048]{1,0:T(8,128)(2,1)S(1)} %collective-permute-done.36, bf16[96,2048]{1,0:T(8,128)(2,1)S(1)} %collective-permute-done.35, bf16[96,2048]{1,0:T(8,128)(2,1)S(1)} %get-tuple-element.20, ...), kind=kOutput, calls=%fused_computation.1 | convolution fusion | flops 2023489536 | bytes 13041664 | tf_op jit(solution)/shard_map/unembed_grad/dot_general | solution.py:12
  238.6 1.3 collective-permute-start.34
  240.6 3.5 %collective-permute-done.34 = bf16[48,1280]{1,0:T(8,128)(2,1)S(1)} collective-permute-done((bf16[48,1280]{1,0:T(8,128)(2,1)S(1)}, bf16[48,1280]{1,0:T(8,128)(2,1)S(1)}, u32[]{:S(2)}, u32[]{:S(2)}) %collective-permute-start.34) | collective-permute-done | bytes 122912 | tf_op jit(solution)/shard_map/joined_grad/ppermute | solution.py:32
  (106 shorter events, 15.5 us)
Async XLA Ops:
  0.6 6.6 %collective-permute-start.4 = (bf16[48,1280]{1,0:T(8,128)(2,1)}, bf16[48,1280]{1,0:T(8,128)(2,1)S(1)}, u32[]{:S(2)}, u32[]{:S(2)}) collective-permute-start(bf16[48,1280]{1,0:T(8,128)(2,1)} %param.8), channel_id=1, source_target_pairs={{0,1},{1,0},{2,3},{3,2},{4,5},{5,4},{6,7},{7,6},{8,9},{9,8},{10,11... | collective-permute-start | bytes 368648 | tf_op jit(solution)/shard_map/inputs/ppermute | solution.py:36
  8.2 4.9 %collective-permute-start = (bf16[48,1280]{1,0:T(8,128)(2,1)S(1)}, bf16[48,1280]{1,0:T(8,128)(2,1)S(1)}, u32[]{:S(2)}, u32[]{:S(2)}) collective-permute-start(bf16[48,1280]{1,0:T(8,128)(2,1)S(1)} %get-tuple-element.37), channel_id=1, source_target_pairs={{0,1},{1,0},{2,3},{3,2},{4,5},{5,4},{6,7},{7,6},{8,9},{9,8},{10,11... | collective-permute-start | bytes 368648 | tf_op jit(solution)/shard_map/inputs/ppermute | solution.py:36
  14.8 18.5 %collective-permute-start.2 = (bf16[96,1280]{1,0:T(8,128)(2,1)S(1)}, bf16[96,1280]{1,0:T(8,128)(2,1)S(1)}, u32[]{:S(2)}, u32[]{:S(2)}) collective-permute-start(bf16[96,1280]{1,0:T(8,128)(2,1)S(1)} %get-tuple-element.34), channel_id=1, source_target_pairs={{0,4},{2,6},{4,0},{6,2},{1,5},{3,7},{5,1},{7,3},{8,12},{10,14},{12... | collective-permute-start | bytes 737288 | tf_op jit(solution)/shard_map/inputs/ppermute | solution.py:28
  17.7 15.8 %collective-permute-start.1 = (bf16[96,1280]{1,0:T(8,128)(2,1)S(1)}, bf16[96,1280]{1,0:T(8,128)(2,1)S(1)}, u32[]{:S(2)}, u32[]{:S(2)}) collective-permute-start(bf16[96,1280]{1,0:T(8,128)(2,1)S(1)} %get-tuple-element.34), channel_id=1, source_target_pairs={{0,2},{2,4},{4,6},{6,0},{1,3},{3,5},{5,7},{7,1},{8,10},{10,12},{12... | collective-permute-start | bytes 737288 | tf_op jit(solution)/shard_map/inputs/ppermute | solution.py:28
  19.2 14.6 %collective-permute-start.3 = (bf16[96,1280]{1,0:T(8,128)(2,1)S(1)}, bf16[96,1280]{1,0:T(8,128)(2,1)S(1)}, u32[]{:S(2)}, u32[]{:S(2)}) collective-permute-start(bf16[96,1280]{1,0:T(8,128)(2,1)S(1)} %get-tuple-element.34), channel_id=1, source_target_pairs={{0,6},{2,0},{4,2},{6,4},{1,7},{3,1},{5,3},{7,5},{8,14},{10,8},{12,... | collective-permute-start | bytes 737288 | tf_op jit(solution)/shard_map/inputs/ppermute | solution.py:28
  33.9 5.4 %copy-start = (bf16[96,1280]{1,0:T(8,128)(2,1)}, bf16[96,1280]{1,0:T(8,128)(2,1)S(1)}, u32[]{:S(2)}) copy-start(bf16[96,1280]{1,0:T(8,128)(2,1)S(1)} %collective-permute-done.3) | copy-start | bytes 737284
  34.0 7.8 %copy-start.5 = (f32[96]{0:T(128)}, f32[96]{0:T(128)S(1)}, u32[]{:S(2)}) copy-start(f32[96]{0:T(128)S(1)} %add_rsqrt_fusion.1) | copy-start | bytes 1156
  39.2 12.2 %copy-start.3 = (f32[1280]{0:T(1024)S(1)}, f32[1280]{0:T(1024)}, u32[]{:S(2)}) copy-start(f32[1280]{0:T(1024)} %param.11) | copy-start | bytes 15364
  44.5 6.3 %collective-permute-start.5 = (bf16[96,1280]{1,0:T(8,128)(2,1)S(1)}, bf16[96,1280]{1,0:T(8,128)(2,1)S(1)}, u32[]{:S(2)}, u32[]{:S(2)}) collective-permute-start(bf16[96,1280]{1,0:T(8,128)(2,1)S(1)} %get-tuple-element.49), channel_id=1, source_target_pairs={{0,1},{1,0},{2,3},{3,2},{4,5},{5,4},{6,7},{7,6},{8,9},{9,8},{10,11... | collective-permute-start | bytes 737288 | tf_op jit(solution)/shard_map/projection/ppermute | solution.py:36
  55.7 22.9 %collective-permute-start.9 = (f32[96,2048]{1,0:T(8,128)S(1)}, f32[96,2048]{1,0:T(8,128)}, u32[]{:S(2)}, u32[]{:S(2)}) collective-permute-start(f32[96,2048]{1,0:T(8,128)S(1)} %fusion.8), channel_id=1, source_target_pairs={{0,2},{6,4},{1,3},{7,5},{8,10},{14,12},{9,11},{15,13},{16,18},{22,... | collective-permute-start | bytes 2359304 | tf_op jit(solution)/shard_map/logits/ppermute | solution.py:106
  80.7 12.2 %collective-permute-start.12 = (f32[96,2048]{1,0:T(8,128)}, f32[96,2048]{1,0:T(8,128)S(1)}, u32[]{:S(2)}, u32[]{:S(2)}) collective-permute-start(f32[96,2048]{1,0:T(8,128)} %add_select_fusion), channel_id=1, source_target_pairs={{6,4},{4,2},{7,5},{5,3},{14,12},{12,10},{15,13},{13,11},{22,20},{2... | collective-permute-start | bytes 2359304 | tf_op jit(solution)/shard_map/logits/ppermute | solution.py:109
  81.4 19.9 %collective-permute-start.10 = (f32[96,2048]{1,0:T(8,128)}, f32[96,2048]{1,0:T(8,128)}, u32[]{:S(2)}, u32[]{:S(2)}) collective-permute-start(f32[96,2048]{1,0:T(8,128)} %add_select_fusion), channel_id=1, source_target_pairs={{0,2},{2,4},{1,3},{3,5},{8,10},{10,12},{9,11},{11,13},{16,18},{18,... | collective-permute-start | bytes 2359304 | tf_op jit(solution)/shard_map/logits/ppermute | solution.py:108
  88.7 20.5 %copy-start.8 = (f32[96]{0:T(128)S(1)}, f32[96]{0:T(128)}, u32[]{:S(2)}) copy-start(f32[96]{0:T(128)} %get-tuple-element.18) | copy-start | bytes 1156
  102.6 25.2 %copy-start.4 = (s32[1,96]{1,0:T(1,128)S(1)}, s32[1,96]{1,0:T(1,128)}, u32[]{:S(2)}) copy-start(s32[1,96]{1,0:T(1,128)} %param.13) | copy-start | bytes 1156
  102.7 34.7 %copy-start.1 = (bf16[96,1280]{1,0:T(8,128)(2,1)S(1)}, bf16[96,1280]{1,0:T(8,128)(2,1)}, u32[]{:S(2)}) copy-start(bf16[96,1280]{1,0:T(8,128)(2,1)} %copy-done) | copy-start | bytes 737284
  102.7 34.7 %copy-start.2 = (bf16[1,96,1280]{2,1,0:T(8,128)(2,1)S(1)}, bf16[1,96,1280]{2,1,0:T(8,128)(2,1)}, u32[]{:S(2)}) copy-start(bf16[1,96,1280]{2,1,0:T(8,128)(2,1)} %get-tuple-element.33) | copy-start | bytes 737284
  102.7 24.9 %collective-permute-start.11 = (f32[96,2048]{1,0:T(8,128)S(1)}, f32[96,2048]{1,0:T(8,128)S(1)}, u32[]{:S(2)}, u32[]{:S(2)}) collective-permute-start(f32[96,2048]{1,0:T(8,128)S(1)} %get-tuple-element.24), channel_id=1, source_target_pairs={{0,2},{2,4},{4,6},{1,3},{3,5},{5,7},{8,10},{10,12},{12,14},{9,11},... | collective-permute-start | bytes 2359304 | tf_op jit(solution)/shard_map/logits/ppermute | solution.py:112
  107.9 19.7 %collective-permute-start.13 = (f32[96,2048]{1,0:T(8,128)S(1)}, f32[96,2048]{1,0:T(8,128)S(1)}, u32[]{:S(2)}, u32[]{:S(2)}) collective-permute-start(f32[96,2048]{1,0:T(8,128)S(1)} %get-tuple-element.25), channel_id=1, source_target_pairs={{6,4},{4,2},{2,0},{7,5},{5,3},{3,1},{14,12},{12,10},{10,8},{15,13}... | collective-permute-start | bytes 2359304 | tf_op jit(solution)/shard_map/logits/ppermute | solution.py:113
  109.2 30.2 %copy-start.7 = (f32[1,96]{1,0:T(1,128)S(1)}, f32[1,96]{1,0:T(1,128)}, u32[]{:S(2)}) copy-start(f32[1,96]{1,0:T(1,128)} %param.14) | copy-start | bytes 1156
  109.3 17.2 %collective-permute-start.8 = (f32[96]{0:T(128)S(1)}, f32[96]{0:T(128)S(1)}, u32[]{:S(2)}, u32[]{:S(2)}) collective-permute-start(f32[96]{0:T(128)S(1)} %copy-done.8), channel_id=1, source_target_pairs={{0,6},{2,0},{4,2},{6,4},{1,7},{3,1},{5,3},{7,5},{8,14},{10,8},{12,... | collective-permute-start | bytes 1160 | tf_op jit(solution)/shard_map/mixed_scale/ppermute | solution.py:28
  113.3 14.2 %collective-permute-start.7 = (f32[96]{0:T(128)S(1)}, f32[96]{0:T(128)S(1)}, u32[]{:S(2)}, u32[]{:S(2)}) collective-permute-start(f32[96]{0:T(128)S(1)} %copy-done.8), channel_id=1, source_target_pairs={{0,4},{2,6},{4,0},{6,2},{1,5},{3,7},{5,1},{7,3},{8,12},{10,14},{12... | collective-permute-start | bytes 1160 | tf_op jit(solution)/shard_map/mixed_scale/ppermute | solution.py:28
  113.9 13.6 %collective-permute-start.6 = (f32[96]{0:T(128)S(1)}, f32[96]{0:T(128)S(1)}, u32[]{:S(2)}, u32[]{:S(2)}) collective-permute-start(f32[96]{0:T(128)S(1)} %copy-done.8), channel_id=1, source_target_pairs={{0,2},{2,4},{4,6},{6,0},{1,3},{3,5},{5,7},{7,1},{8,10},{10,12},{12... | collective-permute-start | bytes 1160 | tf_op jit(solution)/shard_map/mixed_scale/ppermute | solution.py:28
  128.2 3.6 %collective-permute-start.16 = (f32[3,96]{1,0:T(4,128)S(1)}, f32[3,96]{1,0:T(4,128)S(1)}, u32[]{:S(2)}, u32[]{:S(2)}) collective-permute-start(f32[3,96]{1,0:T(4,128)S(1)} %pad_maximum_fusion.3), channel_id=1, source_target_pairs={{0,6},{2,0},{4,2},{6,4},{1,7},{3,1},{5,3},{7,5},{8,14},{10,8},{12,... | collective-permute-start | bytes 3464 | tf_op jit(solution)/shard_map/softmax/ppermute | solution.py:28
  128.3 4.5 %collective-permute-start.15 = (f32[3,96]{1,0:T(4,128)S(1)}, f32[3,96]{1,0:T(4,128)S(1)}, u32[]{:S(2)}, u32[]{:S(2)}) collective-permute-start(f32[3,96]{1,0:T(4,128)S(1)} %pad_maximum_fusion.3), channel_id=1, source_target_pairs={{0,4},{2,6},{4,0},{6,2},{1,5},{3,7},{5,1},{7,3},{8,12},{10,14},{12... | collective-permute-start | bytes 3464 | tf_op jit(solution)/shard_map/softmax/ppermute | solution.py:28
  130.4 5.4 %collective-permute-start.14 = (f32[3,96]{1,0:T(4,128)S(1)}, f32[3,96]{1,0:T(4,128)S(1)}, u32[]{:S(2)}, u32[]{:S(2)}) collective-permute-start(f32[3,96]{1,0:T(4,128)S(1)} %pad_maximum_fusion.3), channel_id=1, source_target_pairs={{0,2},{2,4},{4,6},{6,0},{1,3},{3,5},{5,7},{7,1},{8,10},{10,12},{12... | collective-permute-start | bytes 3464 | tf_op jit(solution)/shard_map/softmax/ppermute | solution.py:28
  135.8 3.7 %collective-permute-start.17 = (f32[3,96]{1,0:T(4,128)S(1)}, f32[3,96]{1,0:T(4,128)S(1)}, u32[]{:S(2)}, u32[]{:S(2)}) collective-permute-start(f32[3,96]{1,0:T(4,128)S(1)} %pad_maximum_fusion.4), channel_id=1, source_target_pairs={{0,1},{1,0},{2,3},{3,2},{4,5},{5,4},{6,7},{7,6},{8,9},{9,8},{10,11... | collective-permute-start | bytes 3464 | tf_op jit(solution)/shard_map/softmax/ppermute | solution.py:36
  140.2 5.6 %collective-permute-start.24 = (f32[96]{0:T(128)S(1)}, f32[96]{0:T(128)S(1)}, u32[]{:S(2)}, u32[]{:S(2)}) collective-permute-start(f32[96]{0:T(128)S(1)} %multiply_reduce_fusion), channel_id=1, source_target_pairs={{0,6},{2,0},{4,2},{6,4},{1,7},{3,1},{5,3},{7,5},{8,14},{10,8},{12,... | collective-permute-start | bytes 1160 | tf_op jit(solution)/shard_map/softmax/ppermute | solution.py:28
  140.7 8.0 %collective-permute-start.23 = (f32[96]{0:T(128)S(1)}, f32[96]{0:T(128)S(1)}, u32[]{:S(2)}, u32[]{:S(2)}) collective-permute-start(f32[96]{0:T(128)S(1)} %multiply_reduce_fusion), channel_id=1, source_target_pairs={{0,4},{2,6},{4,0},{6,2},{1,5},{3,7},{5,1},{7,3},{8,12},{10,14},{12... | collective-permute-start | bytes 1160 | tf_op jit(solution)/shard_map/softmax/ppermute | solution.py:28
  140.7 8.0 %collective-permute-start.22 = (f32[96]{0:T(128)S(1)}, f32[96]{0:T(128)S(1)}, u32[]{:S(2)}, u32[]{:S(2)}) collective-permute-start(f32[96]{0:T(128)S(1)} %multiply_reduce_fusion), channel_id=1, source_target_pairs={{0,2},{2,4},{4,6},{6,0},{1,3},{3,5},{5,7},{7,1},{8,10},{10,12},{12... | collective-permute-start | bytes 1160 | tf_op jit(solution)/shard_map/softmax/ppermute | solution.py:28
  142.3 33.0 %collective-permute-start.20 = (bf16[96,2048]{1,0:T(8,128)(2,1)S(1)}, bf16[96,2048]{1,0:T(8,128)(2,1)S(1)}, u32[]{:S(2)}, u32[]{:S(2)}) collective-permute-start(bf16[96,2048]{1,0:T(8,128)(2,1)S(1)} %get-tuple-element.7), channel_id=1, source_target_pairs={{0,6},{2,0},{4,2},{6,4},{1,7},{3,1},{5,3},{7,5},{8,14},{10,8},{12,... | collective-permute-start | bytes 1179656 | tf_op jit(solution)/shard_map/softmax/ppermute | solution.py:28
  144.7 26.9 %collective-permute-start.19 = (bf16[96,2048]{1,0:T(8,128)(2,1)S(1)}, bf16[96,2048]{1,0:T(8,128)(2,1)S(1)}, u32[]{:S(2)}, u32[]{:S(2)}) collective-permute-start(bf16[96,2048]{1,0:T(8,128)(2,1)S(1)} %get-tuple-element.7), channel_id=1, source_target_pairs={{0,4},{2,6},{4,0},{6,2},{1,5},{3,7},{5,1},{7,3},{8,12},{10,14},{12... | collective-permute-start | bytes 1179656 | tf_op jit(solution)/shard_map/softmax/ppermute | solution.py:28
  145.8 33.3 %collective-permute-start.18 = (bf16[96,2048]{1,0:T(8,128)(2,1)S(1)}, bf16[96,2048]{1,0:T(8,128)(2,1)S(1)}, u32[]{:S(2)}, u32[]{:S(2)}) collective-permute-start(bf16[96,2048]{1,0:T(8,128)(2,1)S(1)} %get-tuple-element.7), channel_id=1, source_target_pairs={{0,2},{2,4},{4,6},{6,0},{1,3},{3,5},{5,7},{7,1},{8,10},{10,12},{12... | collective-permute-start | bytes 1179656 | tf_op jit(solution)/shard_map/softmax/ppermute | solution.py:28
  148.7 5.2 %collective-permute-start.25 = (f32[96]{0:T(128)S(1)}, f32[96]{0:T(128)S(1)}, u32[]{:S(2)}, u32[]{:S(2)}) collective-permute-start(f32[96]{0:T(128)S(1)} %add_add_fusion.1), channel_id=1, source_target_pairs={{0,1},{1,0},{2,3},{3,2},{4,5},{5,4},{6,7},{7,6},{8,9},{9,8},{10,11... | collective-permute-start | bytes 1160 | tf_op jit(solution)/shard_map/softmax/ppermute | solution.py:36
  150.3 41.1 %slice-start = ((s8[13107200]{0:T(1024)(128)(4,1)}), s8[4194304]{0:T(1024)(128)(4,1)S(1)}, s32[]{:S(2)}) async-start(s8[13107200]{0:T(1024)(128)(4,1)} %bitcast.245), calls=%async_computation | async-start | bytes 8388608
  171.7 19.7 %slice-start.1 = ((s8[13107200]{0:T(1024)(128)(4,1)}), s8[4194304]{0:T(1024)(128)(4,1)S(1)}, s32[]{:S(2)}) async-start(s8[13107200]{0:T(1024)(128)(4,1)} %bitcast.245), calls=%async_computation.1 | async-start | bytes 8388608
  175.3 16.0 %slice-start.2 = ((s8[13107200]{0:T(1024)(128)(4,1)}), s8[4194304]{0:T(1024)(128)(4,1)S(1)}, s32[]{:S(2)}) async-start(s8[13107200]{0:T(1024)(128)(4,1)} %bitcast.245), calls=%async_computation.2 | async-start | bytes 8388608
  179.0 12.3 %slice-start.3 = ((s8[13107200]{0:T(1024)(128)(4,1)}), s8[524288]{0:T(1024)(128)(4,1)S(1)}, s32[]{:S(2)}) async-start(s8[13107200]{0:T(1024)(128)(4,1)} %bitcast.245), calls=%async_computation.3 | async-start | bytes 1048576
  182.7 6.3 %collective-permute-start.21 = (bf16[96,1280]{1,0:T(8,128)(2,1)S(1)}, bf16[96,1280]{1,0:T(8,128)(2,1)S(1)}, u32[]{:S(2)}, u32[]{:S(2)}) collective-permute-start(bf16[96,1280]{1,0:T(8,128)(2,1)S(1)} %get-tuple-element.51), channel_id=1, source_target_pairs={{0,1},{1,0},{2,3},{3,2},{4,5},{5,4},{6,7},{7,6},{8,9},{9,8},{10,11... | collective-permute-start | bytes 737288 | tf_op jit(solution)/shard_map/grad_normed/ppermute | solution.py:36
  189.3 8.6 %collective-permute-start.31 = (f32[96]{0:T(128)S(1)}, f32[96]{0:T(128)S(1)}, u32[]{:S(2)}, u32[]{:S(2)}) collective-permute-start(f32[96]{0:T(128)S(1)} %get-tuple-element.8), channel_id=1, source_target_pairs={{0,6},{2,0},{4,2},{6,4},{1,7},{3,1},{5,3},{7,5},{8,14},{10,8},{12,... | collective-permute-start | bytes 1160 | tf_op jit(solution)/shard_map/joined_grad/ppermute | solution.py:28
  189.3 11.6 %collective-permute-start.30 = (f32[96]{0:T(128)S(1)}, f32[96]{0:T(128)S(1)}, u32[]{:S(2)}, u32[]{:S(2)}) collective-permute-start(f32[96]{0:T(128)S(1)} %get-tuple-element.8), channel_id=1, source_target_pairs={{0,4},{2,6},{4,0},{6,2},{1,5},{3,7},{5,1},{7,3},{8,12},{10,14},{12... | collective-permute-start | bytes 1160 | tf_op jit(solution)/shard_map/joined_grad/ppermute | solution.py:28
  189.4 11.6 %collective-permute-start.29 = (f32[96]{0:T(128)S(1)}, f32[96]{0:T(128)S(1)}, u32[]{:S(2)}, u32[]{:S(2)}) collective-permute-start(f32[96]{0:T(128)S(1)} %get-tuple-element.8), channel_id=1, source_target_pairs={{0,2},{2,4},{4,6},{6,0},{1,3},{3,5},{5,7},{7,1},{8,10},{10,12},{12... | collective-permute-start | bytes 1160 | tf_op jit(solution)/shard_map/joined_grad/ppermute | solution.py:28
  192.5 17.9 %copy-start.6 = (f32[96]{0:T(128)S(1)}, f32[96]{0:T(128)}, u32[]{:S(2)}) copy-start(f32[96]{0:T(128)} %copy-done.5) | copy-start | bytes 1156
  194.8 8.3 %collective-permute-start.26 = (bf16[96,1280]{1,0:T(8,128)(2,1)S(1)}, bf16[96,1280]{1,0:T(8,128)(2,1)S(1)}, u32[]{:S(2)}, u32[]{:S(2)}) collective-permute-start(bf16[96,1280]{1,0:T(8,128)(2,1)S(1)} %fusion.61), channel_id=1, source_target_pairs={{0,2},{2,4},{4,6},{6,0},{1,3},{3,5},{5,7},{7,1},{8,10},{10,12},{12... | collective-permute-start | bytes 737288 | tf_op jit(solution)/shard_map/joined_grad/ppermute | solution.py:28
  196.4 14.0 %collective-permute-start.27 = (bf16[96,1280]{1,0:T(8,128)(2,1)S(1)}, bf16[96,1280]{1,0:T(8,128)(2,1)S(1)}, u32[]{:S(2)}, u32[]{:S(2)}) collective-permute-start(bf16[96,1280]{1,0:T(8,128)(2,1)S(1)} %fusion.64), channel_id=1, source_target_pairs={{0,4},{2,6},{4,0},{6,2},{1,5},{3,7},{5,1},{7,3},{8,12},{10,14},{12... | collective-permute-start | bytes 737288 | tf_op jit(solution)/shard_map/joined_grad/ppermute | solution.py:28
  197.9 12.5 %collective-permute-start.28 = (bf16[96,1280]{1,0:T(8,128)(2,1)S(1)}, bf16[96,1280]{1,0:T(8,128)(2,1)S(1)}, u32[]{:S(2)}, u32[]{:S(2)}) collective-permute-start(bf16[96,1280]{1,0:T(8,128)(2,1)S(1)} %fusion.67), channel_id=1, source_target_pairs={{0,6},{2,0},{4,2},{6,4},{1,7},{3,1},{5,3},{7,5},{8,14},{10,8},{12,... | collective-permute-start | bytes 737288 | tf_op jit(solution)/shard_map/joined_grad/ppermute | solution.py:28
  200.9 23.5 %collective-permute-start.37 = (bf16[96,2048]{1,0:T(8,128)(2,1)S(1)}, bf16[96,2048]{1,0:T(8,128)(2,1)S(1)}, u32[]{:S(2)}, u32[]{:S(2)}) collective-permute-start(bf16[96,2048]{1,0:T(8,128)(2,1)S(1)} %get-tuple-element.21), channel_id=1, source_target_pairs={{0,24},{8,16},{16,8},{24,0},{1,25},{9,17},{17,9},{25,1},{2,26},{10... | collective-permute-start | bytes 1179656 | tf_op jit(solution)/shard_map/unembed_grad/ppermute | solution.py:32
  201.0 25.0 %collective-permute-start.36 = (bf16[96,2048]{1,0:T(8,128)(2,1)S(1)}, bf16[96,2048]{1,0:T(8,128)(2,1)S(1)}, u32[]{:S(2)}, u32[]{:S(2)}) collective-permute-start(bf16[96,2048]{1,0:T(8,128)(2,1)S(1)} %get-tuple-element.22), channel_id=1, source_target_pairs={{0,16},{8,24},{16,0},{24,8},{1,17},{9,25},{17,1},{25,9},{2,18},{10... | collective-permute-start | bytes 1179656 | tf_op jit(solution)/shard_map/unembed_grad/ppermute | solution.py:32
  203.1 23.4 %collective-permute-start.35 = (bf16[96,2048]{1,0:T(8,128)(2,1)S(1)}, bf16[96,2048]{1,0:T(8,128)(2,1)S(1)}, u32[]{:S(2)}, u32[]{:S(2)}) collective-permute-start(bf16[96,2048]{1,0:T(8,128)(2,1)S(1)} %get-tuple-element.23), channel_id=1, source_target_pairs={{0,8},{8,0},{16,24},{24,16},{1,9},{9,1},{17,25},{25,17},{2,10},{10... | collective-permute-start | bytes 1179656 | tf_op jit(solution)/shard_map/unembed_grad/ppermute | solution.py:32
  210.4 16.1 %collective-permute-start.40 = (bf16[96,1280]{1,0:T(8,128)(2,1)S(1)}, bf16[96,1280]{1,0:T(8,128)(2,1)S(1)}, u32[]{:S(2)}, u32[]{:S(2)}) collective-permute-start(bf16[96,1280]{1,0:T(8,128)(2,1)S(1)} %get-tuple-element.30), channel_id=1, source_target_pairs={{0,24},{8,16},{16,8},{24,0},{1,25},{9,17},{17,9},{25,1},{2,26},{10... | collective-permute-start | bytes 737288 | tf_op jit(solution)/shard_map/mixed_scale/ppermute | solution.py:32
  211.6 14.3 %collective-permute-start.32 = (bf16[48,1280]{1,0:T(8,128)(2,1)S(1)}, bf16[48,1280]{1,0:T(8,128)(2,1)S(1)}, u32[]{:S(2)}, u32[]{:S(2)}) collective-permute-start(bf16[48,1280]{1,0:T(8,128)(2,1)S(1)} %select_convert_fusion.4), channel_id=1, source_target_pairs={{0,1},{1,0},{2,3},{3,2},{4,5},{5,4},{6,7},{7,6},{8,9},{9,8},{10,11... | collective-permute-start | bytes 368648 | tf_op jit(solution)/shard_map/joined_grad/ppermute | solution.py:36
  224.4 8.5 %collective-permute-start.39 = (bf16[96,1280]{1,0:T(8,128)(2,1)S(1)}, bf16[96,1280]{1,0:T(8,128)(2,1)S(1)}, u32[]{:S(2)}, u32[]{:S(2)}) collective-permute-start(bf16[96,1280]{1,0:T(8,128)(2,1)S(1)} %get-tuple-element.30), channel_id=1, source_target_pairs={{0,16},{8,24},{16,0},{24,8},{1,17},{9,25},{17,1},{25,9},{2,18},{10... | collective-permute-start | bytes 737288 | tf_op jit(solution)/shard_map/mixed_scale/ppermute | solution.py:32
  225.9 7.0 %collective-permute-start.38 = (bf16[96,1280]{1,0:T(8,128)(2,1)S(1)}, bf16[96,1280]{1,0:T(8,128)(2,1)S(1)}, u32[]{:S(2)}, u32[]{:S(2)}) collective-permute-start(bf16[96,1280]{1,0:T(8,128)(2,1)S(1)} %get-tuple-element.30), channel_id=1, source_target_pairs={{0,8},{8,0},{16,24},{24,16},{1,9},{9,1},{17,25},{25,17},{2,10},{10... | collective-permute-start | bytes 737288 | tf_op jit(solution)/shard_map/mixed_scale/ppermute | solution.py:32
  226.0 12.5 %collective-permute-start.33 = (bf16[48,1280]{1,0:T(8,128)(2,1)S(1)}, bf16[48,1280]{1,0:T(8,128)(2,1)S(1)}, u32[]{:S(2)}, u32[]{:S(2)}) collective-permute-start(bf16[48,1280]{1,0:T(8,128)(2,1)S(1)} %fusion.97), channel_id=1, source_target_pairs={{0,8},{8,0},{16,24},{24,16},{1,9},{9,1},{17,25},{25,17},{2,10},{10... | collective-permute-start | bytes 368648 | tf_op jit(solution)/shard_map/joined_grad/ppermute | solution.py:32
  238.6 5.5 %collective-permute-start.34 = (bf16[48,1280]{1,0:T(8,128)(2,1)S(1)}, bf16[48,1280]{1,0:T(8,128)(2,1)S(1)}, u32[]{:S(2)}, u32[]{:S(2)}) collective-permute-start(bf16[48,1280]{1,0:T(8,128)(2,1)S(1)} %add_convert_fusion), channel_id=1, source_target_pairs={{0,16},{8,24},{16,0},{24,8},{1,17},{9,25},{17,1},{25,9},{2,18},{10... | collective-permute-start | bytes 368648 | tf_op jit(solution)/shard_map/joined_grad/ppermute | solution.py:32

commit v2 on v1

--- a/solution.py
+++ b/solution.py
@@ -1,11 +1,16 @@
 import jax
 import jax.numpy as jnp
 from jax import lax
+from jax.experimental import pallas as pl
+from jax.experimental.pallas import tpu as pltpu
 from jax.sharding import PartitionSpec as P
 
 epsilon = 1e-05
 f32 = jnp.float32
 bf16 = jnp.bfloat16
+kernel_memory = 12 << 20
+stream_memory = 44 << 20
+brief = pl.CostEstimate(flops=0, bytes_accessed=0, transcendentals=0)
 
 
 def contract_rows(left, right):
@@ -34,6 +39,221 @@
 
 def swap(value):
     return lax.ppermute(value, "dp", [(0, 1), (1, 0)])
+
+
+def chunk_copy(weight, which, size, block, held, done, j):
+    start = pl.multiple_of(which[0] * size + j * block, block)
+    return pltpu.make_async_copy(weight.at[pl.ds(start, block)], held.at[j], done.at[j])
+
+
+def stream_columns_kernel(which, left, weight, out, held, done):
+    blocks, block, _ = held.shape
+    copies = [
+        chunk_copy(weight, which, blocks * block, block, held, done, j) for j in range(blocks)
+    ]
+    for copy in copies:
+        copy.start()
+    for j, copy in enumerate(copies):
+        copy.wait()
+        out[:, j * block : (j + 1) * block] = contract_cols(left[...], held[j]).astype(out.dtype)
+
+
+def stream_rows_kernel(which, left, weight, out, held, done):
+    blocks, block, _ = held.shape
+    copies = [
+        chunk_copy(weight, which, blocks * block, block, held, done, j) for j in range(blocks)
+    ]
+    for copy in copies:
+        copy.start()
+    for j, copy in enumerate(copies):
+        copy.wait()
+        product = plain_dot(left[:, j * block : (j + 1) * block], held[j])
+        if j == 0:
+            out[...] = product
+        else:
+            out[...] += product
+
+
+def stream(kernel, left, weight, which, size, out_width, blocks):
+    rows = left.shape[0]
+    width = weight.shape[1]
+    block = size // blocks
+    return pl.pallas_call(
+        kernel,
+        out_shape=jax.ShapeDtypeStruct((rows, out_width), f32),
+        in_specs=[
+            pl.BlockSpec(memory_space=pltpu.SMEM),
+            pl.BlockSpec(memory_space=pltpu.VMEM),
+            pl.BlockSpec(memory_space=pl.ANY),
+        ],
+        out_specs=pl.BlockSpec(memory_space=pltpu.VMEM),
+        scratch_shapes=[
+            pltpu.VMEM((blocks, block, width), weight.dtype),
+            pltpu.SemaphoreType.DMA((blocks,)),
+        ],
+        compiler_params=pltpu.CompilerParams(vmem_limit_bytes=stream_memory),
+        cost_estimate=brief,
+    )(which.reshape(1), left, weight)
+
+
+def stream_columns(left, weight, which, size, blocks):
+    return stream(stream_columns_kernel, left, weight, which, size, size, blocks)
+
+
+def stream_rows(left, weight, which, blocks):
+    return stream(
+        stream_rows_kernel, left, weight, which, left.shape[1], weight.shape[1], blocks
+    )
+
+
+def dot_columns_kernel(which, left, right, out):
+    out[...] = contract_cols(left[...], right[...]).astype(out.dtype)
+
+
+def dot_columns(left, weight, which, size, blocks, dtype):
+    rows, depth = left.shape
+    block = size // blocks
+    return pl.pallas_call(
+        dot_columns_kernel,
+        out_shape=jax.ShapeDtypeStruct((rows, size), dtype),
+        grid_spec=pltpu.PrefetchScalarGridSpec(
+            num_scalar_prefetch=1,
+            grid=(blocks,),
+            in_specs=[
+                pl.BlockSpec((rows, depth), lambda j, c: (0, 0)),
+                pl.BlockSpec((block, depth), lambda j, c: (c[0] * blocks + j, 0)),
+            ],
+            out_specs=pl.BlockSpec((rows, block), lambda j, c: (0, j)),
+        ),
+        compiler_params=pltpu.CompilerParams(vmem_limit_bytes=kernel_memory),
+        cost_estimate=brief,
+    )(which.reshape(1), left, weight)
+
+
+def dot_columns_apart_kernel(which, left, right, extra, *outs):
+    size = right.shape[0]
+    for k, out in enumerate(outs):
+
+        @pl.when(pl.program_id(0) == k)
+        def _():
+            out[:, :size] = contract_cols(left[...], right[...]).astype(out.dtype)
+            out[:, size:] = extra[...]
+
+
+def dot_columns_apart(left, weight, which, size, extra):
+    rows, depth = left.shape
+    wide = size + extra.shape[1]
+    return pl.pallas_call(
+        dot_columns_apart_kernel,
+        out_shape=[jax.ShapeDtypeStruct((rows, wide), bf16) for _ in which],
+        grid_spec=pltpu.PrefetchScalarGridSpec(
+            num_scalar_prefetch=1,
+            grid=(len(which),),
+            in_specs=[
+                pl.BlockSpec((rows, depth), lambda i, c: (0, 0)),
+                pl.BlockSpec((size, depth), lambda i, c: (c[i], 0)),
+                pl.BlockSpec(extra.shape, lambda i, c: (0, 0)),
+            ],
+            out_specs=[pl.BlockSpec((rows, wide), lambda i, c: (0, 0)) for _ in which],
+        ),
+        compiler_params=pltpu.CompilerParams(vmem_limit_bytes=kernel_memory),
+        cost_estimate=brief,
+    )(jnp.stack(which), left, weight, extra)
+
+
+def dot_rows_kernel(which, left, right, out):
+    product = plain_dot(left[...], right[...])
+
+    @pl.when(pl.program_id(0) == 0)
+    def _():
+        out[...] = product
+
+    @pl.when(pl.program_id(0) > 0)
+    def _():
+        out[...] += product
+
+
+def dot_rows_onto_kernel(which, left, right, base, out):
+    product = plain_dot(left[...], right[...])
+
+    @pl.when(pl.program_id(0) == 0)
+    def _():
+        out[...] = base[...] + product
+
+    @pl.when(pl.program_id(0) > 0)
+    def _():
+        out[...] += product
+
+
+def dot_rows(left, weight, which, blocks, base=None):
+    rows, size = left.shape
+    width = weight.shape[1]
+    block = size // blocks
+    whole = pl.BlockSpec((rows, width), lambda j, c: (0, 0))
+    return pl.pallas_call(
+        dot_rows_kernel if base is None else dot_rows_onto_kernel,
+        out_shape=jax.ShapeDtypeStruct((rows, width), f32),
+        grid_spec=pltpu.PrefetchScalarGridSpec(
+            num_scalar_prefetch=1,
+            grid=(blocks,),
+            in_specs=[
+                pl.BlockSpec((rows, block), lambda j, c: (0, j)),
+                pl.BlockSpec((block, width), lambda j, c: (c[0] * blocks + j, 0)),
+            ]
+            + ([] if base is None else [whole]),
+            out_specs=whole,
+        ),
+        compiler_params=pltpu.CompilerParams(vmem_limit_bytes=kernel_memory),
+        cost_estimate=brief,
+    )(which.reshape(1), left, weight, *([] if base is None else [base]))
+
+
+def combine_kernel(which, part, grad, out):
+    out[...] = contract_rows(part[0], grad[...])
+
+
+def combine_rows(parts, grad, order, blocks):
+    count, rows, width = parts.shape
+    block = width // blocks
+    return pl.pallas_call(
+        combine_kernel,
+        out_shape=jax.ShapeDtypeStruct((count * width, grad.shape[1]), f32),
+        grid_spec=pltpu.PrefetchScalarGridSpec(
+            num_scalar_prefetch=1,
+            grid=(count, blocks),
+            in_specs=[
+                pl.BlockSpec((1, rows, block), lambda c, j, w: (w[c], 0, j)),
+                pl.BlockSpec((rows, grad.shape[1]), lambda c, j, w: (0, 0)),
+            ],
+            out_specs=pl.BlockSpec((block, grad.shape[1]), lambda c, j, w: (c * blocks + j, 0)),
+        ),
+        compiler_params=pltpu.CompilerParams(vmem_limit_bytes=kernel_memory),
+        cost_estimate=brief,
+    )(order, parts, grad)
+
+
+def head_sum_kernel(*refs):
+    out = refs[-1]
+    count = (len(refs) - 1) // 2
+    left = jnp.concatenate([r[...] for r in refs[:count]], axis=0)
+    right = jnp.concatenate([r[...] for r in refs[count : 2 * count]], axis=0)
+    out[...] = contract_rows(left, right)
+
+
+def head_sum(grads, normed, blocks):
+    rows, size = grads[0].shape
+    width = normed[0].shape[1]
+    block = size // blocks
+    return pl.pallas_call(
+        head_sum_kernel,
+        out_shape=jax.ShapeDtypeStruct((size, width), f32),
+        grid=(blocks,),
+        in_specs=[pl.BlockSpec((rows, block), lambda j: (0, j))] * len(grads)
+        + [pl.BlockSpec((rows, width), lambda j: (0, 0))] * len(normed),
+        out_specs=pl.BlockSpec((block, width), lambda j: (j, 0)),
+        compiler_params=pltpu.CompilerParams(vmem_limit_bytes=kernel_memory),
+        cost_estimate=brief,
+    )(*grads, *normed)
 
 
 def fast_local(
@@ -48,7 +268,6 @@
     loss_scale,
 ):
     half, width = trunk_hidden.shape
-    rows = 2 * half
     features = width * n_tensor
     weight_block = combine_weight[0]
     vocab_part = unembed_weight.shape[0]
@@ -60,134 +279,185 @@
     targets = target_ids[0]
     row_weights = loss_scale[0]
 
-    def combine_rows(which):
-        return lax.dynamic_slice_in_dim(weight_block, which * width, width, 0)
-
-    def vocab_rows(which):
-        return lax.dynamic_slice_in_dim(unembed_weight, which * piece, piece, 0)
-
-    def around(by):
-        return lax.rem(t + by + n_tensor, n_tensor)
-
     def spread(value):
-        return [value] + [shift(value, "tensor", n_tensor, r) for r in range(1, n_tensor)]
+        return [value] + [flip(value, "tensor", n_tensor, r) for r in range(1, n_tensor)]
 
     with jax.named_scope("inputs"):
         embeds = next_embeds[0]
-        other = swap(jnp.where(first, embeds, trunk_hidden))
         kept = jnp.where(first, trunk_hidden, embeds)
-        trunk_other = swap(trunk_hidden)
-        trunk_rows = jnp.concatenate(
-            [jnp.where(first, trunk_hidden, trunk_other), jnp.where(first, trunk_other, trunk_hidden)], axis=0
+        given = jnp.where(first, embeds, trunk_hidden)
+        kept_parts = spread(kept)
+        swapped = swap(jnp.concatenate([given, trunk_hidden], axis=0))
+        kept_parts, swapped = lax.optimization_barrier((kept_parts, swapped))
+        given_parts = spread(swapped[:half])
+
+        def all_rows(k, g):
+            return jnp.concatenate([jnp.where(first, k, g), jnp.where(first, g, k)], axis=0)
+
+        own = all_rows(kept_parts[0], given_parts[0])
+        raw = dot_rows(own, weight_block, t, 2)
+        given_parts, raw = lax.optimization_barrier((given_parts, raw))
+        parts = [own] + [all_rows(k, g) for k, g in zip(kept_parts[1:], given_parts[1:])]
+        trunk_rows = jnp.where(
+            first, own, jnp.concatenate([swapped[half:], trunk_hidden], axis=0)
         ).astype(f32)
-        own = jnp.concatenate(
-            [jnp.where(first, kept, other), jnp.where(first, other, kept)], axis=0
-        )
-        parts = spread(own)
     with jax.named_scope("projection"):
         square_sum = sum(jnp.sum(jnp.square(p.astype(f32)), axis=1) for p in parts)
         in_scale = lax.rsqrt(square_sum / features + epsilon)
-        raw = sum(plain_dot(p, combine_rows(around(-r))) for r, p in enumerate(parts))
+        for r in range(1, n_tensor):
+            raw = dot_rows(parts[r], weight_block, t ^ r, 2, raw)
         projected = raw * in_scale[:, None]
         mixed = trunk_rows + (projected + swap(projected.astype(bf16)).astype(f32))
         gained = mixed * final_gain[None, :]
         low = gained.astype(bf16)
-    with jax.named_scope("mixed_scale"):
-        mixed_sums = sum(spread(jnp.sum(mixed * mixed, axis=1)))
-        mixed_scale = lax.rsqrt(mixed_sums / features + epsilon)
+    with jax.named_scope("logits"):
+        far = stream_columns(low, unembed_weight, t ^ 3, piece, 4)
+        ends = lax.ppermute(far, "tensor", [(0, 1), (3, 2)])
+        middle = lax.ppermute(far, "tensor", [(1, 2), (2, 1)])
+        mixed_squares = spread(jnp.sum(mixed * mixed, axis=1))
+        cross, near, last = [
+            stream_columns(low, unembed_weight, t ^ r, piece, 4) for r in (2, 1, 0)
+        ]
+        wanted = targets - d * vocab_part
+        ends, middle, mixed_squares, cross, near, last, wanted = lax.optimization_barrier(
+            (ends, middle, mixed_squares, cross, near, last, wanted)
+        )
+        mixed_scale = lax.rsqrt(sum(mixed_squares) / features + epsilon)
         normed_out = (gained * mixed_scale[:, None]).astype(bf16)
         normed_heads = [normed_out] + [
             flip(normed_out, "head", n_head, m) for m in range(1, n_head)
         ]
-    with jax.named_scope("logits"):
-        table = jnp.array([[3, 2, 1, 0], [3, 2, 0, 1], [0, 1, 3, 2], [0, 1, 2, 3]], jnp.int32)
-        order = table[t]
-        slots = [contract_cols(low, vocab_rows(order[j])) for j in range(4)]
-        one = lax.ppermute(slots[0], "tensor", [(0, 1), (3, 2)])
-        two = jnp.where((t == 0) | (t == 3), slots[1], slots[0] + one)
-        right = lax.ppermute(two, "tensor", [(0, 1), (1, 2)])
-        left = lax.ppermute(two, "tensor", [(3, 2), (2, 1)])
-        right = jnp.where(t == 1, slots[1], slots[2]) + right
-        left = jnp.where(t == 2, slots[1], slots[2]) + left
-        right = lax.ppermute(right, "tensor", [(0, 1), (1, 2), (2, 3)])
-        left = lax.ppermute(left, "tensor", [(3, 2), (2, 1), (1, 0)])
-        logits = (slots[3] + right + left) * mixed_scale[:, None]
+        cross = flip(cross + ends, "tensor", n_tensor, 2)
+        near = flip(near, "tensor", n_tensor, 1)
+        chosen = lax.broadcasted_iota(jnp.int32, (1, vocab_part), 1) == wanted[:, None]
+        target_rows = stream_rows(chosen.astype(bf16), unembed_weight, jnp.int32(0), 16)
+        cross, near, normed_heads, target_rows = lax.optimization_barrier(
+            (cross, near, normed_heads, target_rows)
+        )
+        logits = (last + middle + cross + near) * mixed_scale[:, None]
+        mixed_normed = mixed * mixed_scale[:, None]
     with jax.named_scope("softmax"):
-        ids = lax.broadcasted_iota(jnp.int32, (1, piece), 1) + d * vocab_part
-        hits = (ids + t * piece) == targets[:, None]
+        ids = lax.broadcasted_iota(jnp.int32, (1, piece), 1)
+        hits = (ids + t * piece) == wanted[:, None]
         top = jnp.max(logits, axis=1)
         shifted = jnp.exp(logits - top[:, None])
         total = jnp.sum(shifted, axis=1)
         at_target = jnp.sum(jnp.where(hits, logits, 0.0), axis=1)
-        stats = spread(jnp.stack([top, total, at_target]))
-        shifted_low = shifted.astype(bf16)
-        shifted_parts = spread(shifted_low)
-        tops = [s[0] for s in stats]
-        part_top = jnp.max(jnp.stack(tops), axis=0)
-        part_sum = sum(s[1] * jnp.exp(s[0] - part_top) for s in stats)
-        part_hit = sum(s[2] for s in stats)
-        there = swap(jnp.stack([part_top, part_sum, part_hit]))
-        largest = jnp.maximum(part_top, there[0])
-        summed = part_sum * jnp.exp(part_top - largest) + there[1] * jnp.exp(there[0] - largest)
-        hit_grad = row_weights * (jnp.exp(part_hit + there[2] - largest) / summed - 1.0)
+        shifted_low = jnp.where(hits, 0.0, shifted).astype(bf16)
+        weighted = jnp.sum(shifted_low.astype(f32) * logits, axis=1)
+        stats = jnp.stack([top, total, at_target, weighted])
+    with jax.named_scope("grad_normed"):
+        cross = flip(shifted_low, "tensor", n_tensor, 2)
+        near = flip(shifted_low, "tensor", n_tensor, 1)
+        there = swap(stats)
+        products = [stream_rows(shifted_low, unembed_weight, t, 4)]
+        cross, near, there, products = lax.optimization_barrier((cross, near, there, products))
+        ends = lax.ppermute(cross, "tensor", [(2, 3), (1, 0)])
+        middle = lax.ppermute(shifted_low, "tensor", [(1, 2), (2, 1)])
+        pair_top = jnp.maximum(top, there[0])
+        here_by, there_by = jnp.exp(top - pair_top), jnp.exp(there[0] - pair_top)
+        stats = spread(
+            jnp.stack(
+                [
+                    top,
+                    pair_top,
+                    total * here_by + there[1] * there_by,
+                    at_target + there[2],
+                    weighted * here_by + there[3] * there_by,
+                ]
+            )
+        )
+        products += [
+            stream_rows(e, unembed_weight, t ^ r, 4) for r, e in ((1, near), (2, cross))
+        ]
+        ends, middle, stats, products = lax.optimization_barrier((ends, middle, stats, products))
+        far = jnp.where((t == 0) | (t == n_tensor - 1), ends, middle)
+        products.append(stream_rows(far, unembed_weight, t ^ 3, 4))
+        shifted_parts = [shifted_low, near, cross, far]
+        largest = jnp.max(jnp.stack([s[1] for s in stats]), axis=0)
+        by = [jnp.exp(s[1] - largest) for s in stats]
+        summed = sum(s[2] * b for s, b in zip(stats, by))
+        hit_logit = sum(s[3] for s in stats)
+        per_row = row_weights / summed
+        hit_grad = row_weights * (jnp.exp(hit_logit - largest) / summed - 1.0)
+        grad_dots = per_row * sum(s[4] * b for s, b in zip(stats, by)) + hit_grad * hit_logit
+        factors = [per_row * jnp.exp(s[0] - largest) for s in stats]
+        grad_part = hit_grad[:, None] * target_rows
+        for factor, product in zip(factors, products):
+            grad_part = grad_part + factor[:, None] * product
+        grad_there = swap(grad_part.astype(bf16))
         grads = []
         for r, e in enumerate(shifted_parts):
-            factor = row_weights * jnp.exp(tops[r] - largest) / summed
-            mine = (ids + around(-r) * piece) == targets[:, None]
+            mine = (ids + (t ^ r) * piece) == wanted[:, None]
             grads.append(
-                jnp.where(mine, hit_grad[:, None], e.astype(f32) * factor[:, None]).astype(bf16)
+                jnp.where(
+                    mine, hit_grad[:, None], e.astype(f32) * factors[r][:, None]
+                ).astype(bf16)
             )
-        dots_part = sum(spread(jnp.sum(grads[0].astype(f32) * logits, axis=1)))
-        grad_dots = dots_part + swap(dots_part)
-    with jax.named_scope("grad_normed"):
-        grad_part = sum(plain_dot(g, vocab_rows(around(-r))) for r, g in enumerate(grads))
-        grad_normed = grad_part + swap(grad_part.astype(bf16)).astype(f32)
-        mixed_normed = mixed * mixed_scale[:, None]
+        grad_stack = jnp.stack(grads)
+        grad_slices = [
+            lax.dynamic_index_in_dim(grad_stack, t ^ h ^ m, 0, keepdims=False)
+            for m in range(n_head)
+        ]
+        grad_there, grad_slices = lax.optimization_barrier((grad_there, grad_slices))
+    with jax.named_scope("grad_mixed"):
+        grad_normed = grad_part + grad_there.astype(f32)
         grad_mixed = mixed_scale[:, None] * (
             grad_normed * final_gain[None, :] - mixed_normed * (grad_dots / features)[:, None]
         )
         grad_low = grad_mixed.astype(bf16)
+        grad_scaled = (in_scale[:, None] * grad_mixed).astype(bf16)
+        part_dots = jnp.sum(grad_low.astype(f32) * projected, axis=1)
+        dots_high = lax.reduce_precision(part_dots, 8, 7)
+        lane = lax.broadcasted_iota(jnp.int32, (1, 128), 1)
+        extra = jnp.where(
+            lane == 0,
+            dots_high[:, None],
+            jnp.where(lane == 1, (part_dots - dots_high)[:, None], 0.0),
+        ).astype(bf16)
     with jax.named_scope("joined_grad"):
-        dots = sum(spread(jnp.sum(grad_low.astype(f32) * projected, axis=1)))
-        side = [
-            shift(contract_cols(grad_low, combine_rows(around(r))).astype(bf16), "tensor", n_tensor, r)
-            for r in range(1, n_tensor)
-        ]
-        side = contract_cols(grad_low, combine_rows(t)) + sum(s.astype(f32) for s in side)
+        sent = dot_columns_apart(grad_low, weight_block, [t ^ 3, t ^ 2, t ^ 1], width, extra)
+        came = [flip(c, "tensor", n_tensor, r) for r, c in zip((3, 2, 1), sent)]
+        heads_far = [flip(grad_slices[m], "head", n_head, m) for m in range(2, n_head)]
+        side = dot_columns(grad_low, weight_block, t, width, 2, f32)
+        order = t ^ jnp.arange(n_tensor, dtype=jnp.int32)
+        combine_grad = combine_rows(jnp.stack(parts), grad_scaled, order, 2)[None]
+        came, heads_far, side, combine_grad = lax.optimization_barrier(
+            (came, heads_far, side, combine_grad)
+        )
+        for c in came:
+            side = side + c[:, :width].astype(f32)
+        dots = part_dots + sum(
+            c[:, width].astype(f32) + c[:, width + 1].astype(f32) for c in came
+        )
+    with jax.named_scope("input_grads"):
         own_normed = own.astype(f32) * in_scale[:, None]
         term = in_scale[:, None] * (side - own_normed * (dots / features)[:, None])
         term = jnp.where(first, term + grad_mixed, term)
-        theirs = swap(jnp.where(first, term[half:], term[:half]).astype(bf16)).astype(f32)
-        embed_grad = jnp.where(first, theirs, term[half:])[None]
-        trunk_sum = jnp.where(first, term[:half], theirs)
-        mask = 1
-        while mask < n_head:
-            trunk_low = trunk_sum.astype(bf16)
-            trunk_sum = trunk_low.astype(f32) + flip(trunk_low, "head", n_head, mask).astype(f32)
-            mask *= 2
-        trunk_grad = trunk_sum
-    with jax.named_scope("combine_grad"):
-        stacked = jnp.stack(parts)
-        ordered = jnp.concatenate(
-            [
-                lax.dynamic_index_in_dim(stacked, around(-c), 0, keepdims=False)
-                for c in range(n_tensor)
-            ],
-            axis=1,
-        )
-        combine_grad = contract_rows(ordered, (in_scale[:, None] * grad_mixed).astype(bf16))[None]
-    with jax.named_scope("unembed_grad"):
-        grad_stack = jnp.stack(grads)
-        grad_heads = []
-        for m in range(n_head):
-            piece_of = lax.dynamic_index_in_dim(
-                grad_stack, around(-(h ^ m)), 0, keepdims=False
-            )
-            grad_heads.append(flip(piece_of, "head", n_head, m) if m else piece_of)
-        unembed_grad = contract_rows(
-            jnp.concatenate(grad_heads, axis=0), jnp.concatenate(normed_heads, axis=0)
+        term_low = term.astype(bf16)
+        pair = flip(term_low, "head", n_head, 1)
+        heads_near = flip(grad_slices[1], "head", n_head, 1)
+        pair, heads_near = lax.optimization_barrier((pair, heads_near))
+        pair = term_low.astype(f32) + pair.astype(f32)
+        pair_low = pair.astype(bf16)
+        crossed = swap(jnp.where(first, pair_low[half:], term_low[:half]))
+        beside = lax.ppermute(
+            pair_low[:half], ("head", "dp"), [(2 * i, 2 * (i ^ 2)) for i in range(n_head)]
+        )
+        across = lax.ppermute(
+            pair_low[half:], ("head", "dp"), [(2 * i, 2 * (i ^ 2) + 1) for i in range(n_head)]
+        )
+        unembed_grad = head_sum([grad_slices[0], heads_near] + heads_far, normed_heads, 4)
+        crossed, beside, across, unembed_grad = lax.optimization_barrier(
+            (crossed, beside, across, unembed_grad)
         )
         unembed_grad = unembed_grad.reshape(1, 1, piece, width)
+        embed_grad = jnp.where(first, crossed.astype(f32), term[half:])[None]
+        trunk_grad = jnp.where(
+            first,
+            pair[:half] + beside.astype(f32),
+            crossed.astype(f32) + across.astype(f32),
+        )
     return (trunk_grad, embed_grad, combine_grad, unembed_grad)
 
 

time: 245 us -> 211 us (0.86)
  matrix products: 63.2 us -> 0 us
  Pallas kernels: 0 us -> 60.5 us
  waiting for transfers between devices: 94.9 us -> 72.4 us
  starting transfers between devices: 69.7 us -> 51.3 us
  other arithmetic: 11.6 us -> 17.9 us
  local copies, waits for them, and re-layouts: 1.64 us -> 6.75 us
    ppermute x26 -> x6, waiting for transfers between devices: 69.7 us -> 0.02 us  [the longest x1 0.01 us: fast_local(): ends = lax.ppermute(far, 'tensor', [(0, 1), (3, 2)])]
    dot_general x18 -> x0, matrix products: 63.2 us -> none  [the longest x8 25 us: plain_dot(): return jnp.dot(left, right, preferred_element_type=f32)]
    pallas_call x0 -> x17, Pallas kernels: none -> 60.5 us  [the longest x9 33.3 us: stream(): pl.pallas_call(kernel, out_shape=jax.ShapeDtypeStruct((rows, out_width),...]
    ppermute x8 -> x26, waiting for transfers between devices: 9.83 us -> 61.6 us  [flip(): return lax.ppermute(value, axis, [(i, i ^ mask) for i in range(size)])]
    ppermute x26 -> x6, starting transfers between devices: 52.2 us -> 13.1 us  [the longest x1 4.73 us: fast_local(): ends = lax.ppermute(far, 'tensor', [(0, 1), (3, 2)])]
    ppermute x8 -> x26, starting transfers between devices: 5.03 us -> 33 us  [flip(): return lax.ppermute(value, axis, [(i, i ^ mask) for i in range(size)])]
    ppermute x7 -> x5, starting transfers between devices: 12.5 us -> 5.29 us  [swap(): return lax.ppermute(value, 'dp', [(0, 1), (1, 0)])]
    unnamed x26 -> x78, local copies, waits for them, and re-layouts: 0.07 us -> 4.9 us
  transfers between devices with their start and end apart: 41 -> 37, of which waited for: 20 -> 11; matrix products, arithmetic and copies ran while one was open for 20% -> 4% of each run, Pallas kernels for 0% -> 24%
where the time goes in v2:
time: 211 us; the launch traced here: 210 us
  waiting for transfers between devices  72.4 us (34%)
  Pallas kernels  60.5 us (29%)
  starting transfers between devices  51.3 us (24%)
  other arithmetic  17.9 us (8%)
  local copies, waits for them, and re-layouts  6.75 us (3%)
    ppermute x26, waiting for transfers between devices, flip(): return lax.ppermute(value, axis, [(i, i ^ mask) for i in range(size)])  61.6 us
    pallas_call x9, Pallas kernels, stream(): pl.pallas_call(kernel, out_shape=jax.ShapeDtypeStruct((rows, out_width),...  33.3 us
    ppermute x26, starting transfers between devices, flip(): return lax.ppermute(value, axis, [(i, i ^ mask) for i in range(size)])  33 us
    pallas_call x1, Pallas kernels, combine_rows(): pl.pallas_call(combine_kernel, out_shape=jax.ShapeDtypeStruct((count * wi...  11 us
    ppermute x5, waiting for transfers between devices, swap(): return lax.ppermute(value, 'dp', [(0, 1), (1, 0)])  10.8 us
    pallas_call x1, Pallas kernels, head_sum(): pl.pallas_call(head_sum_kernel, out_shape=jax.ShapeDtypeStruct((size, wid...  5.78 us
    ppermute x5, starting transfers between devices, swap(): return lax.ppermute(value, 'dp', [(0, 1), (1, 0)])  5.29 us
    pallas_call x1, Pallas kernels, dot_columns_apart(): pl.pallas_call(dot_columns_apart_kernel, out_shape=[jax.ShapeDtypeStruct(...  4.91 us
  transfers between devices with their start and end apart: 37, of which 11 were waited for; matrix products, arithmetic and copies ran while one was open for 4% of the time, Pallas kernels for 24%

profile of v2, /device:TPU:0, one launch (start us, length us, event | category | flops | bytes accessed | tf_op | source)
XLA Modules:
  0.0 210.3 jit_solution(7668463575305168281)
XLA Ops:
  0.6 1.0 bitcast_select_fusion
  1.6 0.9 pad_maximum_fusion.3
  2.5 3.0 %collective-permute-start.3 = (bf16[96,1280]{1,0:T(8,128)(2,1)S(1)}, bf16[96,1280]{1,0:T(8,128)(2,1)S(1)}, u32[]{:S(2)}, u32[]{:S(2)}) collective-permute-start(bf16[96,1280]{1,0:T(8,128)(2,1)S(1)} %pad_maximum_fusion.3), channel_id=1, source_target_pairs={{0,1},{1,0},{2,3},{3,2},{4,5},{5,4},{6,7},{7,6},{8,9},{9,8},{10,11... | collective-permute-start | bytes 737288 | tf_op jit(solution)/shard_map/inputs/ppermute | solution.py:41
  5.6 1.6 collective-permute-start
  7.2 2.6 %collective-permute-start.1 = (bf16[48,1280]{1,0:T(8,128)(2,1)S(1)}, bf16[48,1280]{1,0:T(8,128)(2,1)S(1)}, u32[]{:S(2)}, u32[]{:S(2)}) collective-permute-start(bf16[48,1280]{1,0:T(8,128)(2,1)S(1)} %get-tuple-element.64), channel_id=1, source_target_pairs={{0,4},{2,6},{4,0},{6,2},{1,5},{3,7},{5,1},{7,3},{8,12},{10,14},{12... | collective-permute-start | bytes 368648 | tf_op jit(solution)/shard_map/inputs/ppermute | solution.py:37
  10.0 1.8 collective-permute-done
  11.8 7.4 %collective-permute-done.1 = bf16[48,1280]{1,0:T(8,128)(2,1)S(1)} collective-permute-done((bf16[48,1280]{1,0:T(8,128)(2,1)S(1)}, bf16[48,1280]{1,0:T(8,128)(2,1)S(1)}, u32[]{:S(2)}, u32[]{:S(2)}) %collective-permute-start.1) | collective-permute-done | bytes 122912 | tf_op jit(solution)/shard_map/inputs/ppermute | solution.py:37
  19.3 1.9 collective-permute-start.4
  21.2 1.2 collective-permute-start.5
  22.4 1.4 collective-permute-start.6
  23.7 0.7 fusion.44
  24.5 4.7 %copy-done = bf16[1,5120,1280]{2,1,0:T(8,128)(2,1)S(1)} copy-done((bf16[1,5120,1280]{2,1,0:T(8,128)(2,1)S(1)}, bf16[1,5120,1280]{2,1,0:T(8,128)(2,1)}, u32[]{:S(2)}) %copy-start) | copy-done | bytes 13107224
  29.2 1.0 inputs.1.base
  30.3 1.8 collective-permute-done.5
  33.0 0.7 fusion.42
  33.9 0.7 fusion.41
  34.8 1.0 projection.3.base
  35.8 1.0 projection.4.base
  36.9 1.0 projection.5
  38.6 5.7 %collective-permute-done.7 = bf16[96,1280]{1,0:T(8,128)(2,1)S(1)} collective-permute-done((bf16[96,1280]{1,0:T(8,128)(2,1)S(1)}, bf16[96,1280]{1,0:T(8,128)(2,1)S(1)}, u32[]{:S(2)}, u32[]{:S(2)}) %collective-permute-start.7) | collective-permute-done | bytes 245792 | tf_op jit(solution)/shard_map/projection/ppermute | solution.py:41
  44.6 3.6 %logits.5 = f32[96,2048]{1,0:T(8,128)S(1)} custom-call(s32[1]{0:T(128)} %bitcast.3.which, bf16[96,1280]{1,0:T(8,128)(2,1)S(1)} %multiply_convert_fusion.2.left, bf16[8192,1280]{1,0:T(8,128)(2,1)} %weight.17), custom_call_target="tpu_custom_call" | custom-call | tf_op jit(solution)/shard_map/logits/pallas_call | solution.py:81
  48.3 4.7 %collective-permute-start.8 = (f32[96,2048]{1,0:T(8,128)S(1)}, f32[96,2048]{1,0:T(8,128)}, u32[]{:S(2)}, u32[]{:S(2)}) collective-permute-start(f32[96,2048]{1,0:T(8,128)S(1)} %logits.5), channel_id=1, source_target_pairs={{0,2},{6,4},{1,3},{7,5},{8,10},{14,12},{9,11},{15,13},{16,18},{22,... | collective-permute-start | bytes 2359304 | tf_op jit(solution)/shard_map/logits/ppermute | solution.py:315
  53.0 1.6 collective-permute-start.9
  54.6 1.5 collective-permute-start.10
  56.1 2.4 %collective-permute-start.11 = (f32[96]{0:T(128)S(1)}, f32[96]{0:T(128)S(1)}, u32[]{:S(2)}, u32[]{:S(2)}) collective-permute-start(f32[96]{0:T(128)S(1)} %get-tuple-element.73), channel_id=1, source_target_pairs={{0,4},{2,6},{4,0},{6,2},{1,5},{3,7},{5,1},{7,3},{8,12},{10,14},{12... | collective-permute-start | bytes 1160 | tf_op jit(solution)/shard_map/logits/ppermute | solution.py:37
  59.0 3.5 %logits.6 = f32[96,2048]{1,0:T(8,128)S(1)} custom-call(s32[1]{0:T(128)} %bitcast.4.which, bf16[96,1280]{1,0:T(8,128)(2,1)S(1)} %multiply_convert_fusion.2.left, bf16[8192,1280]{1,0:T(8,128)(2,1)} %weight.17), custom_call_target="tpu_custom_call" | custom-call | tf_op jit(solution)/shard_map/logits/pallas_call | solution.py:81
  62.5 3.5 %logits.7 = f32[96,2048]{1,0:T(8,128)S(1)} custom-call(s32[1]{0:T(128)} %bitcast.5.which, bf16[96,1280]{1,0:T(8,128)(2,1)S(1)} %multiply_convert_fusion.2.left, bf16[8192,1280]{1,0:T(8,128)(2,1)} %weight.17), custom_call_target="tpu_custom_call" | custom-call | tf_op jit(solution)/shard_map/logits/pallas_call | solution.py:81
  65.9 3.5 %logits.8 = f32[96,2048]{1,0:T(8,128)S(1)} custom-call(s32[1]{0:T(128)} %bitcast.1.which, bf16[96,1280]{1,0:T(8,128)(2,1)S(1)} %multiply_convert_fusion.2.left, bf16[8192,1280]{1,0:T(8,128)(2,1)} %weight.17), custom_call_target="tpu_custom_call" | custom-call | tf_op jit(solution)/shard_map/logits/pallas_call | solution.py:81
  69.4 1.8 collective-permute-done.11
  71.5 1.6 collective-permute-start.16
  73.3 1.2 add.339
  74.6 1.9 collective-permute-start.13
  76.5 1.3 collective-permute-start.14
  78.2 7.5 %logits.9 = f32[96,1280]{1,0:T(8,128)S(1)} custom-call(s32[1]{0:T(128)} %constant.49.clone.1.which, bf16[96,8192]{1,0:T(8,128)(2,1)S(1)} %fusion.left, bf16[8192,1280]{1,0:T(8,128)(2,1)} %weight.17), custom_call_target="tpu_custom_call" | custom-call | tf_op jit(solution)/shard_map/logits/pallas_call | solution.py:81
  85.8 26.5 %collective-permute-done.13 = f32[96,2048]{1,0:T(8,128)S(1)} collective-permute-done((f32[96,2048]{1,0:T(8,128)S(1)}, f32[96,2048]{1,0:T(8,128)S(1)}, u32[]{:S(2)}, u32[]{:S(2)}) %collective-permute-start.13) | collective-permute-done | bytes 786464 | tf_op jit(solution)/shard_map/logits/ppermute | solution.py:37
  112.6 1.5 fusion.48
  115.0 2.5 %collective-permute-start.19 = (bf16[96,2048]{1,0:T(8,128)(2,1)S(1)}, bf16[96,2048]{1,0:T(8,128)(2,1)S(1)}, u32[]{:S(2)}, u32[]{:S(2)}) collective-permute-start(bf16[96,2048]{1,0:T(8,128)(2,1)S(1)} %get-tuple-element.142.left), channel_id=1, source_target_pairs={{0,2},{2,0},{4,6},{6,4},{1,3},{3,1},{5,7},{7,5},{8,10},{10,8},{12,... | collective-permute-start | bytes 1179656 | tf_op jit(solution)/shard_map/grad_normed/ppermute | solution.py:37
  119.3 2.9 %grad_normed.4 = f32[96,1280]{1,0:T(8,128)S(1)} custom-call(s32[1]{0:T(128)} %bitcast.1.which, bf16[96,2048]{1,0:T(8,128)(2,1)S(1)} %get-tuple-element.142.left, bf16[8192,1280]{1,0:T(8,128)(2,1)} %weight.17), custom_call_target="tpu_custom_call" | custom-call | tf_op jit(solution)/shard_map/grad_normed/pallas_call | solution.py:81
  122.2 1.4 collective-permute-start.22
  123.6 11.1 %collective-permute-done.18.left = bf16[96,2048]{1,0:T(8,128)(2,1)S(1)} collective-permute-done((bf16[96,2048]{1,0:T(8,128)(2,1)S(1)}, bf16[96,2048]{1,0:T(8,128)(2,1)S(1)}, u32[]{:S(2)}, u32[]{:S(2)}) %collective-permute-start.18) | collective-permute-done | bytes 393248 | tf_op jit(solution)/shard_map/grad_normed/ppermute | solution.py:37
  134.7 1.5 collective-permute-start.21
  136.9 3.3 %collective-permute-start.23 = (f32[5,96]{1,0:T(8,128)S(1)}, f32[5,96]{1,0:T(8,128)S(1)}, u32[]{:S(2)}, u32[]{:S(2)}) collective-permute-start(f32[5,96]{1,0:T(8,128)S(1)} %stack.75), channel_id=1, source_target_pairs={{0,2},{2,0},{4,6},{6,4},{1,3},{3,1},{5,7},{7,5},{8,10},{10,8},{12,... | collective-permute-start | bytes 5768 | tf_op jit(solution)/shard_map/grad_normed/ppermute | solution.py:37
  140.3 2.2 %collective-permute-start.25 = (f32[5,96]{1,0:T(8,128)S(1)}, f32[5,96]{1,0:T(8,128)S(1)}, u32[]{:S(2)}, u32[]{:S(2)}) collective-permute-start(f32[5,96]{1,0:T(8,128)S(1)} %stack.75), channel_id=1, source_target_pairs={{0,6},{2,4},{4,2},{6,0},{1,7},{3,5},{5,3},{7,1},{8,14},{10,12},{12... | collective-permute-start | bytes 5768 | tf_op jit(solution)/shard_map/grad_normed/ppermute | solution.py:37
  142.6 2.9 %grad_normed.6 = f32[96,1280]{1,0:T(8,128)S(1)} custom-call(s32[1]{0:T(128)} %bitcast.4.which, bf16[96,2048]{1,0:T(8,128)(2,1)S(1)} %collective-permute-done.18.left, bf16[8192,1280]{1,0:T(8,128)(2,1)} %weight.17), custom_call_target="tpu_custom_call" | custom-call | tf_op jit(solution)/shard_map/grad_normed/pallas_call | solution.py:81
  145.6 2.9 %grad_normed.5 = f32[96,1280]{1,0:T(8,128)S(1)} custom-call(s32[1]{0:T(128)} %bitcast.5.which, bf16[96,2048]{1,0:T(8,128)(2,1)S(1)} %collective-permute-done.19.left, bf16[8192,1280]{1,0:T(8,128)(2,1)} %weight.17), custom_call_target="tpu_custom_call" | custom-call | tf_op jit(solution)/shard_map/grad_normed/pallas_call | solution.py:81
  148.7 1.8 fusion.13
  150.6 3.1 %grad_normed.7 = f32[96,1280]{1,0:T(8,128)S(1)} custom-call(s32[1]{0:T(128)} %bitcast.3.which, bf16[96,2048]{1,0:T(8,128)(2,1)S(1)} %get-tuple-element.185.left, bf16[8192,1280]{1,0:T(8,128)(2,1)} %weight.17), custom_call_target="tpu_custom_call" | custom-call | tf_op jit(solution)/shard_map/grad_normed/pallas_call | solution.py:81
  154.7 1.1 dynamic-slice_bitcast_fusion
  155.8 5.0 %collective-permute-done.26 = bf16[96,1280]{1,0:T(8,128)(2,1)S(1)} collective-permute-done((bf16[96,1280]{1,0:T(8,128)(2,1)S(1)}, bf16[96,1280]{1,0:T(8,128)(2,1)S(1)}, u32[]{:S(2)}, u32[]{:S(2)}) %collective-permute-start.26) | collective-permute-done | bytes 245792 | tf_op jit(solution)/shard_map/grad_normed/ppermute | solution.py:41
  161.3 1.6 collective-permute-start.30
  163.1 4.9 %joined_grad.3 = (bf16[96,1408]{1,0:T(8,128)(2,1)}, bf16[96,1408]{1,0:T(8,128)(2,1)}, bf16[96,1408]{1,0:T(8,128)(2,1)}) custom-call(s32[3]{0:T(128)S(1)} %pad_add_fusion.which, bf16[96,1280]{1,0:T(8,128)(2,1)S(1)} %get-tuple-element.132.left, bf16[5120,1280]{1,0:T(8,128)(2,1)S(1)} %bitcast.201, bf16[96,128]{1,0:T(8,128)(2,1)S(1)} %select_convert_fusion.3.extra), custom_call_target="tpu_custom_call" | custom-call | tf_op jit(solution)/shard_map/joined_grad/pallas_call | solution.py:146
  168.0 1.4 collective-permute-start.27
  169.4 0.8 collective-permute-start.28
  170.2 2.2 %collective-permute-start.29 = (bf16[96,1408]{1,0:T(8,128)(2,1)}, bf16[96,1408]{1,0:T(8,128)(2,1)}, u32[]{:S(2)}, u32[]{:S(2)}) collective-permute-start(bf16[96,1408]{1,0:T(8,128)(2,1)} %get-tuple-element.102), channel_id=1, source_target_pairs={{0,2},{2,0},{4,6},{6,4},{1,3},{3,1},{5,7},{7,5},{8,10},{10,8},{12,... | collective-permute-start | bytes 811016 | tf_op jit(solution)/shard_map/joined_grad/ppermute | solution.py:37
  172.6 1.3 joined_grad.4
  174.6 11.0 %joined_grad.5 = f32[5120,1280]{1,0:T(8,128)} custom-call(s32[4]{0:T(128)S(1)} %iota_xor_fusion.which, bf16[4,96,1280]{2,1,0:T(8,128)(2,1)S(1)} %pad_maximum_fusion.1.part, bf16[96,1280]{1,0:T(8,128)(2,1)S(1)} %get-tuple-element.129.grad), custom_call_target="tpu_custom_call" | custom-call | tf_op jit(solution)/shard_map/joined_grad/pallas_call | solution.py:218
  185.7 9.3 %collective-permute-done.28 = bf16[96,1408]{1,0:T(8,128)(2,1)} collective-permute-done((bf16[96,1408]{1,0:T(8,128)(2,1)}, bf16[96,1408]{1,0:T(8,128)(2,1)}, u32[]{:S(2)}, u32[]{:S(2)}) %collective-permute-start.28) | collective-permute-done | bytes 270368 | tf_op jit(solution)/shard_map/joined_grad/ppermute | solution.py:37
  195.0 1.1 multiply_reduce_fusion.5
  196.0 1.5 fusion.45
  197.6 1.5 collective-permute-done.32
  199.8 2.2 %collective-permute-start.35 = (bf16[48,1280]{1,0:T(8,128)(2,1)S(1)}, bf16[48,1280]{1,0:T(8,128)(2,1)S(1)}, u32[]{:S(2)}, u32[]{:S(2)}) collective-permute-start(bf16[48,1280]{1,0:T(8,128)(2,1)S(1)} %get-tuple-element.157), channel_id=1, source_target_pairs={{0,16},{8,24},{16,0},{24,8},{2,18},{10,26},{18,2},{26,10},{4,20},{... | collective-permute-start | bytes 368648 | tf_op jit(solution)/shard_map/input_grads/ppermute | solution.py:444
  202.0 1.6 collective-permute-start.36
  203.7 5.8 %input_grads.1 = f32[2048,1280]{1,0:T(8,128)} custom-call(bf16[96,2048]{1,0:T(8,128)(2,1)S(1)} %get-tuple-element.111.refs_0_, bf16[96,2048]{1,0:T(8,128)(2,1)S(1)} %collective-permute-done.33.refs_1_, bf16[96,2048]{1,0:T(8,128)(2,1)S(1)} %collective-permute-done.30.refs_2_, bf16[96,2048]{1,0:T(8,128)(2,1)S(1)} %collective-permute-done.31.refs_3_, ...), custom_call_target="tpu_custom_call" | custom-call | tf_op jit(solution)/shard_map/input_grads/pallas_call | solution.py:247
  209.5 0.9 fusion.16
  (157 shorter events, 11.2 us)
Async XLA Ops:
  2.5 16.6 %collective-permute-start.3 = (bf16[96,1280]{1,0:T(8,128)(2,1)S(1)}, bf16[96,1280]{1,0:T(8,128)(2,1)S(1)}, u32[]{:S(2)}, u32[]{:S(2)}) collective-permute-start(bf16[96,1280]{1,0:T(8,128)(2,1)S(1)} %pad_maximum_fusion.3), channel_id=1, source_target_pairs={{0,1},{1,0},{2,3},{3,2},{4,5},{5,4},{6,7},{7,6},{8,9},{9,8},{10,11... | collective-permute-start | bytes 737288 | tf_op jit(solution)/shard_map/inputs/ppermute | solution.py:41
  5.6 6.2 %collective-permute-start = (bf16[48,1280]{1,0:T(8,128)(2,1)S(1)}, bf16[48,1280]{1,0:T(8,128)(2,1)S(1)}, u32[]{:S(2)}, u32[]{:S(2)}) collective-permute-start(bf16[48,1280]{1,0:T(8,128)(2,1)S(1)} %get-tuple-element.64), channel_id=1, source_target_pairs={{0,2},{2,0},{4,6},{6,4},{1,3},{3,1},{5,7},{7,5},{8,10},{10,8},{12,... | collective-permute-start | bytes 368648 | tf_op jit(solution)/shard_map/inputs/ppermute | solution.py:37
  7.2 12.0 %collective-permute-start.1 = (bf16[48,1280]{1,0:T(8,128)(2,1)S(1)}, bf16[48,1280]{1,0:T(8,128)(2,1)S(1)}, u32[]{:S(2)}, u32[]{:S(2)}) collective-permute-start(bf16[48,1280]{1,0:T(8,128)(2,1)S(1)} %get-tuple-element.64), channel_id=1, source_target_pairs={{0,4},{2,6},{4,0},{6,2},{1,5},{3,7},{5,1},{7,3},{8,12},{10,14},{12... | collective-permute-start | bytes 368648 | tf_op jit(solution)/shard_map/inputs/ppermute | solution.py:37
  9.7 9.4 %collective-permute-start.2 = (bf16[48,1280]{1,0:T(8,128)(2,1)S(1)}, bf16[48,1280]{1,0:T(8,128)(2,1)S(1)}, u32[]{:S(2)}, u32[]{:S(2)}) collective-permute-start(bf16[48,1280]{1,0:T(8,128)(2,1)S(1)} %get-tuple-element.64), channel_id=1, source_target_pairs={{0,6},{2,4},{4,2},{6,0},{1,7},{3,5},{5,3},{7,1},{8,14},{10,12},{12... | collective-permute-start | bytes 368648 | tf_op jit(solution)/shard_map/inputs/ppermute | solution.py:37
  19.2 25.1 %copy-start.10 = (bf16[48,1280]{1,0:T(8,128)(2,1)}, bf16[48,1280]{1,0:T(8,128)(2,1)S(1)}, u32[]{:S(2)}) copy-start(bf16[48,1280]{1,0:T(8,128)(2,1)S(1)} %get-tuple-element.153) | copy-start | bytes 368644
  19.2 25.1 %copy-start.12 = (bf16[48,1280]{1,0:T(8,128)(2,1)}, bf16[48,1280]{1,0:T(8,128)(2,1)S(1)}, u32[]{:S(2)}) copy-start(bf16[48,1280]{1,0:T(8,128)(2,1)S(1)} %get-tuple-element.154) | copy-start | bytes 368644
  19.3 11.1 %collective-permute-start.4 = (bf16[48,1280]{1,0:T(8,128)(2,1)S(1)}, bf16[48,1280]{1,0:T(8,128)(2,1)S(1)}, u32[]{:S(2)}, u32[]{:S(2)}) collective-permute-start(bf16[48,1280]{1,0:T(8,128)(2,1)S(1)} %get-tuple-element.173), channel_id=1, source_target_pairs={{0,2},{2,0},{4,6},{6,4},{1,3},{3,1},{5,7},{7,5},{8,10},{10,8},{12,... | collective-permute-start | bytes 368648 | tf_op jit(solution)/shard_map/inputs/ppermute | solution.py:37
  21.2 10.9 %collective-permute-start.5 = (bf16[48,1280]{1,0:T(8,128)(2,1)S(1)}, bf16[48,1280]{1,0:T(8,128)(2,1)S(1)}, u32[]{:S(2)}, u32[]{:S(2)}) collective-permute-start(bf16[48,1280]{1,0:T(8,128)(2,1)S(1)} %get-tuple-element.173), channel_id=1, source_target_pairs={{0,4},{2,6},{4,0},{6,2},{1,5},{3,7},{5,1},{7,3},{8,12},{10,14},{12... | collective-permute-start | bytes 368648 | tf_op jit(solution)/shard_map/inputs/ppermute | solution.py:37
  22.4 9.7 %collective-permute-start.6 = (bf16[48,1280]{1,0:T(8,128)(2,1)S(1)}, bf16[48,1280]{1,0:T(8,128)(2,1)S(1)}, u32[]{:S(2)}, u32[]{:S(2)}) collective-permute-start(bf16[48,1280]{1,0:T(8,128)(2,1)S(1)} %get-tuple-element.173), channel_id=1, source_target_pairs={{0,6},{2,4},{4,2},{6,0},{1,7},{3,5},{5,3},{7,1},{8,14},{10,12},{12... | collective-permute-start | bytes 368648 | tf_op jit(solution)/shard_map/inputs/ppermute | solution.py:37
  36.9 7.5 %copy-start.14 = (bf16[48,1280]{1,0:T(8,128)(2,1)S(1)}, bf16[48,1280]{1,0:T(8,128)(2,1)}, u32[]{:S(2)}) copy-start(bf16[48,1280]{1,0:T(8,128)(2,1)} %param.7) | copy-start | bytes 368644
  37.9 6.7 %copy-start.21 = (f32[1280]{0:T(1024)S(1)}, f32[1280]{0:T(1024)}, u32[]{:S(2)}) copy-start(f32[1280]{0:T(1024)} %param.10) | copy-start | bytes 15364
  38.0 6.3 %collective-permute-start.7 = (bf16[96,1280]{1,0:T(8,128)(2,1)S(1)}, bf16[96,1280]{1,0:T(8,128)(2,1)S(1)}, u32[]{:S(2)}, u32[]{:S(2)}) collective-permute-start(bf16[96,1280]{1,0:T(8,128)(2,1)S(1)} %multiply_convert_fusion.3), channel_id=1, source_target_pairs={{0,1},{1,0},{2,3},{3,2},{4,5},{5,4},{6,7},{7,6},{8,9},{9,8},{10,11... | collective-permute-start | bytes 737288 | tf_op jit(solution)/shard_map/projection/ppermute | solution.py:41
  44.6 26.7 %copy-start.6 = (f32[96,1280]{1,0:T(8,128)}, f32[96,1280]{1,0:T(8,128)S(1)}, u32[]{:S(2)}) copy-start(f32[96,1280]{1,0:T(8,128)S(1)} %get-tuple-element.146) | copy-start | bytes 1474564
  44.6 9.9 %copy-start.34 = (s32[1,96]{1,0:T(1,128)S(1)}, s32[1,96]{1,0:T(1,128)}, u32[]{:S(2)}) copy-start(s32[1,96]{1,0:T(1,128)} %param.12) | copy-start | bytes 1156
  48.3 23.0 %collective-permute-start.8 = (f32[96,2048]{1,0:T(8,128)S(1)}, f32[96,2048]{1,0:T(8,128)}, u32[]{:S(2)}, u32[]{:S(2)}) collective-permute-start(f32[96,2048]{1,0:T(8,128)S(1)} %logits.5), channel_id=1, source_target_pairs={{0,2},{6,4},{1,3},{7,5},{8,10},{14,12},{9,11},{15,13},{16,18},{22,... | collective-permute-start | bytes 2359304 | tf_op jit(solution)/shard_map/logits/ppermute | solution.py:315
  53.0 18.3 %collective-permute-start.9 = (f32[96,2048]{1,0:T(8,128)S(1)}, f32[96,2048]{1,0:T(8,128)}, u32[]{:S(2)}, u32[]{:S(2)}) collective-permute-start(f32[96,2048]{1,0:T(8,128)S(1)} %logits.5), channel_id=1, source_target_pairs={{2,4},{4,2},{3,5},{5,3},{10,12},{12,10},{11,13},{13,11},{18,20},{2... | collective-permute-start | bytes 2359304 | tf_op jit(solution)/shard_map/logits/ppermute | solution.py:316
  54.6 59.6 %copy-start.29 = (s32[96]{0:T(128)}, s32[96]{0:T(128)S(1)}, u32[]{:S(2)}) copy-start(s32[96]{0:T(128)S(1)} %subtract_bitcast_fusion) | copy-start | bytes 1156
  54.6 14.8 %collective-permute-start.10 = (f32[96]{0:T(128)S(1)}, f32[96]{0:T(128)S(1)}, u32[]{:S(2)}, u32[]{:S(2)}) collective-permute-start(f32[96]{0:T(128)S(1)} %get-tuple-element.73), channel_id=1, source_target_pairs={{0,2},{2,0},{4,6},{6,4},{1,3},{3,1},{5,7},{7,5},{8,10},{10,8},{12,... | collective-permute-start | bytes 1160 | tf_op jit(solution)/shard_map/logits/ppermute | solution.py:37
  56.1 15.2 %collective-permute-start.11 = (f32[96]{0:T(128)S(1)}, f32[96]{0:T(128)S(1)}, u32[]{:S(2)}, u32[]{:S(2)}) collective-permute-start(f32[96]{0:T(128)S(1)} %get-tuple-element.73), channel_id=1, source_target_pairs={{0,4},{2,6},{4,0},{6,2},{1,5},{3,7},{5,1},{7,3},{8,12},{10,14},{12... | collective-permute-start | bytes 1160 | tf_op jit(solution)/shard_map/logits/ppermute | solution.py:37
  58.5 12.8 %collective-permute-start.12 = (f32[96]{0:T(128)S(1)}, f32[96]{0:T(128)S(1)}, u32[]{:S(2)}, u32[]{:S(2)}) collective-permute-start(f32[96]{0:T(128)S(1)} %get-tuple-element.73), channel_id=1, source_target_pairs={{0,6},{2,4},{4,2},{6,0},{1,7},{3,5},{5,3},{7,1},{8,14},{10,12},{12... | collective-permute-start | bytes 1160 | tf_op jit(solution)/shard_map/logits/ppermute | solution.py:37
  59.0 55.2 %copy-start.22 = (s32[2048]{0:T(1024)}, s32[2048]{0:T(1024)S(1)}, u32[]{:S(2)}) copy-start(s32[2048]{0:T(1024)S(1)} %iota_add_fusion.3) | copy-start | bytes 24580
  71.3 41.4 %copy-start.27 = (f32[96]{0:T(128)}, f32[96]{0:T(128)S(1)}, u32[]{:S(2)}) copy-start(f32[96]{0:T(128)S(1)} %add_rsqrt_fusion) | copy-start | bytes 1156
  71.4 14.3 %collective-permute-start.15 = (bf16[96,1280]{1,0:T(8,128)(2,1)S(1)}, bf16[96,1280]{1,0:T(8,128)(2,1)S(1)}, u32[]{:S(2)}, u32[]{:S(2)}) collective-permute-start(bf16[96,1280]{1,0:T(8,128)(2,1)S(1)} %multiply_convert_fusion.1.refs_4_), channel_id=1, source_target_pairs={{0,8},{8,0},{16,24},{24,16},{1,9},{9,1},{17,25},{25,17},{2,10},{10... | collective-permute-start | bytes 737288 | tf_op jit(solution)/shard_map/logits/ppermute | solution.py:37
  71.5 14.3 %collective-permute-start.16 = (bf16[96,1280]{1,0:T(8,128)(2,1)S(1)}, bf16[96,1280]{1,0:T(8,128)(2,1)S(1)}, u32[]{:S(2)}, u32[]{:S(2)}) collective-permute-start(bf16[96,1280]{1,0:T(8,128)(2,1)S(1)} %multiply_convert_fusion.1.refs_4_), channel_id=1, source_target_pairs={{0,16},{8,24},{16,0},{24,8},{1,17},{9,25},{17,1},{25,9},{2,18},{10... | collective-permute-start | bytes 737288 | tf_op jit(solution)/shard_map/logits/ppermute | solution.py:37
  73.1 12.7 %collective-permute-start.17 = (bf16[96,1280]{1,0:T(8,128)(2,1)S(1)}, bf16[96,1280]{1,0:T(8,128)(2,1)S(1)}, u32[]{:S(2)}, u32[]{:S(2)}) collective-permute-start(bf16[96,1280]{1,0:T(8,128)(2,1)S(1)} %multiply_convert_fusion.1.refs_4_), channel_id=1, source_target_pairs={{0,24},{8,16},{16,8},{24,0},{1,25},{9,17},{17,9},{25,1},{2,26},{10... | collective-permute-start | bytes 737288 | tf_op jit(solution)/shard_map/logits/ppermute | solution.py:37
  74.6 37.7 %collective-permute-start.13 = (f32[96,2048]{1,0:T(8,128)S(1)}, f32[96,2048]{1,0:T(8,128)S(1)}, u32[]{:S(2)}, u32[]{:S(2)}) collective-permute-start(f32[96,2048]{1,0:T(8,128)S(1)} %add.339), channel_id=1, source_target_pairs={{0,4},{2,6},{4,0},{6,2},{1,5},{3,7},{5,1},{7,3},{8,12},{10,14},{12... | collective-permute-start | bytes 2359304 | tf_op jit(solution)/shard_map/logits/ppermute | solution.py:37
  76.5 36.1 %collective-permute-start.14 = (f32[96,2048]{1,0:T(8,128)S(1)}, f32[96,2048]{1,0:T(8,128)S(1)}, u32[]{:S(2)}, u32[]{:S(2)}) collective-permute-start(f32[96,2048]{1,0:T(8,128)S(1)} %logits.7), channel_id=1, source_target_pairs={{0,2},{2,0},{4,6},{6,4},{1,3},{3,1},{5,7},{7,5},{8,10},{10,8},{12,... | collective-permute-start | bytes 2359304 | tf_op jit(solution)/shard_map/logits/ppermute | solution.py:37
  85.8 28.4 %copy-start.2 = (bf16[96,1280]{1,0:T(8,128)(2,1)}, bf16[96,1280]{1,0:T(8,128)(2,1)S(1)}, u32[]{:S(2)}) copy-start(bf16[96,1280]{1,0:T(8,128)(2,1)S(1)} %collective-permute-done.16.refs_6_) | copy-start | bytes 737284
  85.8 28.4 %copy-start.4 = (bf16[96,1280]{1,0:T(8,128)(2,1)}, bf16[96,1280]{1,0:T(8,128)(2,1)S(1)}, u32[]{:S(2)}) copy-start(bf16[96,1280]{1,0:T(8,128)(2,1)S(1)} %collective-permute-done.17.refs_7_) | copy-start | bytes 737284
  114.7 20.1 %collective-permute-start.18 = (bf16[96,2048]{1,0:T(8,128)(2,1)S(1)}, bf16[96,2048]{1,0:T(8,128)(2,1)S(1)}, u32[]{:S(2)}, u32[]{:S(2)}) collective-permute-start(bf16[96,2048]{1,0:T(8,128)(2,1)S(1)} %get-tuple-element.142.left), channel_id=1, source_target_pairs={{0,4},{2,6},{4,0},{6,2},{1,5},{3,7},{5,1},{7,3},{8,12},{10,14},{12... | collective-permute-start | bytes 1179656 | tf_op jit(solution)/shard_map/grad_normed/ppermute | solution.py:37
  115.0 19.7 %collective-permute-start.19 = (bf16[96,2048]{1,0:T(8,128)(2,1)S(1)}, bf16[96,2048]{1,0:T(8,128)(2,1)S(1)}, u32[]{:S(2)}, u32[]{:S(2)}) collective-permute-start(bf16[96,2048]{1,0:T(8,128)(2,1)S(1)} %get-tuple-element.142.left), channel_id=1, source_target_pairs={{0,2},{2,0},{4,6},{6,4},{1,3},{3,1},{5,7},{7,5},{8,10},{10,8},{12,... | collective-permute-start | bytes 1179656 | tf_op jit(solution)/shard_map/grad_normed/ppermute | solution.py:37
  118.1 5.5 %collective-permute-start.20 = (f32[4,96]{1,0:T(4,128)S(1)}, f32[4,96]{1,0:T(4,128)S(1)}, u32[]{:S(2)}, u32[]{:S(2)}) collective-permute-start(f32[4,96]{1,0:T(4,128)S(1)} %pad_maximum_fusion.8), channel_id=1, source_target_pairs={{0,1},{1,0},{2,3},{3,2},{4,5},{5,4},{6,7},{7,6},{8,9},{9,8},{10,11... | collective-permute-start | bytes 4616 | tf_op jit(solution)/shard_map/grad_normed/ppermute | solution.py:41
  122.2 26.4 %collective-permute-start.22 = (bf16[96,2048]{1,0:T(8,128)(2,1)S(1)}, bf16[96,2048]{1,0:T(8,128)(2,1)}, u32[]{:S(2)}, u32[]{:S(2)}) collective-permute-start(bf16[96,2048]{1,0:T(8,128)(2,1)S(1)} %get-tuple-element.142.left), channel_id=1, source_target_pairs={{2,4},{4,2},{3,5},{5,3},{10,12},{12,10},{11,13},{13,11},{18,20},{2... | collective-permute-start | bytes 1179656 | tf_op jit(solution)/shard_map/grad_normed/ppermute | solution.py:356
  134.7 13.9 %collective-permute-start.21 = (bf16[96,2048]{1,0:T(8,128)(2,1)S(1)}, bf16[96,2048]{1,0:T(8,128)(2,1)}, u32[]{:S(2)}, u32[]{:S(2)}) collective-permute-start(bf16[96,2048]{1,0:T(8,128)(2,1)S(1)} %collective-permute-done.18.left), channel_id=1, source_target_pairs={{4,6},{2,0},{5,7},{3,1},{12,14},{10,8},{13,15},{11,9},{20,22},{18,... | collective-permute-start | bytes 1179656 | tf_op jit(solution)/shard_map/grad_normed/ppermute | solution.py:355
  136.9 11.7 %collective-permute-start.23 = (f32[5,96]{1,0:T(8,128)S(1)}, f32[5,96]{1,0:T(8,128)S(1)}, u32[]{:S(2)}, u32[]{:S(2)}) collective-permute-start(f32[5,96]{1,0:T(8,128)S(1)} %stack.75), channel_id=1, source_target_pairs={{0,2},{2,0},{4,6},{6,4},{1,3},{3,1},{5,7},{7,5},{8,10},{10,8},{12,... | collective-permute-start | bytes 5768 | tf_op jit(solution)/shard_map/grad_normed/ppermute | solution.py:37
  140.1 8.5 %collective-permute-start.24 = (f32[5,96]{1,0:T(8,128)S(1)}, f32[5,96]{1,0:T(8,128)S(1)}, u32[]{:S(2)}, u32[]{:S(2)}) collective-permute-start(f32[5,96]{1,0:T(8,128)S(1)} %stack.75), channel_id=1, source_target_pairs={{0,4},{2,6},{4,0},{6,2},{1,5},{3,7},{5,1},{7,3},{8,12},{10,14},{12... | collective-permute-start | bytes 5768 | tf_op jit(solution)/shard_map/grad_normed/ppermute | solution.py:37
  140.3 8.2 %collective-permute-start.25 = (f32[5,96]{1,0:T(8,128)S(1)}, f32[5,96]{1,0:T(8,128)S(1)}, u32[]{:S(2)}, u32[]{:S(2)}) collective-permute-start(f32[5,96]{1,0:T(8,128)S(1)} %stack.75), channel_id=1, source_target_pairs={{0,6},{2,4},{4,2},{6,0},{1,7},{3,5},{5,3},{7,1},{8,14},{10,12},{12... | collective-permute-start | bytes 5768 | tf_op jit(solution)/shard_map/grad_normed/ppermute | solution.py:37
  150.5 12.5 %slice-start = ((s8[13107200]{0:T(1024)(128)(4,1)}), s8[524288]{0:T(1024)(128)(4,1)S(1)}, s32[]{:S(2)}) async-start(s8[13107200]{0:T(1024)(128)(4,1)} %bitcast.199), calls=%async_computation | async-start | bytes 1048576
  150.5 12.5 %slice-start.1 = ((s8[13107200]{0:T(1024)(128)(4,1)}), s8[4194304]{0:T(1024)(128)(4,1)S(1)}, s32[]{:S(2)}) async-start(s8[13107200]{0:T(1024)(128)(4,1)} %bitcast.199), calls=%async_computation.1 | async-start | bytes 8388608
  150.5 12.5 %slice-start.2 = ((s8[13107200]{0:T(1024)(128)(4,1)}), s8[4194304]{0:T(1024)(128)(4,1)S(1)}, s32[]{:S(2)}) async-start(s8[13107200]{0:T(1024)(128)(4,1)} %bitcast.199), calls=%async_computation.2 | async-start | bytes 8388608
  153.9 6.9 %collective-permute-start.26 = (bf16[96,1280]{1,0:T(8,128)(2,1)S(1)}, bf16[96,1280]{1,0:T(8,128)(2,1)S(1)}, u32[]{:S(2)}, u32[]{:S(2)}) collective-permute-start(bf16[96,1280]{1,0:T(8,128)(2,1)S(1)} %get-tuple-element.138), channel_id=1, source_target_pairs={{0,1},{1,0},{2,3},{3,2},{4,5},{5,4},{6,7},{7,6},{8,9},{9,8},{10,11... | collective-permute-start | bytes 737288 | tf_op jit(solution)/shard_map/grad_normed/ppermute | solution.py:41
  154.5 8.6 %slice-start.3 = ((s8[13107200]{0:T(1024)(128)(4,1)}), s8[4194304]{0:T(1024)(128)(4,1)S(1)}, s32[]{:S(2)}) async-start(s8[13107200]{0:T(1024)(128)(4,1)} %bitcast.199), calls=%async_computation.3 | async-start | bytes 8388608
  154.7 6.2 %copy-start.7 = (f32[96,1280]{1,0:T(8,128)S(1)}, f32[96,1280]{1,0:T(8,128)}, u32[]{:S(2)}) copy-start(f32[96,1280]{1,0:T(8,128)} %copy-done.6) | copy-start | bytes 1474564
  154.7 6.2 %copy-start.28 = (f32[96]{0:T(128)S(1)}, f32[96]{0:T(128)}, u32[]{:S(2)}) copy-start(f32[96]{0:T(128)} %copy-done.27) | copy-start | bytes 1156
  161.1 6.9 %copy-start.8 = (f32[96,1280]{1,0:T(8,128)}, f32[96,1280]{1,0:T(8,128)S(1)}, u32[]{:S(2)}) copy-start(f32[96,1280]{1,0:T(8,128)S(1)} %get-tuple-element.130) | copy-start | bytes 1474564
  161.3 33.6 %collective-permute-start.30 = (bf16[96,2048]{1,0:T(8,128)(2,1)}, bf16[96,2048]{1,0:T(8,128)(2,1)S(1)}, u32[]{:S(2)}, u32[]{:S(2)}) collective-permute-start(bf16[96,2048]{1,0:T(8,128)(2,1)} %get-tuple-element.103), channel_id=1, source_target_pairs={{0,16},{8,24},{16,0},{24,8},{1,17},{9,25},{17,1},{25,9},{2,18},{10... | collective-permute-start | bytes 1179656 | tf_op jit(solution)/shard_map/joined_grad/ppermute | solution.py:37
  162.9 32.0 %collective-permute-start.31 = (bf16[96,2048]{1,0:T(8,128)(2,1)}, bf16[96,2048]{1,0:T(8,128)(2,1)S(1)}, u32[]{:S(2)}, u32[]{:S(2)}) collective-permute-start(bf16[96,2048]{1,0:T(8,128)(2,1)} %get-tuple-element.104), channel_id=1, source_target_pairs={{0,24},{8,16},{16,8},{24,0},{1,25},{9,17},{17,9},{25,1},{2,26},{10... | collective-permute-start | bytes 1179656 | tf_op jit(solution)/shard_map/joined_grad/ppermute | solution.py:37
  163.0 9.4 %copy-start.15 = (bf16[1,96,1280]{2,1,0:T(8,128)(2,1)S(1)}, bf16[1,96,1280]{2,1,0:T(8,128)(2,1)}, u32[]{:S(2)}) copy-start(bf16[1,96,1280]{2,1,0:T(8,128)(2,1)} %get-tuple-element.158) | copy-start | bytes 737284
  163.1 9.4 %copy-start.16 = (bf16[1,96,1280]{2,1,0:T(8,128)(2,1)S(1)}, bf16[1,96,1280]{2,1,0:T(8,128)(2,1)}, u32[]{:S(2)}) copy-start(bf16[1,96,1280]{2,1,0:T(8,128)(2,1)} %get-tuple-element.160) | copy-start | bytes 737284
  163.1 9.3 %copy-start.17 = (bf16[1,96,1280]{2,1,0:T(8,128)(2,1)S(1)}, bf16[1,96,1280]{2,1,0:T(8,128)(2,1)}, u32[]{:S(2)}) copy-start(bf16[1,96,1280]{2,1,0:T(8,128)(2,1)} %get-tuple-element.162) | copy-start | bytes 737284
  163.1 9.3 %copy-start.18 = (bf16[1,96,1280]{2,1,0:T(8,128)(2,1)S(1)}, bf16[1,96,1280]{2,1,0:T(8,128)(2,1)}, u32[]{:S(2)}) copy-start(bf16[1,96,1280]{2,1,0:T(8,128)(2,1)} %get-tuple-element.164) | copy-start | bytes 737284
  168.0 17.6 %collective-permute-start.27 = (bf16[96,1408]{1,0:T(8,128)(2,1)}, bf16[96,1408]{1,0:T(8,128)(2,1)}, u32[]{:S(2)}, u32[]{:S(2)}) collective-permute-start(bf16[96,1408]{1,0:T(8,128)(2,1)} %get-tuple-element.100), channel_id=1, source_target_pairs={{0,6},{2,4},{4,2},{6,0},{1,7},{3,5},{5,3},{7,1},{8,14},{10,12},{12... | collective-permute-start | bytes 811016 | tf_op jit(solution)/shard_map/joined_grad/ppermute | solution.py:37
  169.4 25.5 %collective-permute-start.28 = (bf16[96,1408]{1,0:T(8,128)(2,1)}, bf16[96,1408]{1,0:T(8,128)(2,1)}, u32[]{:S(2)}, u32[]{:S(2)}) collective-permute-start(bf16[96,1408]{1,0:T(8,128)(2,1)} %get-tuple-element.101), channel_id=1, source_target_pairs={{0,4},{2,6},{4,0},{6,2},{1,5},{3,7},{5,1},{7,3},{8,12},{10,14},{12... | collective-permute-start | bytes 811016 | tf_op jit(solution)/shard_map/joined_grad/ppermute | solution.py:37
  170.2 24.7 %collective-permute-start.29 = (bf16[96,1408]{1,0:T(8,128)(2,1)}, bf16[96,1408]{1,0:T(8,128)(2,1)}, u32[]{:S(2)}, u32[]{:S(2)}) collective-permute-start(bf16[96,1408]{1,0:T(8,128)(2,1)} %get-tuple-element.102), channel_id=1, source_target_pairs={{0,2},{2,0},{4,6},{6,4},{1,3},{3,1},{5,7},{7,5},{8,10},{10,8},{12,... | collective-permute-start | bytes 811016 | tf_op jit(solution)/shard_map/joined_grad/ppermute | solution.py:37
  174.6 11.1 %copy-start.19 = (bf16[96,2048]{1,0:T(8,128)(2,1)S(1)}, bf16[96,2048]{1,0:T(8,128)(2,1)}, u32[]{:S(2)}) copy-start(bf16[96,2048]{1,0:T(8,128)(2,1)} %get-tuple-element.109) | copy-start | bytes 1179652
  174.6 20.3 %copy-start.20 = (f32[96,1]{1,0:T(8,128)S(1)}, f32[96,1]{1,0:T(8,128)}, u32[]{:S(2)}) copy-start(f32[96,1]{1,0:T(8,128)} %copy.13) | copy-start | bytes 1156
  174.6 21.4 %copy-start.9 = (f32[96,1280]{1,0:T(8,128)S(1)}, f32[96,1280]{1,0:T(8,128)}, u32[]{:S(2)}) copy-start(f32[96,1280]{1,0:T(8,128)} %copy-done.8) | copy-start | bytes 1474564
  174.6 21.4 %copy-start.11 = (bf16[48,1280]{1,0:T(8,128)(2,1)S(1)}, bf16[48,1280]{1,0:T(8,128)(2,1)}, u32[]{:S(2)}) copy-start(bf16[48,1280]{1,0:T(8,128)(2,1)} %copy-done.10) | copy-start | bytes 368644
  174.6 21.4 %copy-start.13 = (bf16[48,1280]{1,0:T(8,128)(2,1)S(1)}, bf16[48,1280]{1,0:T(8,128)(2,1)}, u32[]{:S(2)}) copy-start(bf16[48,1280]{1,0:T(8,128)(2,1)} %copy-done.12) | copy-start | bytes 368644
  185.7 11.9 %collective-permute-start.33 = (bf16[96,2048]{1,0:T(8,128)(2,1)S(1)}, bf16[96,2048]{1,0:T(8,128)(2,1)S(1)}, u32[]{:S(2)}, u32[]{:S(2)}) collective-permute-start(bf16[96,2048]{1,0:T(8,128)(2,1)S(1)} %copy-done.19), channel_id=1, source_target_pairs={{0,8},{8,0},{16,24},{24,16},{1,9},{9,1},{17,25},{25,17},{2,10},{10... | collective-permute-start | bytes 1179656 | tf_op jit(solution)/shard_map/input_grads/ppermute | solution.py:37
  197.5 1.6 collective-permute-start.32
  199.2 10.2 %collective-permute-start.34 = (bf16[48,1280]{1,0:T(8,128)(2,1)S(1)}, bf16[48,1280]{1,0:T(8,128)(2,1)S(1)}, u32[]{:S(2)}, u32[]{:S(2)}) collective-permute-start(bf16[48,1280]{1,0:T(8,128)(2,1)S(1)} %get-tuple-element.156), channel_id=1, source_target_pairs={{0,1},{1,0},{2,3},{3,2},{4,5},{5,4},{6,7},{7,6},{8,9},{9,8},{10,11... | collective-permute-start | bytes 368648 | tf_op jit(solution)/shard_map/input_grads/ppermute | solution.py:41
  199.8 9.7 %collective-permute-start.35 = (bf16[48,1280]{1,0:T(8,128)(2,1)S(1)}, bf16[48,1280]{1,0:T(8,128)(2,1)S(1)}, u32[]{:S(2)}, u32[]{:S(2)}) collective-permute-start(bf16[48,1280]{1,0:T(8,128)(2,1)S(1)} %get-tuple-element.157), channel_id=1, source_target_pairs={{0,16},{8,24},{16,0},{24,8},{2,18},{10,26},{18,2},{26,10},{4,20},{... | collective-permute-start | bytes 368648 | tf_op jit(solution)/shard_map/input_grads/ppermute | solution.py:444
  202.0 7.5 %collective-permute-start.36 = (bf16[48,1280]{1,0:T(8,128)(2,1)S(1)}, bf16[48,1280]{1,0:T(8,128)(2,1)S(1)}, u32[]{:S(2)}, u32[]{:S(2)}) collective-permute-start(bf16[48,1280]{1,0:T(8,128)(2,1)S(1)} %get-tuple-element.155), channel_id=1, source_target_pairs={{0,17},{8,25},{16,1},{24,9},{2,19},{10,27},{18,3},{26,11},{4,21},{... | collective-permute-start | bytes 368648 | tf_op jit(solution)/shard_map/input_grads/ppermute | solution.py:447
  (12 other events, 45.4 us)

commit v3 on v1

v3 whole, which is shorter than its diff:
```python
import functools

import jax
import jax.numpy as jnp
from jax import lax
from jax.experimental import pallas as pl
from jax.experimental.pallas import tpu as pltpu
from jax.sharding import PartitionSpec as P

epsilon = 1e-05
f32 = jnp.float32
bf16 = jnp.bfloat16
kernel_memory = 16 << 20
brief = pl.CostEstimate(flops=0, bytes_accessed=0, transcendentals=0)
in_vmem = pl.BlockSpec(memory_space=pltpu.VMEM)
in_smem = pl.BlockSpec(memory_space=pltpu.SMEM)


def contract_rows(left, right):
    return lax.dot_general(
        left, right, (((0,), (0,)), ((), ())), preferred_element_type=f32
    )


def contract_cols(left, right):
    return lax.dot_general(
        left, right, (((1,), (1,)), ((), ())), preferred_element_type=f32
    )


def plain_dot(left, right):
    return jnp.dot(left, right, preferred_element_type=f32)


def flip(value, axis, size, mask):
    return lax.ppermute(value, axis, [(i, i ^ mask) for i in range(size)])


def swap(value):
    return lax.ppermute(value, "dp", [(0, 1), (1, 0)])


def params(memory):
    return pltpu.CompilerParams(vmem_limit_bytes=memory)


def shaped(*shape_and_type):
    *shape, dtype = shape_and_type
    return jax.ShapeDtypeStruct(tuple(shape), dtype)


def tensor_at(places):
    return places[0] % 16


def dp_at(places):
    return places[0] // 16


def whole_call(kernel, places, arrays, outs):
    return pl.pallas_call(
        kernel,
        out_shape=outs,
        in_specs=[in_smem] + [in_vmem] * len(arrays),
        out_specs=[in_vmem] * len(outs),
        compiler_params=params(kernel_memory),
        cost_estimate=brief,
    )(places, *arrays)


def join_rows(places, kept, given, put):
    half = kept.shape[0]

    @pl.when(dp_at(places) == 0)
    def _():
        put(slice(0, half), kept[...])
        put(slice(half, 2 * half), given[...])

    @pl.when(dp_at(places) != 0)
    def _():
        put(slice(0, half), given[...])
        put(slice(half, 2 * half), kept[...])


def column_block(j, block):
    return pl.ds(pl.multiple_of(j * block, 128), block)


def project_own_kernel(places, kept, given, weight, own, raw, squares):
    j = pl.program_id(0)

    @pl.when(j == 0)
    def _():
        def put(rows, value):
            own[rows] = value

        join_rows(places, kept, given, put)
        values = own[...].astype(f32)
        squares[...] = jnp.sum(values * values, axis=1, keepdims=True)
        raw[...] = jnp.zeros_like(raw)

    raw[...] += plain_dot(own[:, column_block(j, weight.shape[0])], weight[...])


def project_own(places, kept, given, weight, blocks):
    half, width = kept.shape
    rows = 2 * half
    fixed = lambda j, c: (0, 0)
    return pl.pallas_call(
        project_own_kernel,
        out_shape=[shaped(rows, width, bf16), shaped(rows, width, f32), shaped(rows, 1, f32)],
        grid_spec=pltpu.PrefetchScalarGridSpec(
            num_scalar_prefetch=1,
            grid=(blocks,),
            in_specs=[
                pl.BlockSpec((half, width), fixed),
                pl.BlockSpec((half, width), fixed),
                pl.BlockSpec((width // blocks, width), lambda j, c: (tensor_at(c) * blocks + j, 0)),
            ],
            out_specs=[
                pl.BlockSpec((rows, width), fixed),
                pl.BlockSpec((rows, width), fixed),
                pl.BlockSpec((rows, 1), fixed),
            ],
        ),
        compiler_params=params(kernel_memory),
        cost_estimate=brief,
    )(places, kept, given, weight)


def project_kernel(features, count, blocks, places, *refs):
    kept, given = refs[:count], refs[count : 2 * count]
    weight, raw, own_squares = refs[2 * count : 2 * count + 3]
    parts, projected, low, scale, held, done = refs[2 * count + 3 :]
    squares = own_squares[...]
    total = projected
    chunks = list(range(1, count + 1))
    for n, right in streamed(places, weight, chunks, blocks, held, done):
        k, j = n // blocks, n % blocks
        block = right.shape[0]
        if j == 0:

            def put(rows, value, k=k):
                parts[k, rows] = value

            join_rows(places, kept[k], given[k], put)
            values = parts[k].astype(f32)
            squares = squares + jnp.sum(values * values, axis=1, keepdims=True)
        product = plain_dot(parts[k, :, j * block : (j + 1) * block], right)
        total[...] = product + (raw[...] if n == 0 else total[...])
    scale[...] = lax.rsqrt(squares / features + epsilon)
    projected[...] = total[...] * scale[...]
    low[...] = projected[...].astype(bf16)


def project(places, kept, given, weight, raw, squares, features, blocks):
    count = len(kept)
    half, width = kept[0].shape
    rows = 2 * half
    return pl.pallas_call(
        functools.partial(project_kernel, features, count, blocks),
        out_shape=[
            shaped(count, rows, width, bf16),
            shaped(rows, width, f32),
            shaped(rows, width, bf16),
            shaped(rows, 1, f32),
        ],
        in_specs=[in_smem]
        + [in_vmem] * (2 * count)
        + [pl.BlockSpec(memory_space=pl.ANY), in_vmem, in_vmem],
        out_specs=[in_vmem] * 4,
        scratch_shapes=[
            pltpu.VMEM((count * blocks, width // blocks, width), weight.dtype),
            pltpu.SemaphoreType.DMA((count * blocks,)),
        ],
        compiler_params=params(kernel_memory),
        cost_estimate=brief,
    )(places, *kept, *given, weight, raw, squares)


def held_columns_kernel(count, _, left, *refs):
    rights, extras, outs = refs[:count], refs[count:-count], refs[-count:]
    size = rights[0].shape[0]
    for right, out in zip(rights, outs):
        out[:, :size] = contract_cols(left[...], right[...]).astype(out.dtype)
        for extra in extras:
            out[:, size:] = extra[...]


def held_columns(places, left, rights, dtype, extra=None):
    extras = [] if extra is None else [extra]
    wide = rights[0].shape[0] + sum(e.shape[1] for e in extras)
    return whole_call(
        functools.partial(held_columns_kernel, len(rights)),
        places,
        [left] + rights + extras,
        [shaped(left.shape[0], wide, dtype) for _ in rights],
    )


def held_between_kernel(places, outer, inner, right, out):
    t = tensor_at(places)
    left = jnp.where((t == 0) | (t == 3), outer[...], inner[...])
    out[...] = plain_dot(left, right[...])


def streamed(places, weight, chunks, blocks, held, done):
    slots, block, _ = held.shape
    copies = []
    for n in range(blocks * len(chunks)):
        start = (n % blocks) * block
        if chunks[n // blocks] is not None:
            place = tensor_at(places) ^ chunks[n // blocks]
            start = pl.multiple_of(place * (blocks * block) + start, block)
        slot = n % slots
        copies.append(
            pltpu.make_async_copy(weight.at[pl.ds(start, block)], held.at[slot], done.at[slot])
        )
    for copy in copies[:slots]:
        copy.start()
    for n, copy in enumerate(copies):
        copy.wait()
        yield n, held[n % slots]
        if n + slots < len(copies):
            copies[n + slots].start()


def stream_columns_kernel(chunks, blocks, places, left, weight, *refs):
    outs, (held, done) = refs[:-2], refs[-2:]
    block = held.shape[1]
    for n, right in streamed(places, weight, chunks, blocks, held, done):
        j = n % blocks
        product = contract_cols(left[...], right)
        outs[n // blocks][:, j * block : (j + 1) * block] = product.astype(outs[0].dtype)


def stream_rows_kernel(chunks, blocks, places, *refs):
    count = len(chunks)
    lefts, weight, outs, (held, done) = refs[:count], refs[count], refs[count + 1 : -2], refs[-2:]
    block = held.shape[1]
    for n, right in streamed(places, weight, chunks, blocks, held, done):
        k, j = n // blocks, n % blocks
        product = plain_dot(lefts[k][:, j * block : (j + 1) * block], right)
        if j == 0:
            outs[k][...] = product
        else:
            outs[k][...] += product


def stream(kernel, places, lefts, weight, chunks, size, outs, blocks, slots):
    return pl.pallas_call(
        functools.partial(kernel, chunks, blocks),
        out_shape=outs,
        in_specs=[in_smem] + [in_vmem] * len(lefts) + [pl.BlockSpec(memory_space=pl.ANY)],
        out_specs=[in_vmem] * len(outs),
        scratch_shapes=[
            pltpu.VMEM((slots, size // blocks, weight.shape[1]), weight.dtype),
            pltpu.SemaphoreType.DMA((slots,)),
        ],
        compiler_params=params(kernel_memory),
        cost_estimate=brief,
    )(places, *lefts, weight)


def stream_columns(places, left, weight, chunks, size, blocks, dtype):
    outs = [shaped(left.shape[0], size, dtype) for _ in chunks]
    slots = blocks * len(chunks)
    return stream(
        stream_columns_kernel, places, [left], weight, chunks, size, outs, blocks, slots
    )


def stream_rows(places, lefts, weight, chunks, blocks, slots):
    rows, size = lefts[0].shape
    outs = [shaped(rows, weight.shape[1], f32) for _ in chunks]
    return stream(
        stream_rows_kernel, places, lefts, weight, chunks, size, outs, blocks, slots
    )


def combine_kernel(places, own, part, grad, out):
    c = pl.program_id(0)

    @pl.when(tensor_at(places) == c)
    def _():
        out[...] = contract_rows(own[...], grad[...])

    @pl.when(tensor_at(places) != c)
    def _():
        out[...] = contract_rows(part[0], grad[...])


def combine(places, own, parts, grad):
    rows, width = own.shape
    count = parts.shape[0] + 1
    fixed = lambda c, w: (0, 0)
    return pl.pallas_call(
        combine_kernel,
        out_shape=shaped(count * width, grad.shape[1], f32),
        grid_spec=pltpu.PrefetchScalarGridSpec(
            num_scalar_prefetch=1,
            grid=(count,),
            in_specs=[
                pl.BlockSpec((rows, width), fixed),
                pl.BlockSpec(
                    (1, rows, width), lambda c, w: (jnp.maximum((tensor_at(w) ^ c) - 1, 0), 0, 0)
                ),
                pl.BlockSpec((rows, grad.shape[1]), fixed),
            ],
            out_specs=pl.BlockSpec((width, grad.shape[1]), lambda c, w: (c, 0)),
        ),
        compiler_params=params(kernel_memory),
        cost_estimate=brief,
    )(places, own, parts, grad)


def head_sum_kernel(*refs):
    out = refs[-1]
    count = (len(refs) - 1) // 2
    left = jnp.concatenate([r[...] for r in refs[:count]], axis=0)
    right = jnp.concatenate([r[...] for r in refs[count : 2 * count]], axis=0)
    out[...] = contract_rows(left, right)


def head_sum(grads, normed, blocks):
    rows, size = grads[0].shape
    width = normed[0].shape[1]
    block = size // blocks
    return pl.pallas_call(
        head_sum_kernel,
        out_shape=shaped(size, width, f32),
        grid=(blocks,),
        in_specs=[pl.BlockSpec((rows, block), lambda j: (0, j))] * len(grads)
        + [pl.BlockSpec((rows, width), lambda j: (0, 0))] * len(normed),
        out_specs=pl.BlockSpec((block, width), lambda j: (j, 0)),
        compiler_params=params(kernel_memory),
        cost_estimate=brief,
    )(*grads, *normed)


def input_grad_kernel(features, places, side, own, in_scale, grad_mixed, dots, *refs):
    came, (term, term_low) = refs[:-2], refs[-2:]
    width = side.shape[1]
    total = side[...]
    dot = dots[...]
    for each in came:
        total = total + each[:, :width].astype(f32)
        dot = dot + (
            each[:, width : width + 1].astype(f32) + each[:, width + 1 : width + 2].astype(f32)
        )
    normed = own[...].astype(f32) * in_scale[...]
    value = in_scale[...] * (total - normed * (dot / features))
    value = value + jnp.where(dp_at(places) == 0, grad_mixed[...], 0.0)
    term[...] = value
    term_low[...] = value.astype(bf16)


def fast_local(
    n_head,
    n_tensor,
    trunk_hidden,
    next_embeds,
    combine_weight,
    final_gain,
    unembed_weight,
    target_ids,
    loss_scale,
):
    half, width = trunk_hidden.shape
    rows = 2 * half
    features = width * n_tensor
    vocab_part = unembed_weight.shape[0]
    piece = vocab_part // n_tensor
    combine_whole, unembed_whole = combine_weight[0], unembed_weight
    weight_block = pltpu.with_memory_space_constraint(combine_weight[0], pltpu.HBM)
    unembed_weight = pltpu.with_memory_space_constraint(unembed_weight, pltpu.HBM)
    d = lax.axis_index("dp")
    t = lax.axis_index("tensor")
    h = lax.axis_index("head")
    first = d == 0
    places = (t + 16 * d).astype(jnp.int32).reshape(1)
    row_weights = loss_scale[0]

    def chunk_of(weight, r, size):
        return lax.dynamic_slice_in_dim(weight, (t ^ r) * size, size, 0)

    def spread(value):
        return [value] + [flip(value, "tensor", n_tensor, r) for r in range(1, n_tensor)]

    with jax.named_scope("inputs"):
        embeds = next_embeds[0]
        kept = jnp.where(first, trunk_hidden, embeds)
        given = jnp.where(first, embeds, trunk_hidden)
        kept_parts = spread(kept)
        swapped = swap(given)
        kept_parts, swapped = lax.optimization_barrier((kept_parts, swapped))
        given_parts = spread(swapped)
        trunk_other = swap(trunk_hidden)
        own, raw, squares = project_own(places, kept_parts[0], swapped, weight_block, 2)
        given_parts, trunk_other, own, raw, squares = lax.optimization_barrier(
            (given_parts, trunk_other, own, raw, squares)
        )
    with jax.named_scope("projection"):
        parts, projected, projected_low, in_scale = project(
            places, kept_parts[1:], given_parts[1:], weight_block, raw, squares, features, 2
        )
        projected_there = swap(projected_low)
        weight_far = chunk_of(unembed_whole, 3, piece)
        projected_there, weight_far = lax.optimization_barrier((projected_there, weight_far))
        trunk_rows = jnp.where(
            first, own, jnp.concatenate([trunk_other, trunk_hidden], axis=0)
        ).astype(f32)
        mixed = trunk_rows + (projected + projected_there.astype(f32))
        gained = mixed * final_gain[None, :]
        low = gained.astype(bf16)
    with jax.named_scope("logits"):
        (far,) = held_columns(places, low, [weight_far], f32)
        ends = lax.ppermute(far, "tensor", [(0, 1), (3, 2)])
        middle = lax.ppermute(far, "tensor", [(1, 2), (2, 1)])
        mixed_squares = spread(jnp.sum(mixed * mixed, axis=1))
        cross, near = stream_columns(places, low, unembed_weight, [2, 1], piece, 4, f32)
        wanted = (target_ids[0] - d * vocab_part)[:, None]
        ends, middle, mixed_squares, cross, near, low, wanted = lax.optimization_barrier(
            (ends, middle, mixed_squares, cross, near, low, wanted)
        )
        mixed_scale = lax.rsqrt(sum(mixed_squares) / features + epsilon)[:, None]
        normed_out = (gained * mixed_scale).astype(bf16)
        normed_heads = [normed_out] + [
            flip(normed_out, "head", n_head, m) for m in range(1, n_head)
        ]
        cross = flip(cross + ends, "tensor", n_tensor, 2)
        near = flip(near, "tensor", n_tensor, 1)
        chosen = lax.broadcasted_iota(jnp.int32, (1, vocab_part), 1) == wanted
        (target_rows,) = stream_rows(
            places, [chosen.astype(bf16)], unembed_weight, [None], 16, 8
        )
        (last,) = stream_columns(places, low, unembed_weight, [0], piece, 4, f32)
        cross, near, normed_heads, target_rows, last = lax.optimization_barrier(
            (cross, near, normed_heads, target_rows, last)
        )
        logits = (last + middle + cross + near) * mixed_scale
    with jax.named_scope("softmax"):
        hits = (lax.broadcasted_iota(jnp.int32, (1, piece), 1) + t * piece) == wanted
        top = jnp.max(logits, axis=1)
        shifted = jnp.exp(logits - top[:, None])
        shifted_low = jnp.where(hits, 0.0, shifted).astype(bf16)
        stats = jnp.stack(
            [
                top,
                jnp.sum(shifted, axis=1),
                jnp.sum(jnp.where(hits, logits, 0.0), axis=1),
                jnp.sum(shifted_low.astype(f32) * logits, axis=1),
            ]
        )
    with jax.named_scope("grad_normed"):
        cross = flip(shifted_low, "tensor", n_tensor, 2)
        near = flip(shifted_low, "tensor", n_tensor, 1)
        there = swap(stats)
        products = stream_rows(places, [shifted_low], unembed_weight, [0], 4, 4)
        weight_sent = [chunk_of(combine_whole, r, width) for r in (3, 2, 1)]
        weight_far = chunk_of(unembed_whole, 3, piece)
        cross, near, there, products, value, weight_sent, weight_far = lax.optimization_barrier(
            (cross, near, there, products, shifted_low, weight_sent, weight_far)
        )
        ends = lax.ppermute(cross, "tensor", [(2, 3), (1, 0)])
        middle = lax.ppermute(value, "tensor", [(1, 2), (2, 1)])
        pair_top = jnp.maximum(top, there[0])
        here_by, there_by = jnp.exp(top - pair_top), jnp.exp(there[0] - pair_top)
        stats = spread(
            jnp.stack(
                [
                    top,
                    pair_top,
                    stats[1] * here_by + there[1] * there_by,
                    stats[2] + there[2],
                    stats[3] * here_by + there[3] * there_by,
                ]
            )
        )
        stats, near, cross = lax.optimization_barrier((stats, near, cross))
        products += stream_rows(places, [near, cross], unembed_weight, [1, 2], 4, 8)
        ends, middle, products = lax.optimization_barrier((ends, middle, products))
        products += whole_call(
            held_between_kernel,
            places,
            [ends, middle, weight_far],
            [shaped(rows, width, f32)],
        )
        far = jnp.where((t == 0) | (t == n_tensor - 1), ends, middle)
        shifted_parts = [shifted_low, near, cross, far]
        largest = jnp.max(jnp.stack([s[1] for s in stats]), axis=0)
        by = [jnp.exp(s[1] - largest) for s in stats]
        summed = sum(s[2] * b for s, b in zip(stats, by))
        hit_logit = sum(s[3] for s in stats)
        per_row = row_weights / summed
        hit_grad = row_weights * (jnp.exp(hit_logit - largest) / summed - 1.0)
        grad_dots = per_row * sum(s[4] * b for s, b in zip(stats, by)) + hit_grad * hit_logit
        factors = [per_row * jnp.exp(s[0] - largest) for s in stats]
        grad_part = hit_grad[:, None] * target_rows
        for r, product in enumerate(products):
            grad_part = grad_part + factors[r][:, None] * product
        grad_there = swap(grad_part.astype(bf16))
        ids = lax.broadcasted_iota(jnp.int32, (1, piece), 1)
        grad_stack = jnp.stack(
            [
                jnp.where(
                    (ids + (t ^ r) * piece) == wanted,
                    hit_grad[:, None],
                    e.astype(f32) * factors[r][:, None],
                ).astype(bf16)
                for r, e in enumerate(shifted_parts)
            ]
        )
        grad_slices = [
            lax.dynamic_index_in_dim(grad_stack, t ^ h ^ m, 0, keepdims=False)
            for m in range(n_head)
        ]
        grad_there, grad_slices = lax.optimization_barrier((grad_there, grad_slices))
    with jax.named_scope("grad_mixed"):
        grad_normed = grad_part + grad_there.astype(f32)
        mixed_normed = mixed * mixed_scale
        grad_mixed = mixed_scale * (
            grad_normed * final_gain[None, :] - mixed_normed * (grad_dots / features)[:, None]
        )
        grad_low = grad_mixed.astype(bf16)
        grad_scaled = (in_scale * grad_mixed).astype(bf16)
        dots = jnp.sum(grad_low.astype(f32) * projected, axis=1, keepdims=True)
        dots_high = lax.reduce_precision(dots, 8, 7)
        lane = lax.broadcasted_iota(jnp.int32, (1, 128), 1)
        extra = jnp.where(
            lane == 0, dots_high, jnp.where(lane == 1, dots - dots_high, 0.0)
        ).astype(bf16)
    with jax.named_scope("joined_grad"):
        sent = held_columns(places, grad_low, weight_sent, bf16, extra)
        came = [flip(c, "tensor", n_tensor, r) for r, c in zip((3, 2, 1), sent)]
        heads_given = [flip(grad_slices[m], "head", n_head, m) for m in range(1, n_head)]
        (side,) = stream_columns(places, grad_low, weight_block, [0], width, 2, f32)
        combine_grad = combine(places, own, parts, grad_scaled)[None]
        unembed_grad = head_sum([grad_slices[0]] + heads_given, normed_heads, 2)
        unembed_grad = unembed_grad.reshape(1, 1, piece, width)
        came, side, combine_grad, unembed_grad = lax.optimization_barrier(
            (came, side, combine_grad, unembed_grad)
        )
    with jax.named_scope("input_grads"):
        term, term_low = whole_call(
            functools.partial(input_grad_kernel, features),
            places,
            [side, own, in_scale, grad_mixed, dots] + came,
            [shaped(rows, width, f32), shaped(rows, width, bf16)],
        )
        pair = flip(term_low, "head", n_head, 1)
        pair = term_low.astype(f32) + pair.astype(f32)
        pair_low = pair.astype(bf16)
        crossed = swap(jnp.where(first, pair_low[half:], term_low[:half]))
        beside = lax.ppermute(
            pair_low[:half], ("head", "dp"), [(2 * i, 2 * (i ^ 2)) for i in range(n_head)]
        )
        across = lax.ppermute(
            pair_low[half:], ("head", "dp"), [(2 * i, 2 * (i ^ 2) + 1) for i in range(n_head)]
        )
        crossed, beside, across = [v.astype(f32) for v in (crossed, beside, across)]
        embed_grad = jnp.where(first, crossed, term[half:])[None]
        trunk_grad = jnp.where(first, pair[:half] + beside, crossed + across)
    return (trunk_grad, embed_grad, combine_grad, unembed_grad)


def general_local(
    n_tensor,
    trunk_hidden,
    next_embeds,
    combine_weight,
    final_gain,
    unembed_weight,
    target_ids,
    loss_scale,
):
    rows, part_width = trunk_hidden.shape
    features = part_width * n_tensor
    vocab_part = unembed_weight.shape[0]
    weight_block = combine_weight[0]
    trunk_whole, embed_whole = (
        lax.all_gather(trunk_hidden, "tensor", axis=1, tiled=True),
        lax.all_gather(next_embeds[0], "tensor", axis=1, tiled=True),
    )
    trunk_float = trunk_whole.astype(f32)
    embed_float = embed_whole.astype(f32)
    trunk_scale = lax.rsqrt(jnp.sum(trunk_float * trunk_float, axis=1) / features + epsilon)
    embed_scale = lax.rsqrt(jnp.sum(embed_float * embed_float, axis=1) / features + epsilon)
    trunk_normed = trunk_float * trunk_scale[:, None]
    embed_normed = embed_float * embed_scale[:, None]
    joined = jnp.concatenate([trunk_normed.astype(bf16), embed_normed.astype(bf16)], axis=1)
    feature_start = lax.axis_index("tensor") * part_width
    trunk_local = lax.dynamic_slice_in_dim(trunk_normed, feature_start, part_width, 1)
    embed_local = lax.dynamic_slice_in_dim(embed_normed, feature_start, part_width, 1)
    blocks = lax.all_to_all(joined, "dp", split_axis=1, concat_axis=0, tiled=True)
    projected = lax.psum_scatter(
        plain_dot(blocks, weight_block).astype(bf16), "dp", scatter_dimension=0, tiled=True
    ).astype(f32)
    mixed = trunk_hidden.astype(f32) + projected
    mixed_sums = lax.psum(jnp.sum(mixed * mixed, axis=1), "tensor")
    mixed_scale = lax.rsqrt(mixed_sums / features + epsilon)
    mixed_normed = mixed * mixed_scale[:, None]
    normed_out = (mixed_normed * final_gain[None, :]).astype(bf16)
    normed_all = lax.all_gather(normed_out, "dp", axis=0, tiled=True)
    logits = lax.psum(contract_cols(normed_all, unembed_weight), "tensor")
    largest = lax.pmax(jnp.max(logits, axis=1), "dp")
    shifted = jnp.exp(logits - largest[:, None])
    summed = lax.psum(jnp.sum(shifted, axis=1), "dp")
    probs = shifted / summed[:, None]
    vocab_ids = (
        lax.broadcasted_iota(jnp.int32, (1, vocab_part), 1) + lax.axis_index("dp") * vocab_part
    )
    hits = (vocab_ids == target_ids[0][:, None]).astype(f32)
    grad_local = (loss_scale[0][:, None] * (probs - hits)).astype(bf16)
    grad_normed = lax.psum_scatter(
        plain_dot(grad_local, unembed_weight).astype(bf16), "dp", scatter_dimension=0, tiled=True
    ).astype(f32)
    vocab_term = contract_rows(grad_local, normed_all).astype(bf16)
    vocab_total = lax.psum_scatter(vocab_term, "head", scatter_dimension=0, tiled=True).astype(f32)
    unembed_grad = vocab_total.reshape(1, 1, vocab_total.shape[0], part_width)
    scaled_grad = grad_normed * final_gain[None, :]
    grad_dots = lax.psum(jnp.sum(scaled_grad * mixed_normed, axis=1), "tensor")
    grad_mixed = mixed_scale[:, None] * (
        scaled_grad - mixed_normed * (grad_dots / features)[:, None]
    )
    grad_all = lax.all_gather(grad_mixed.astype(bf16), "dp", axis=0, tiled=True)
    combine_grad = contract_rows(blocks, grad_all)[None]
    joined_part = lax.all_to_all(
        contract_cols(grad_all, weight_block).astype(bf16),
        "dp",
        split_axis=0,
        concat_axis=1,
        tiled=True,
    )
    joined_grad = lax.psum_scatter(
        joined_part.reshape(rows, 2, features), "tensor", scatter_dimension=2, tiled=True
    ).astype(f32)
    trunk_side = joined_grad[:, 0]
    embed_side = joined_grad[:, 1]
    trunk_dots, embed_dots = lax.psum(
        (jnp.sum(trunk_side * trunk_local, axis=1), jnp.sum(embed_side * embed_local, axis=1)),
        "tensor",
    )
    trunk_term = trunk_scale[:, None] * (
        trunk_side - trunk_local * (trunk_dots / features)[:, None]
    )
    embed_grad = (
        embed_scale[:, None] * (embed_side - embed_local * (embed_dots / features)[:, None])
    )[None]
    trunk_grad = lax.psum((grad_mixed + trunk_term).astype(bf16), "head").astype(f32)
    return (trunk_grad, embed_grad, combine_grad, unembed_grad)


def solution(mesh):
    n_head, n_tensor, n_dp = mesh.shape["head"], mesh.shape["tensor"], mesh.shape["dp"]
    in_specs = (
        P("dp", "tensor"),
        P("head", "dp", "tensor"),
        P("head", "dp", "tensor"),
        P("tensor"),
        P("dp", "tensor"),
        P("head", None),
        P("head", None),
    )
    out_specs = (
        P("dp", "tensor"),
        P("head", "dp", "tensor"),
        P("head", "dp", "tensor"),
        P("dp", "head", None, "tensor"),
    )
    if n_dp == 2 and n_tensor == 4 and n_head == 4:

        def local(*args):
            return fast_local(n_head, n_tensor, *args)

    else:

        def local(*args):
            return general_local(n_tensor, *args)

    return jax.shard_map(local, mesh=mesh, in_specs=in_specs, out_specs=out_specs, check_vma=False)
```

time: 245 us -> 204 us (0.83)
  matrix products: 63.2 us -> 0 us
  Pallas kernels: 0 us -> 59.4 us
  waiting for transfers between devices: 94.9 us -> 63.9 us
  starting transfers between devices: 69.7 us -> 50.9 us
  local copies, waits for them, and re-layouts: 1.64 us -> 14.2 us
    ppermute x26 -> x6, waiting for transfers between devices: 69.7 us -> 1.99 us  [the longest x1 1.48 us: fast_local(): lax.ppermute(pair_low[half:], ('head', 'dp'), [(2 * i, 2 * (i ^ 2) + 1) f...]
    dot_general x18 -> x0, matrix products: 63.2 us -> none  [the longest x8 25 us: plain_dot(): return jnp.dot(left, right, preferred_element_type=f32)]
    pallas_call x0 -> x14, Pallas kernels: none -> 59.4 us  [the longest x6 28 us: stream(): pl.pallas_call(functools.partial(kernel, chunks, blocks), out_shape=outs,...]
    ppermute x8 -> x26, waiting for transfers between devices: 9.83 us -> 54.6 us  [flip(): return lax.ppermute(value, axis, [(i, i ^ mask) for i in range(size)])]
    ppermute x26 -> x6, starting transfers between devices: 52.2 us -> 14.6 us  [the longest x1 4.15 us: fast_local(): ends = lax.ppermute(far, 'tensor', [(0, 1), (3, 2)])]
    ppermute x8 -> x26, starting transfers between devices: 5.03 us -> 31.2 us  [flip(): return lax.ppermute(value, axis, [(i, i ^ mask) for i in range(size)])]
    dynamic_slice x1 -> x2, local copies, waits for them, and re-layouts: 0.69 us -> 10.8 us  [chunk_of(): return lax.dynamic_slice_in_dim(weight, (t ^ r) * size, size, 0)]
    ppermute x7 -> x6, waiting for transfers between devices: 15.4 us -> 7.24 us  [swap(): return lax.ppermute(value, 'dp', [(0, 1), (1, 0)])]
  transfers between devices with their start and end apart: 41 -> 38, of which waited for: 20 -> 15; matrix products, arithmetic and copies ran while one was open for 20% -> 11% of each run, Pallas kernels for 0% -> 25%
where the time goes in v3:
time: 204 us; the launch traced here: 203 us
  waiting for transfers between devices  63.9 us (31%)
  Pallas kernels  59.4 us (29%)
  starting transfers between devices  50.9 us (25%)
  local copies, waits for them, and re-layouts  14.2 us (7%)
  other arithmetic  13.2 us (6%)
    ppermute x26, waiting for transfers between devices, flip(): return lax.ppermute(value, axis, [(i, i ^ mask) for i in range(size)])  54.6 us
    ppermute x26, starting transfers between devices, flip(): return lax.ppermute(value, axis, [(i, i ^ mask) for i in range(size)])  31.2 us
    pallas_call x6, Pallas kernels, stream(): pl.pallas_call(functools.partial(kernel, chunks, blocks), out_shape=outs,...  28 us
    dynamic_slice x2, local copies, waits for them, and re-layouts, chunk_of(): return lax.dynamic_slice_in_dim(weight, (t ^ r) * size, size, 0)  10.8 us
    pallas_call x1, Pallas kernels, combine(): pl.pallas_call(combine_kernel, out_shape=shaped(count * width, grad.shape...  9.98 us
    pallas_call x4, Pallas kernels, whole_call(): pl.pallas_call(kernel, out_shape=outs, in_specs=[in_smem] + [in_vmem] * l...  7.97 us
    ppermute x6, waiting for transfers between devices, swap(): return lax.ppermute(value, 'dp', [(0, 1), (1, 0)])  7.24 us
    pallas_call x1, Pallas kernels, head_sum(): pl.pallas_call(head_sum_kernel, out_shape=shaped(size, width, f32), grid=...  6.65 us
  transfers between devices with their start and end apart: 38, of which 15 were waited for; matrix products, arithmetic and copies ran while one was open for 11% of the time, Pallas kernels for 25%

profile of v3, /device:TPU:0, one launch (start us, length us, event | category | flops | bytes accessed | tf_op | source)
XLA Modules:
  0.0 203.0 jit_solution(7099636330745120473)
XLA Ops:
  0.6 1.0 bitcast_select_fusion
  1.6 3.0 %collective-permute-start.3 = (bf16[48,1280]{1,0:T(8,128)(2,1)S(1)}, bf16[48,1280]{1,0:T(8,128)(2,1)S(1)}, u32[]{:S(2)}, u32[]{:S(2)}) collective-permute-start(bf16[48,1280]{1,0:T(8,128)(2,1)S(1)} %get-tuple-element.193), channel_id=1, source_target_pairs={{0,1},{1,0},{2,3},{3,2},{4,5},{5,4},{6,7},{7,6},{8,9},{9,8},{10,11... | collective-permute-start | bytes 368648 | tf_op jit(solution)/shard_map/inputs/ppermute | solution.py:40
  4.7 3.6 %collective-permute-start.2 = (bf16[48,1280]{1,0:T(8,128)(2,1)S(1)}, bf16[48,1280]{1,0:T(8,128)(2,1)S(1)}, u32[]{:S(2)}, u32[]{:S(2)}) collective-permute-start(bf16[48,1280]{1,0:T(8,128)(2,1)S(1)} %get-tuple-element.84.kept), channel_id=1, source_target_pairs={{0,6},{2,4},{4,2},{6,0},{1,7},{3,5},{5,3},{7,1},{8,14},{10,12},{12... | collective-permute-start | bytes 368648 | tf_op jit(solution)/shard_map/inputs/ppermute | solution.py:36
  8.3 0.8 collective-permute-start
  9.3 3.5 %collective-permute-done.2.refs_2_ = bf16[48,1280]{1,0:T(8,128)(2,1)S(1)} collective-permute-done((bf16[48,1280]{1,0:T(8,128)(2,1)S(1)}, bf16[48,1280]{1,0:T(8,128)(2,1)S(1)}, u32[]{:S(2)}, u32[]{:S(2)}) %collective-permute-start.2) | collective-permute-done | bytes 122912 | tf_op jit(solution)/shard_map/inputs/ppermute | solution.py:36
  12.8 5.5 %collective-permute-done.1.refs_1_ = bf16[48,1280]{1,0:T(8,128)(2,1)S(1)} collective-permute-done((bf16[48,1280]{1,0:T(8,128)(2,1)S(1)}, bf16[48,1280]{1,0:T(8,128)(2,1)S(1)}, u32[]{:S(2)}, u32[]{:S(2)}) %collective-permute-start.1) | collective-permute-done | bytes 122912 | tf_op jit(solution)/shard_map/inputs/ppermute | solution.py:36
  18.4 2.7 %collective-permute-start.6 = (bf16[48,1280]{1,0:T(8,128)(2,1)S(1)}, bf16[48,1280]{1,0:T(8,128)(2,1)S(1)}, u32[]{:S(2)}, u32[]{:S(2)}) collective-permute-start(bf16[48,1280]{1,0:T(8,128)(2,1)S(1)} %collective-permute-done.3.given), channel_id=1, source_target_pairs={{0,6},{2,4},{4,2},{6,0},{1,7},{3,5},{5,3},{7,1},{8,14},{10,12},{12... | collective-permute-start | bytes 368648 | tf_op jit(solution)/shard_map/inputs/ppermute | solution.py:36
  21.1 1.7 collective-permute-start.4
  22.7 2.5 %inputs.1 = (bf16[96,1280]{1,0:T(8,128)(2,1)S(1)}, f32[96,1280]{1,0:T(8,128)S(1)}, f32[96,1]{1,0:T(8,128)S(1)}) custom-call(s32[1]{0:T(128)} %bitcast.places._, bf16[48,1280]{1,0:T(8,128)(2,1)S(1)} %get-tuple-element.84.kept, bf16[48,1280]{1,0:T(8,128)(2,1)S(1)} %collective-permute-done.3.given, bf16[5120,1280]{1,0:T(8,128)(2,1)} %bitcast.193), custom_call_target="tpu_custom_call" | custom-call | tf_op jit(solution)/shard_map/inputs/pallas_call | solution.py:109
  25.2 1.2 collective-permute-done.6.refs_5_
  26.4 4.2 %collective-permute-done.5.refs_4_ = bf16[48,1280]{1,0:T(8,128)(2,1)S(1)} collective-permute-done((bf16[48,1280]{1,0:T(8,128)(2,1)S(1)}, bf16[48,1280]{1,0:T(8,128)(2,1)S(1)}, u32[]{:S(2)}, u32[]{:S(2)}) %collective-permute-start.5) | collective-permute-done | bytes 122912 | tf_op jit(solution)/shard_map/inputs/ppermute | solution.py:36
  30.6 4.4 %projection.1 = (bf16[3,96,1280]{2,1,0:T(8,128)(2,1)S(1)}, f32[96,1280]{1,0:T(8,128)S(1)}, bf16[96,1280]{1,0:T(8,128)(2,1)S(1)}, f32[96,1]{1,0:T(8,128)S(1)}) custom-call(s32[1]{0:T(128)} %bitcast.places._, bf16[48,1280]{1,0:T(8,128)(2,1)S(1)} %collective-permute-done.refs_0_, bf16[48,1280]{1,0:T(8,128)(2,1)S(1)} %collective-permute-done.1.refs_1_, ...), custom_call_target="tpu_custom_call" | custom-call | tf_op jit(solution)/shard_map/projection/pallas_call | solution.py:160
  35.0 0.9 copy-done.6
  37.0 2.8 %constant_dynamic-slice_fusion.refs_0_.right = bf16[2048,1280]{1,0:T(8,128)(2,1)S(1)} fusion(bf16[8192,1280]{1,0:T(8,128)(2,1)} %refs_2_.1, s32[]{:T(128)S(6)} %select_n.102), kind=kLoop, calls=%fused_computation.53 | loop fusion | bytes 10485764 | tf_op jit(solution)/shard_map/projection/dynamic_slice | solution.py:385
  39.8 3.9 %collective-permute-done.8 = bf16[96,1280]{1,0:T(8,128)(2,1)S(1)} collective-permute-done((bf16[96,1280]{1,0:T(8,128)(2,1)S(1)}, bf16[96,1280]{1,0:T(8,128)(2,1)S(1)}, u32[]{:S(2)}, u32[]{:S(2)}) %collective-permute-start.8) | collective-permute-done | bytes 245792 | tf_op jit(solution)/shard_map/projection/ppermute | solution.py:40
  44.0 1.7 logits.4
  45.7 0.7 collective-permute-start.10
  46.5 4.2 %collective-permute-start.9 = (f32[96,2048]{1,0:T(8,128)S(1)}, f32[96,2048]{1,0:T(8,128)}, u32[]{:S(2)}, u32[]{:S(2)}) collective-permute-start(f32[96,2048]{1,0:T(8,128)S(1)} %logits.4), channel_id=1, source_target_pairs={{0,2},{6,4},{1,3},{7,5},{8,10},{14,12},{9,11},{15,13},{16,18},{22,... | collective-permute-start | bytes 2359304 | tf_op jit(solution)/shard_map/logits/ppermute | solution.py:418
  50.6 1.8 collective-permute-start.13
  52.5 2.6 %collective-permute-start.11 = (f32[96]{0:T(128)S(1)}, f32[96]{0:T(128)S(1)}, u32[]{:S(2)}, u32[]{:S(2)}) collective-permute-start(f32[96]{0:T(128)S(1)} %get-tuple-element.104), channel_id=1, source_target_pairs={{0,2},{2,0},{4,6},{6,4},{1,3},{3,1},{5,7},{7,5},{8,10},{10,8},{12,... | collective-permute-start | bytes 1160 | tf_op jit(solution)/shard_map/logits/ppermute | solution.py:36
  55.1 5.6 %logits.5 = (f32[96,2048]{1,0:T(8,128)S(1)}, f32[96,2048]{1,0:T(8,128)S(1)}) custom-call(s32[1]{0:T(128)} %bitcast.places._, bf16[96,1280]{1,0:T(8,128)(2,1)S(1)} %multiply_convert_fusion.2.left, bf16[8192,1280]{1,0:T(8,128)(2,1)} %refs_2_.1), custom_call_target="tpu_custom_call" | custom-call | tf_op jit(solution)/shard_map/logits/pallas_call | solution.py:251
  60.7 6.1 %collective-permute-done.13 = f32[96]{0:T(128)S(1)} collective-permute-done((f32[96]{0:T(128)S(1)}, f32[96]{0:T(128)S(1)}, u32[]{:S(2)}, u32[]{:S(2)}) %collective-permute-start.13) | collective-permute-done | bytes 416 | tf_op jit(solution)/shard_map/logits/ppermute | solution.py:36
  67.1 1.6 collective-permute-start.17
  68.9 1.2 add.290
  70.2 1.2 collective-permute-start.14
  71.4 1.5 collective-permute-start.15
  73.2 3.5 %logits.7 = f32[96,2048]{1,0:T(8,128)S(1)} custom-call(s32[1]{0:T(128)} %bitcast.places._, bf16[96,1280]{1,0:T(8,128)(2,1)S(1)} %multiply_convert_fusion.2.left, bf16[8192,1280]{1,0:T(8,128)(2,1)} %refs_2_.1), custom_call_target="tpu_custom_call" | custom-call | tf_op jit(solution)/shard_map/logits/pallas_call | solution.py:251
  76.7 7.7 %logits.6 = f32[96,1280]{1,0:T(8,128)S(1)} custom-call(s32[1]{0:T(128)} %bitcast.places._, bf16[96,8192]{1,0:T(8,128)(2,1)S(1)} %fusion.refs_0_, bf16[8192,1280]{1,0:T(8,128)(2,1)} %refs_2_.1), custom_call_target="tpu_custom_call" | custom-call | tf_op jit(solution)/shard_map/logits/pallas_call | solution.py:251
  84.4 23.3 %collective-permute-done.14 = f32[96,2048]{1,0:T(8,128)S(1)} collective-permute-done((f32[96,2048]{1,0:T(8,128)S(1)}, f32[96,2048]{1,0:T(8,128)S(1)}, u32[]{:S(2)}, u32[]{:S(2)}) %collective-permute-start.14) | collective-permute-done | bytes 786464 | tf_op jit(solution)/shard_map/logits/ppermute | solution.py:36
  108.8 2.3 %collective-permute-start.19 = (bf16[96,2048]{1,0:T(8,128)(2,1)S(1)}, bf16[96,2048]{1,0:T(8,128)(2,1)}, u32[]{:S(2)}, u32[]{:S(2)}) collective-permute-start(bf16[96,2048]{1,0:T(8,128)(2,1)S(1)} %get-tuple-element.125.refs_0_), channel_id=1, source_target_pairs={{0,4},{2,6},{4,0},{6,2},{1,5},{3,7},{5,1},{7,3},{8,12},{10,14},{12... | collective-permute-start | bytes 1179656 | tf_op jit(solution)/shard_map/grad_normed/ppermute | solution.py:36
  111.1 7.9 %dynamic-slice_bitcast_fusion = (bf16[1280,1280]{1,0:T(8,128)(2,1)}, bf16[1280,1280]{1,0:T(8,128)(2,1)}, bf16[1280,1280]{1,0:T(8,128)(2,1)}) fusion(bf16[1,5120,1280]{2,1,0:T(8,128)(2,1)} %param.9, s32[]{:T(128)S(6)} %select_n.107, s32[]{:T(128)S(6)} %select_n.105, s32[]{:T(128)S(6)} %select_n.106), kind=kLoop, calls=%fused_computation | loop fusion | bytes 19660812 | tf_op jit(solution)/shard_map/grad_normed/dynamic_slice | solution.py:385
  120.9 2.9 %grad_normed.3 = f32[96,1280]{1,0:T(8,128)S(1)} custom-call(s32[1]{0:T(128)} %bitcast.places._, bf16[96,2048]{1,0:T(8,128)(2,1)S(1)} %get-tuple-element.125.refs_0_, bf16[8192,1280]{1,0:T(8,128)(2,1)} %refs_2_.1), custom_call_target="tpu_custom_call" | custom-call | tf_op jit(solution)/shard_map/grad_normed/pallas_call | solution.py:251
  123.8 3.6 %collective-permute-done.20.refs_0_ = bf16[96,2048]{1,0:T(8,128)(2,1)S(1)} collective-permute-done((bf16[96,2048]{1,0:T(8,128)(2,1)S(1)}, bf16[96,2048]{1,0:T(8,128)(2,1)S(1)}, u32[]{:S(2)}, u32[]{:S(2)}) %collective-permute-start.20) | collective-permute-done | bytes 393248 | tf_op jit(solution)/shard_map/grad_normed/ppermute | solution.py:36
  127.4 1.8 collective-permute-done.19.refs_1_
  129.2 0.6 stack.44
  129.8 2.0 collective-permute-start.24
  131.8 2.4 %collective-permute-start.22 = (f32[5,96]{1,0:T(8,128)}, f32[5,96]{1,0:T(8,128)}, u32[]{:S(2)}, u32[]{:S(2)}) collective-permute-start(f32[5,96]{1,0:T(8,128)} %stack.44), channel_id=1, source_target_pairs={{0,2},{2,0},{4,6},{6,4},{1,3},{3,1},{5,7},{7,5},{8,10},{10,8},{12,... | collective-permute-start | bytes 5768 | tf_op jit(solution)/shard_map/grad_normed/ppermute | solution.py:36
  134.8 1.5 reduce.4
  136.3 0.8 collective-permute-start.26
  137.1 1.6 collective-permute-start.25
  138.8 5.5 %grad_normed.4 = (f32[96,1280]{1,0:T(8,128)S(1)}, f32[96,1280]{1,0:T(8,128)S(1)}) custom-call(s32[1]{0:T(128)} %bitcast.places._, bf16[96,2048]{1,0:T(8,128)(2,1)S(1)} %collective-permute-done.20.refs_0_, bf16[96,2048]{1,0:T(8,128)(2,1)} %collective-permute-done.19.refs_1_, bf16[8192,1280]{1,0:T(8,128)(2,1)} %refs_2_.1), custom_call_target="tpu_custom_call" | custom-call | tf_op jit(solution)/shard_map/grad_normed/pallas_call | solution.py:251
  144.3 0.8 fusion.25
  145.1 0.9 fusion.34
  146.0 0.7 fusion.24
  147.3 1.0 grad_normed.5
  149.1 1.9 fusion.9
  151.3 1.1 dynamic-slice_bitcast_fusion.3
  152.4 2.4 %collective-permute-done.27 = bf16[96,1280]{1,0:T(8,128)(2,1)S(1)} collective-permute-done((bf16[96,1280]{1,0:T(8,128)(2,1)S(1)}, bf16[96,1280]{1,0:T(8,128)(2,1)S(1)}, u32[]{:S(2)}, u32[]{:S(2)}) %collective-permute-start.27) | collective-permute-done | bytes 245792 | tf_op jit(solution)/shard_map/grad_normed/ppermute | solution.py:40
  155.2 1.3 collective-permute-start.32
  157.2 3.9 %joined_grad.4 = (bf16[96,1408]{1,0:T(8,128)(2,1)}, bf16[96,1408]{1,0:T(8,128)(2,1)}, bf16[96,1408]{1,0:T(8,128)(2,1)}) custom-call(s32[1]{0:T(128)} %bitcast.places._, bf16[96,1280]{1,0:T(8,128)(2,1)S(1)} %get-tuple-element.168.left, bf16[1280,1280]{1,0:T(8,128)(2,1)S(1)} %copy-done.2, bf16[1280,1280]{1,0:T(8,128)(2,1)S(1)} %copy-done.3, ...), custom_call_target="tpu_custom_call" | custom-call | tf_op jit(solution)/shard_map/joined_grad/pallas_call | solution.py:61
  161.1 2.3 %collective-permute-start.28 = (bf16[96,1408]{1,0:T(8,128)(2,1)}, bf16[96,1408]{1,0:T(8,128)(2,1)}, u32[]{:S(2)}, u32[]{:S(2)}) collective-permute-start(bf16[96,1408]{1,0:T(8,128)(2,1)} %get-tuple-element.141), channel_id=1, source_target_pairs={{0,6},{2,4},{4,2},{6,0},{1,7},{3,5},{5,3},{7,1},{8,14},{10,12},{12... | collective-permute-start | bytes 811016 | tf_op jit(solution)/shard_map/joined_grad/ppermute | solution.py:36
  163.4 1.4 collective-permute-start.29
  164.8 0.7 collective-permute-start.30
  165.5 2.8 %joined_grad.5.side = f32[96,1280]{1,0:T(8,128)S(1)} custom-call(s32[1]{0:T(128)} %bitcast.places._, bf16[96,1280]{1,0:T(8,128)(2,1)S(1)} %get-tuple-element.168.left, bf16[5120,1280]{1,0:T(8,128)(2,1)} %bitcast.195), custom_call_target="tpu_custom_call" | custom-call | tf_op jit(solution)/shard_map/joined_grad/pallas_call | solution.py:251
  168.5 10.0 %joined_grad.6 = f32[5120,1280]{1,0:T(8,128)} custom-call(s32[1]{0:T(128)} %bitcast.places._, bf16[96,1280]{1,0:T(8,128)(2,1)S(1)} %get-tuple-element.88.own, bf16[3,96,1280]{2,1,0:T(8,128)(2,1)S(1)} %copy-done.7, bf16[96,1280]{1,0:T(8,128)(2,1)S(1)} %get-tuple-element.165.grad), custom_call_target="tpu_custom_call" | custom-call | tf_op jit(solution)/shard_map/joined_grad/pallas_call | solution.py:297
  178.6 6.6 %joined_grad.7 = f32[2048,1280]{1,0:T(8,128)} custom-call(bf16[96,2048]{1,0:T(8,128)(2,1)S(1)} %get-tuple-element.146.refs_0_, bf16[96,2048]{1,0:T(8,128)(2,1)S(1)} %collective-permute-done.31.refs_1_, bf16[96,2048]{1,0:T(8,128)(2,1)S(1)} %collective-permute-done.32.refs_2_, bf16[96,2048]{1,0:T(8,128)(2,1)} %collective-permute-done.33.refs_3_, ...), custom_call_target="tpu_custom_call" | custom-call | tf_op jit(solution)/shard_map/joined_grad/pallas_call | solution.py:329
  185.2 4.0 %collective-permute-done.29.refs_1_ = bf16[96,1408]{1,0:T(8,128)(2,1)} collective-permute-done((bf16[96,1408]{1,0:T(8,128)(2,1)}, bf16[96,1408]{1,0:T(8,128)(2,1)}, u32[]{:S(2)}, u32[]{:S(2)}) %collective-permute-start.29) | collective-permute-done | bytes 270368 | tf_op jit(solution)/shard_map/joined_grad/ppermute | solution.py:36
  189.2 1.4 input_grads.1
  190.7 1.5 collective-permute-done.34
  192.3 3.2 %collective-permute-start.35 = (bf16[48,1280]{1,0:T(8,128)(2,1)S(1)}, bf16[48,1280]{1,0:T(8,128)(2,1)S(1)}, u32[]{:S(2)}, u32[]{:S(2)}) collective-permute-start(bf16[48,1280]{1,0:T(8,128)(2,1)S(1)} %get-tuple-element.190), channel_id=1, source_target_pairs={{0,16},{8,24},{16,0},{24,8},{2,18},{10,26},{18,2},{26,10},{4,20},{... | collective-permute-start | bytes 368648 | tf_op jit(solution)/shard_map/input_grads/ppermute | solution.py:555
  195.6 4.1 %collective-permute-start.37 = (bf16[48,1280]{1,0:T(8,128)(2,1)S(1)}, bf16[48,1280]{1,0:T(8,128)(2,1)S(1)}, u32[]{:S(2)}, u32[]{:S(2)}) collective-permute-start(bf16[48,1280]{1,0:T(8,128)(2,1)S(1)} %get-tuple-element.192), channel_id=1, source_target_pairs={{0,17},{8,25},{16,1},{24,9},{2,19},{10,27},{18,3},{26,11},{4,21},{... | collective-permute-start | bytes 368648 | tf_op jit(solution)/shard_map/input_grads/ppermute | solution.py:558
  199.7 0.9 collective-permute-done.36
  200.6 1.5 collective-permute-done.37
  202.1 0.8 fusion.11
  (136 shorter events, 9.2 us)
Async XLA Ops:
  1.6 7.7 %collective-permute-start.3 = (bf16[48,1280]{1,0:T(8,128)(2,1)S(1)}, bf16[48,1280]{1,0:T(8,128)(2,1)S(1)}, u32[]{:S(2)}, u32[]{:S(2)}) collective-permute-start(bf16[48,1280]{1,0:T(8,128)(2,1)S(1)} %get-tuple-element.193), channel_id=1, source_target_pairs={{0,1},{1,0},{2,3},{3,2},{4,5},{5,4},{6,7},{7,6},{8,9},{9,8},{10,11... | collective-permute-start | bytes 368648 | tf_op jit(solution)/shard_map/inputs/ppermute | solution.py:40
  4.7 8.2 %collective-permute-start.2 = (bf16[48,1280]{1,0:T(8,128)(2,1)S(1)}, bf16[48,1280]{1,0:T(8,128)(2,1)S(1)}, u32[]{:S(2)}, u32[]{:S(2)}) collective-permute-start(bf16[48,1280]{1,0:T(8,128)(2,1)S(1)} %get-tuple-element.84.kept), channel_id=1, source_target_pairs={{0,6},{2,4},{4,2},{6,0},{1,7},{3,5},{5,3},{7,1},{8,14},{10,12},{12... | collective-permute-start | bytes 368648 | tf_op jit(solution)/shard_map/inputs/ppermute | solution.py:36
  8.3 10.1 %collective-permute-start.1 = (bf16[48,1280]{1,0:T(8,128)(2,1)S(1)}, bf16[48,1280]{1,0:T(8,128)(2,1)S(1)}, u32[]{:S(2)}, u32[]{:S(2)}) collective-permute-start(bf16[48,1280]{1,0:T(8,128)(2,1)S(1)} %get-tuple-element.84.kept), channel_id=1, source_target_pairs={{0,4},{2,6},{4,0},{6,2},{1,5},{3,7},{5,1},{7,3},{8,12},{10,14},{12... | collective-permute-start | bytes 368648 | tf_op jit(solution)/shard_map/inputs/ppermute | solution.py:36
  8.3 10.1 %collective-permute-start = (bf16[48,1280]{1,0:T(8,128)(2,1)S(1)}, bf16[48,1280]{1,0:T(8,128)(2,1)S(1)}, u32[]{:S(2)}, u32[]{:S(2)}) collective-permute-start(bf16[48,1280]{1,0:T(8,128)(2,1)S(1)} %get-tuple-element.84.kept), channel_id=1, source_target_pairs={{0,2},{2,0},{4,6},{6,4},{1,3},{3,1},{5,7},{7,5},{8,10},{10,8},{12,... | collective-permute-start | bytes 368648 | tf_op jit(solution)/shard_map/inputs/ppermute | solution.py:36
  9.0 16.2 %collective-permute-start.7 = (bf16[48,1280]{1,0:T(8,128)(2,1)}, bf16[48,1280]{1,0:T(8,128)(2,1)S(1)}, u32[]{:S(2)}, u32[]{:S(2)}) collective-permute-start(bf16[48,1280]{1,0:T(8,128)(2,1)} %param.7), channel_id=1, source_target_pairs={{0,1},{1,0},{2,3},{3,2},{4,5},{5,4},{6,7},{7,6},{8,9},{9,8},{10,11... | collective-permute-start | bytes 368648 | tf_op jit(solution)/shard_map/inputs/ppermute | solution.py:40
  18.4 8.1 %collective-permute-start.6 = (bf16[48,1280]{1,0:T(8,128)(2,1)S(1)}, bf16[48,1280]{1,0:T(8,128)(2,1)S(1)}, u32[]{:S(2)}, u32[]{:S(2)}) collective-permute-start(bf16[48,1280]{1,0:T(8,128)(2,1)S(1)} %collective-permute-done.3.given), channel_id=1, source_target_pairs={{0,6},{2,4},{4,2},{6,0},{1,7},{3,5},{5,3},{7,1},{8,14},{10,12},{12... | collective-permute-start | bytes 368648 | tf_op jit(solution)/shard_map/inputs/ppermute | solution.py:36
  21.1 9.5 %collective-permute-start.5 = (bf16[48,1280]{1,0:T(8,128)(2,1)S(1)}, bf16[48,1280]{1,0:T(8,128)(2,1)S(1)}, u32[]{:S(2)}, u32[]{:S(2)}) collective-permute-start(bf16[48,1280]{1,0:T(8,128)(2,1)S(1)} %collective-permute-done.3.given), channel_id=1, source_target_pairs={{0,4},{2,6},{4,0},{6,2},{1,5},{3,7},{5,1},{7,3},{8,12},{10,14},{12... | collective-permute-start | bytes 368648 | tf_op jit(solution)/shard_map/inputs/ppermute | solution.py:36
  21.1 9.5 %collective-permute-start.4 = (bf16[48,1280]{1,0:T(8,128)(2,1)S(1)}, bf16[48,1280]{1,0:T(8,128)(2,1)S(1)}, u32[]{:S(2)}, u32[]{:S(2)}) collective-permute-start(bf16[48,1280]{1,0:T(8,128)(2,1)S(1)} %collective-permute-done.3.given), channel_id=1, source_target_pairs={{0,2},{2,0},{4,6},{6,4},{1,3},{3,1},{5,7},{7,5},{8,10},{10,8},{12,... | collective-permute-start | bytes 368648 | tf_op jit(solution)/shard_map/inputs/ppermute | solution.py:36
  36.5 7.3 %copy-start.18 = (bf16[48,1280]{1,0:T(8,128)(2,1)S(1)}, bf16[48,1280]{1,0:T(8,128)(2,1)}, u32[]{:S(2)}) copy-start(bf16[48,1280]{1,0:T(8,128)(2,1)} %param.7) | copy-start | bytes 368644
  36.5 7.5 %copy-start.19 = (f32[1280]{0:T(1024)S(1)}, f32[1280]{0:T(1024)}, u32[]{:S(2)}) copy-start(f32[1280]{0:T(1024)} %param.10) | copy-start | bytes 15364
  36.5 7.3 %collective-permute-start.8 = (bf16[96,1280]{1,0:T(8,128)(2,1)S(1)}, bf16[96,1280]{1,0:T(8,128)(2,1)S(1)}, u32[]{:S(2)}, u32[]{:S(2)}) collective-permute-start(bf16[96,1280]{1,0:T(8,128)(2,1)S(1)} %get-tuple-element.99), channel_id=1, source_target_pairs={{0,1},{1,0},{2,3},{3,2},{4,5},{5,4},{6,7},{7,6},{8,9},{9,8},{10,11... | collective-permute-start | bytes 737288 | tf_op jit(solution)/shard_map/projection/ppermute | solution.py:40
  39.8 5.9 %copy-start = (bf16[2048,1280]{1,0:T(8,128)(2,1)}, bf16[2048,1280]{1,0:T(8,128)(2,1)S(1)}, u32[]{:S(2)}) copy-start(bf16[2048,1280]{1,0:T(8,128)(2,1)S(1)} %constant_dynamic-slice_fusion.refs_0_.right) | copy-start | bytes 15728644
  44.0 22.9 %copy-start.16 = (f32[96,1280]{1,0:T(8,128)}, f32[96,1280]{1,0:T(8,128)S(1)}, u32[]{:S(2)}) copy-start(f32[96,1280]{1,0:T(8,128)S(1)} %get-tuple-element.180) | copy-start | bytes 1474564
  44.0 6.6 %copy-start.34 = (s32[1,96]{1,0:T(1,128)S(1)}, s32[1,96]{1,0:T(1,128)}, u32[]{:S(2)}) copy-start(s32[1,96]{1,0:T(1,128)} %param.12) | copy-start | bytes 1156
  45.7 21.1 %collective-permute-start.10 = (f32[96,2048]{1,0:T(8,128)S(1)}, f32[96,2048]{1,0:T(8,128)S(1)}, u32[]{:S(2)}, u32[]{:S(2)}) collective-permute-start(f32[96,2048]{1,0:T(8,128)S(1)} %logits.4), channel_id=1, source_target_pairs={{2,4},{4,2},{3,5},{5,3},{10,12},{12,10},{11,13},{13,11},{18,20},{2... | collective-permute-start | bytes 2359304 | tf_op jit(solution)/shard_map/logits/ppermute | solution.py:419
  46.5 20.4 %collective-permute-start.9 = (f32[96,2048]{1,0:T(8,128)S(1)}, f32[96,2048]{1,0:T(8,128)}, u32[]{:S(2)}, u32[]{:S(2)}) collective-permute-start(f32[96,2048]{1,0:T(8,128)S(1)} %logits.4), channel_id=1, source_target_pairs={{0,2},{6,4},{1,3},{7,5},{8,10},{14,12},{9,11},{15,13},{16,18},{22,... | collective-permute-start | bytes 2359304 | tf_op jit(solution)/shard_map/logits/ppermute | solution.py:418
  50.6 57.4 %copy-start.21 = (s32[2048]{0:T(1024)}, s32[2048]{0:T(1024)S(1)}, u32[]{:S(2)}) copy-start(s32[2048]{0:T(1024)S(1)} %iota_add_fusion.3) | copy-start | bytes 24580
  50.6 57.4 %copy-start.28 = (s32[96,1]{0,1:T(1,128)}, s32[96,1]{0,1:T(1,128)S(1)}, u32[]{:S(2)}) copy-start(s32[96,1]{0,1:T(1,128)S(1)} %subtract_bitcast_fusion) | copy-start | bytes 1156
  50.6 16.2 %collective-permute-start.13 = (f32[96]{0:T(128)S(1)}, f32[96]{0:T(128)S(1)}, u32[]{:S(2)}, u32[]{:S(2)}) collective-permute-start(f32[96]{0:T(128)S(1)} %get-tuple-element.104), channel_id=1, source_target_pairs={{0,6},{2,4},{4,2},{6,0},{1,7},{3,5},{5,3},{7,1},{8,14},{10,12},{12... | collective-permute-start | bytes 1160 | tf_op jit(solution)/shard_map/logits/ppermute | solution.py:36
  52.5 14.4 %collective-permute-start.12 = (f32[96]{0:T(128)S(1)}, f32[96]{0:T(128)S(1)}, u32[]{:S(2)}, u32[]{:S(2)}) collective-permute-start(f32[96]{0:T(128)S(1)} %get-tuple-element.104), channel_id=1, source_target_pairs={{0,4},{2,6},{4,0},{6,2},{1,5},{3,7},{5,1},{7,3},{8,12},{10,14},{12... | collective-permute-start | bytes 1160 | tf_op jit(solution)/shard_map/logits/ppermute | solution.py:36
  52.5 14.4 %collective-permute-start.11 = (f32[96]{0:T(128)S(1)}, f32[96]{0:T(128)S(1)}, u32[]{:S(2)}, u32[]{:S(2)}) collective-permute-start(f32[96]{0:T(128)S(1)} %get-tuple-element.104), channel_id=1, source_target_pairs={{0,2},{2,0},{4,6},{6,4},{1,3},{3,1},{5,7},{7,5},{8,10},{10,8},{12,... | collective-permute-start | bytes 1160 | tf_op jit(solution)/shard_map/logits/ppermute | solution.py:36
  66.9 40.8 %copy-start.26 = (f32[96]{0:T(128)}, f32[96]{0:T(128)S(1)}, u32[]{:S(2)}) copy-start(f32[96]{0:T(128)S(1)} %add_rsqrt_fusion) | copy-start | bytes 1156
  67.0 9.7 %copy-start.4 = (bf16[96,1280]{1,0:T(8,128)(2,1)}, bf16[96,1280]{1,0:T(8,128)(2,1)S(1)}, u32[]{:S(2)}) copy-start(bf16[96,1280]{1,0:T(8,128)(2,1)S(1)} %multiply_convert_fusion.1.refs_4_) | copy-start | bytes 737284
  67.0 17.3 %collective-permute-start.18 = (bf16[96,1280]{1,0:T(8,128)(2,1)S(1)}, bf16[96,1280]{1,0:T(8,128)(2,1)S(1)}, u32[]{:S(2)}, u32[]{:S(2)}) collective-permute-start(bf16[96,1280]{1,0:T(8,128)(2,1)S(1)} %multiply_convert_fusion.1.refs_4_), channel_id=1, source_target_pairs={{0,24},{8,16},{16,8},{24,0},{1,25},{9,17},{17,9},{25,1},{2,26},{10... | collective-permute-start | bytes 737288 | tf_op jit(solution)/shard_map/logits/ppermute | solution.py:36
  67.1 17.3 %collective-permute-start.17 = (bf16[96,1280]{1,0:T(8,128)(2,1)S(1)}, bf16[96,1280]{1,0:T(8,128)(2,1)S(1)}, u32[]{:S(2)}, u32[]{:S(2)}) collective-permute-start(bf16[96,1280]{1,0:T(8,128)(2,1)S(1)} %multiply_convert_fusion.1.refs_4_), channel_id=1, source_target_pairs={{0,16},{8,24},{16,0},{24,8},{1,17},{9,25},{17,1},{25,9},{2,18},{10... | collective-permute-start | bytes 737288 | tf_op jit(solution)/shard_map/logits/ppermute | solution.py:36
  68.6 15.7 %collective-permute-start.16 = (bf16[96,1280]{1,0:T(8,128)(2,1)S(1)}, bf16[96,1280]{1,0:T(8,128)(2,1)S(1)}, u32[]{:S(2)}, u32[]{:S(2)}) collective-permute-start(bf16[96,1280]{1,0:T(8,128)(2,1)S(1)} %multiply_convert_fusion.1.refs_4_), channel_id=1, source_target_pairs={{0,8},{8,0},{16,24},{24,16},{1,9},{9,1},{17,25},{25,17},{2,10},{10... | collective-permute-start | bytes 737288 | tf_op jit(solution)/shard_map/logits/ppermute | solution.py:36
  70.2 37.5 %collective-permute-start.14 = (f32[96,2048]{1,0:T(8,128)S(1)}, f32[96,2048]{1,0:T(8,128)S(1)}, u32[]{:S(2)}, u32[]{:S(2)}) collective-permute-start(f32[96,2048]{1,0:T(8,128)S(1)} %add.290), channel_id=1, source_target_pairs={{0,4},{2,6},{4,0},{6,2},{1,5},{3,7},{5,1},{7,3},{8,12},{10,14},{12... | collective-permute-start | bytes 2359304 | tf_op jit(solution)/shard_map/logits/ppermute | solution.py:36
  71.4 36.3 %collective-permute-start.15 = (f32[96,2048]{1,0:T(8,128)S(1)}, f32[96,2048]{1,0:T(8,128)S(1)}, u32[]{:S(2)}, u32[]{:S(2)}) collective-permute-start(f32[96,2048]{1,0:T(8,128)S(1)} %get-tuple-element.110), channel_id=1, source_target_pairs={{0,2},{2,0},{4,6},{6,4},{1,3},{3,1},{5,7},{7,5},{8,10},{10,8},{12,... | collective-permute-start | bytes 2359304 | tf_op jit(solution)/shard_map/logits/ppermute | solution.py:36
  84.3 34.7 %copy-start.8 = (bf16[96,1280]{1,0:T(8,128)(2,1)}, bf16[96,1280]{1,0:T(8,128)(2,1)S(1)}, u32[]{:S(2)}) copy-start(bf16[96,1280]{1,0:T(8,128)(2,1)S(1)} %collective-permute-done.18.refs_7_) | copy-start | bytes 737284
  84.4 34.7 %copy-start.10 = (bf16[96,1280]{1,0:T(8,128)(2,1)}, bf16[96,1280]{1,0:T(8,128)(2,1)S(1)}, u32[]{:S(2)}) copy-start(bf16[96,1280]{1,0:T(8,128)(2,1)S(1)} %collective-permute-done.17.refs_6_) | copy-start | bytes 737284
  84.4 23.6 %copy-start.12 = (bf16[96,1280]{1,0:T(8,128)(2,1)}, bf16[96,1280]{1,0:T(8,128)(2,1)S(1)}, u32[]{:S(2)}) copy-start(bf16[96,1280]{1,0:T(8,128)(2,1)S(1)} %collective-permute-done.16.refs_5_) | copy-start | bytes 737284
  108.5 18.9 %collective-permute-start.20 = (bf16[96,2048]{1,0:T(8,128)(2,1)S(1)}, bf16[96,2048]{1,0:T(8,128)(2,1)S(1)}, u32[]{:S(2)}, u32[]{:S(2)}) collective-permute-start(bf16[96,2048]{1,0:T(8,128)(2,1)S(1)} %get-tuple-element.125.refs_0_), channel_id=1, source_target_pairs={{0,2},{2,0},{4,6},{6,4},{1,3},{3,1},{5,7},{7,5},{8,10},{10,8},{12,... | collective-permute-start | bytes 1179656 | tf_op jit(solution)/shard_map/grad_normed/ppermute | solution.py:36
  108.8 20.4 %collective-permute-start.19 = (bf16[96,2048]{1,0:T(8,128)(2,1)S(1)}, bf16[96,2048]{1,0:T(8,128)(2,1)}, u32[]{:S(2)}, u32[]{:S(2)}) collective-permute-start(bf16[96,2048]{1,0:T(8,128)(2,1)S(1)} %get-tuple-element.125.refs_0_), channel_id=1, source_target_pairs={{0,4},{2,6},{4,0},{6,2},{1,5},{3,7},{5,1},{7,3},{8,12},{10,14},{12... | collective-permute-start | bytes 1179656 | tf_op jit(solution)/shard_map/grad_normed/ppermute | solution.py:36
  119.7 4.1 %collective-permute-start.21 = (f32[4,96]{1,0:T(4,128)S(1)}, f32[4,96]{1,0:T(4,128)S(1)}, u32[]{:S(2)}, u32[]{:S(2)}) collective-permute-start(f32[4,96]{1,0:T(4,128)S(1)} %pad_maximum_fusion.1), channel_id=1, source_target_pairs={{0,1},{1,0},{2,3},{3,2},{4,5},{5,4},{6,7},{7,6},{8,9},{9,8},{10,11... | collective-permute-start | bytes 4616 | tf_op jit(solution)/shard_map/grad_normed/ppermute | solution.py:40
  129.8 9.0 %collective-permute-start.24 = (f32[5,96]{1,0:T(8,128)}, f32[5,96]{1,0:T(8,128)}, u32[]{:S(2)}, u32[]{:S(2)}) collective-permute-start(f32[5,96]{1,0:T(8,128)} %stack.44), channel_id=1, source_target_pairs={{0,6},{2,4},{4,2},{6,0},{1,7},{3,5},{5,3},{7,1},{8,14},{10,12},{12... | collective-permute-start | bytes 5768 | tf_op jit(solution)/shard_map/grad_normed/ppermute | solution.py:36
  131.8 7.0 %collective-permute-start.23 = (f32[5,96]{1,0:T(8,128)}, f32[5,96]{1,0:T(8,128)}, u32[]{:S(2)}, u32[]{:S(2)}) collective-permute-start(f32[5,96]{1,0:T(8,128)} %stack.44), channel_id=1, source_target_pairs={{0,4},{2,6},{4,0},{6,2},{1,5},{3,7},{5,1},{7,3},{8,12},{10,14},{12... | collective-permute-start | bytes 5768 | tf_op jit(solution)/shard_map/grad_normed/ppermute | solution.py:36
  131.8 7.0 %collective-permute-start.22 = (f32[5,96]{1,0:T(8,128)}, f32[5,96]{1,0:T(8,128)}, u32[]{:S(2)}, u32[]{:S(2)}) collective-permute-start(f32[5,96]{1,0:T(8,128)} %stack.44), channel_id=1, source_target_pairs={{0,2},{2,0},{4,6},{6,4},{1,3},{3,1},{5,7},{7,5},{8,10},{10,8},{12,... | collective-permute-start | bytes 5768 | tf_op jit(solution)/shard_map/grad_normed/ppermute | solution.py:36
  134.8 12.4 %slice-start = ((s8[5242880]{0:T(1024)(128)(4,1)}), s8[1048576]{0:T(1024)(128)(4,1)S(1)}, s32[]{:S(2)}) async-start(s8[5242880]{0:T(1024)(128)(4,1)} %bitcast.191), calls=%async_computation | async-start | bytes 2097152
  136.3 8.8 %copy-start.31 = (f32[1,96]{1,0:T(1,128)S(1)}, f32[1,96]{1,0:T(1,128)}, u32[]{:S(2)}) copy-start(f32[1,96]{1,0:T(1,128)} %param.13) | copy-start | bytes 1156
  136.3 10.9 %slice-start.1 = ((s8[5242880]{0:T(1024)(128)(4,1)}), s8[4194304]{0:T(1024)(128)(4,1)S(1)}, s32[]{:S(2)}) async-start(s8[5242880]{0:T(1024)(128)(4,1)} %bitcast.191), calls=%async_computation.1 | async-start | bytes 8388608
  136.3 10.4 %collective-permute-start.26 = (bf16[96,2048]{1,0:T(8,128)(2,1)S(1)}, bf16[96,2048]{1,0:T(8,128)(2,1)S(1)}, u32[]{:S(2)}, u32[]{:S(2)}) collective-permute-start(bf16[96,2048]{1,0:T(8,128)(2,1)S(1)} %get-tuple-element.125.refs_0_), channel_id=1, source_target_pairs={{2,4},{4,2},{3,5},{5,3},{10,12},{12,10},{11,13},{13,11},{18,20},{2... | collective-permute-start | bytes 1179656 | tf_op jit(solution)/shard_map/grad_normed/ppermute | solution.py:466
  137.1 10.1 %collective-permute-start.25 = (bf16[96,2048]{1,0:T(8,128)(2,1)}, bf16[96,2048]{1,0:T(8,128)(2,1)S(1)}, u32[]{:S(2)}, u32[]{:S(2)}) collective-permute-start(bf16[96,2048]{1,0:T(8,128)(2,1)} %collective-permute-done.19.refs_1_), channel_id=1, source_target_pairs={{4,6},{2,0},{5,7},{3,1},{12,14},{10,8},{13,15},{11,9},{20,22},{18,... | collective-permute-start | bytes 1179656 | tf_op jit(solution)/shard_map/grad_normed/ppermute | solution.py:465
  148.5 6.3 %collective-permute-start.27 = (bf16[96,1280]{1,0:T(8,128)(2,1)S(1)}, bf16[96,1280]{1,0:T(8,128)(2,1)S(1)}, u32[]{:S(2)}, u32[]{:S(2)}) collective-permute-start(bf16[96,1280]{1,0:T(8,128)(2,1)S(1)} %get-tuple-element.172), channel_id=1, source_target_pairs={{0,1},{1,0},{2,3},{3,2},{4,5},{5,4},{6,7},{7,6},{8,9},{9,8},{10,11... | collective-permute-start | bytes 737288 | tf_op jit(solution)/shard_map/grad_normed/ppermute | solution.py:40
  149.1 8.1 %copy-start.3 = (bf16[1280,1280]{1,0:T(8,128)(2,1)S(1)}, bf16[1280,1280]{1,0:T(8,128)(2,1)}, u32[]{:S(2)}) copy-start(bf16[1280,1280]{1,0:T(8,128)(2,1)} %get-tuple-element.139.refs_1_) | copy-start | bytes 9830404
  151.1 3.7 %copy-start.17 = (f32[96,1280]{1,0:T(8,128)S(1)}, f32[96,1280]{1,0:T(8,128)}, u32[]{:S(2)}) copy-start(f32[96,1280]{1,0:T(8,128)} %copy-done.16) | copy-start | bytes 1474564
  151.1 6.1 %copy-start.2 = (bf16[1280,1280]{1,0:T(8,128)(2,1)S(1)}, bf16[1280,1280]{1,0:T(8,128)(2,1)}, u32[]{:S(2)}) copy-start(bf16[1280,1280]{1,0:T(8,128)(2,1)} %get-tuple-element.138.refs_0_) | copy-start | bytes 9830404
  151.3 5.8 %copy-start.32 = (pred[128]{0:T(512)(128)(4,1)S(1)}, pred[128]{0:T(512)(128)(4,1)}, u32[]{:S(2)}) copy-start(pred[128]{0:T(512)(128)(4,1)} %get-tuple-element.213) | copy-start | bytes 388
  151.3 5.8 %copy-start.33 = (pred[128]{0:T(512)(128)(4,1)S(1)}, pred[128]{0:T(512)(128)(4,1)}, u32[]{:S(2)}) copy-start(pred[128]{0:T(512)(128)(4,1)} %get-tuple-element.214) | copy-start | bytes 388
  151.3 5.9 %copy-start.1 = (bf16[1280,1280]{1,0:T(8,128)(2,1)S(1)}, bf16[1280,1280]{1,0:T(8,128)(2,1)}, u32[]{:S(2)}) copy-start(bf16[1280,1280]{1,0:T(8,128)(2,1)} %get-tuple-element.140.refs_2_) | copy-start | bytes 9830404
  155.2 9.6 %collective-permute-start.31 = (bf16[96,2048]{1,0:T(8,128)(2,1)S(1)}, bf16[96,2048]{1,0:T(8,128)(2,1)S(1)}, u32[]{:S(2)}, u32[]{:S(2)}) collective-permute-start(bf16[96,2048]{1,0:T(8,128)(2,1)S(1)} %get-tuple-element.147), channel_id=1, source_target_pairs={{0,8},{8,0},{16,24},{24,16},{1,9},{9,1},{17,25},{25,17},{2,10},{10... | collective-permute-start | bytes 1179656 | tf_op jit(solution)/shard_map/joined_grad/ppermute | solution.py:36
  155.2 23.3 %collective-permute-start.32 = (bf16[96,2048]{1,0:T(8,128)(2,1)}, bf16[96,2048]{1,0:T(8,128)(2,1)S(1)}, u32[]{:S(2)}, u32[]{:S(2)}) collective-permute-start(bf16[96,2048]{1,0:T(8,128)(2,1)} %get-tuple-element.148), channel_id=1, source_target_pairs={{0,16},{8,24},{16,0},{24,8},{1,17},{9,25},{17,1},{25,9},{2,18},{10... | collective-permute-start | bytes 1179656 | tf_op jit(solution)/shard_map/joined_grad/ppermute | solution.py:36
  156.5 22.0 %collective-permute-start.33 = (bf16[96,2048]{1,0:T(8,128)(2,1)}, bf16[96,2048]{1,0:T(8,128)(2,1)}, u32[]{:S(2)}, u32[]{:S(2)}) collective-permute-start(bf16[96,2048]{1,0:T(8,128)(2,1)} %get-tuple-element.149), channel_id=1, source_target_pairs={{0,24},{8,16},{16,8},{24,0},{1,25},{9,17},{17,9},{25,1},{2,26},{10... | collective-permute-start | bytes 1179656 | tf_op jit(solution)/shard_map/joined_grad/ppermute | solution.py:36
  161.1 24.1 %collective-permute-start.28 = (bf16[96,1408]{1,0:T(8,128)(2,1)}, bf16[96,1408]{1,0:T(8,128)(2,1)}, u32[]{:S(2)}, u32[]{:S(2)}) collective-permute-start(bf16[96,1408]{1,0:T(8,128)(2,1)} %get-tuple-element.141), channel_id=1, source_target_pairs={{0,6},{2,4},{4,2},{6,0},{1,7},{3,5},{5,3},{7,1},{8,14},{10,12},{12... | collective-permute-start | bytes 811016 | tf_op jit(solution)/shard_map/joined_grad/ppermute | solution.py:36
  163.4 25.8 %collective-permute-start.29 = (bf16[96,1408]{1,0:T(8,128)(2,1)}, bf16[96,1408]{1,0:T(8,128)(2,1)}, u32[]{:S(2)}, u32[]{:S(2)}) collective-permute-start(bf16[96,1408]{1,0:T(8,128)(2,1)} %get-tuple-element.142), channel_id=1, source_target_pairs={{0,4},{2,6},{4,0},{6,2},{1,5},{3,7},{5,1},{7,3},{8,12},{10,14},{12... | collective-permute-start | bytes 811016 | tf_op jit(solution)/shard_map/joined_grad/ppermute | solution.py:36
  164.8 24.4 %collective-permute-start.30 = (bf16[96,1408]{1,0:T(8,128)(2,1)}, bf16[96,1408]{1,0:T(8,128)(2,1)}, u32[]{:S(2)}, u32[]{:S(2)}) collective-permute-start(bf16[96,1408]{1,0:T(8,128)(2,1)} %get-tuple-element.143), channel_id=1, source_target_pairs={{0,2},{2,0},{4,6},{6,4},{1,3},{3,1},{5,7},{7,5},{8,10},{10,8},{12,... | collective-permute-start | bytes 811016 | tf_op jit(solution)/shard_map/joined_grad/ppermute | solution.py:36
  168.5 10.0 %copy-start.5 = (bf16[96,1280]{1,0:T(8,128)(2,1)S(1)}, bf16[96,1280]{1,0:T(8,128)(2,1)}, u32[]{:S(2)}) copy-start(bf16[96,1280]{1,0:T(8,128)(2,1)} %copy-done.4) | copy-start | bytes 737284
  168.5 10.0 %copy-start.9 = (bf16[96,1280]{1,0:T(8,128)(2,1)S(1)}, bf16[96,1280]{1,0:T(8,128)(2,1)}, u32[]{:S(2)}) copy-start(bf16[96,1280]{1,0:T(8,128)(2,1)} %copy-done.8) | copy-start | bytes 737284
  168.5 10.0 %copy-start.11 = (bf16[96,1280]{1,0:T(8,128)(2,1)S(1)}, bf16[96,1280]{1,0:T(8,128)(2,1)}, u32[]{:S(2)}) copy-start(bf16[96,1280]{1,0:T(8,128)(2,1)} %copy-done.10) | copy-start | bytes 737284
  168.5 10.0 %copy-start.13 = (bf16[96,1280]{1,0:T(8,128)(2,1)S(1)}, bf16[96,1280]{1,0:T(8,128)(2,1)}, u32[]{:S(2)}) copy-start(bf16[96,1280]{1,0:T(8,128)(2,1)} %copy-done.12) | copy-start | bytes 737284
  178.5 10.7 %copy-start.15 = (f32[96,1]{1,0:T(8,128)S(1)}, f32[96,1]{1,0:T(8,128)}, u32[]{:S(2)}) copy-start(f32[96,1]{1,0:T(8,128)} %copy-done.14) | copy-start | bytes 1156
  190.6 1.6 collective-permute-start.34
  192.3 7.4 %collective-permute-start.35 = (bf16[48,1280]{1,0:T(8,128)(2,1)S(1)}, bf16[48,1280]{1,0:T(8,128)(2,1)S(1)}, u32[]{:S(2)}, u32[]{:S(2)}) collective-permute-start(bf16[48,1280]{1,0:T(8,128)(2,1)S(1)} %get-tuple-element.190), channel_id=1, source_target_pairs={{0,16},{8,24},{16,0},{24,8},{2,18},{10,26},{18,2},{26,10},{4,20},{... | collective-permute-start | bytes 368648 | tf_op jit(solution)/shard_map/input_grads/ppermute | solution.py:555
  195.5 5.1 %collective-permute-start.36 = (bf16[48,1280]{1,0:T(8,128)(2,1)S(1)}, bf16[48,1280]{1,0:T(8,128)(2,1)S(1)}, u32[]{:S(2)}, u32[]{:S(2)}) collective-permute-start(bf16[48,1280]{1,0:T(8,128)(2,1)S(1)} %get-tuple-element.191), channel_id=1, source_target_pairs={{0,1},{1,0},{2,3},{3,2},{4,5},{5,4},{6,7},{7,6},{8,9},{9,8},{10,11... | collective-permute-start | bytes 368648 | tf_op jit(solution)/shard_map/input_grads/ppermute | solution.py:40
  195.6 6.5 %collective-permute-start.37 = (bf16[48,1280]{1,0:T(8,128)(2,1)S(1)}, bf16[48,1280]{1,0:T(8,128)(2,1)S(1)}, u32[]{:S(2)}, u32[]{:S(2)}) collective-permute-start(bf16[48,1280]{1,0:T(8,128)(2,1)S(1)} %get-tuple-element.192), channel_id=1, source_target_pairs={{0,17},{8,25},{16,1},{24,9},{2,19},{10,27},{18,3},{26,11},{4,21},{... | collective-permute-start | bytes 368648 | tf_op jit(solution)/shard_map/input_grads/ppermute | solution.py:558
  (11 other events, 25.8 us)

commit v4 on v3

--- a/solution.py
+++ b/solution.py
@@ -131,7 +131,10 @@
 def project_kernel(features, count, blocks, places, *refs):
     kept, given = refs[:count], refs[count : 2 * count]
     weight, raw, own_squares = refs[2 * count : 2 * count + 3]
-    parts, projected, low, scale, held, done = refs[2 * count + 3 :]
+    parts_out, projected, low, scale, parts, held, done, written = refs[2 * count + 3 :]
+    writes = [
+        pltpu.make_async_copy(parts.at[k], parts_out.at[k], written.at[k]) for k in range(count)
+    ]
     squares = own_squares[...]
     total = projected
     chunks = list(range(1, count + 1))
@@ -144,6 +147,7 @@
                 parts[k, rows] = value
 
             join_rows(places, kept[k], given[k], put)
+            writes[k].start()
             values = parts[k].astype(f32)
             squares = squares + jnp.sum(values * values, axis=1, keepdims=True)
         product = plain_dot(parts[k, :, j * block : (j + 1) * block], right)
@@ -151,6 +155,8 @@
     scale[...] = lax.rsqrt(squares / features + epsilon)
     projected[...] = total[...] * scale[...]
     low[...] = projected[...].astype(bf16)
+    for write in writes:
+        write.wait()
 
 
 def project(places, kept, given, weight, raw, squares, features, blocks):
@@ -160,7 +166,7 @@
     return pl.pallas_call(
         functools.partial(project_kernel, features, count, blocks),
         out_shape=[
-            shaped(count, rows, width, bf16),
+            pltpu.HBM((count, rows, width), bf16),
             shaped(rows, width, f32),
             shaped(rows, width, bf16),
             shaped(rows, 1, f32),
@@ -168,10 +174,12 @@
         in_specs=[in_smem]
         + [in_vmem] * (2 * count)
         + [pl.BlockSpec(memory_space=pl.ANY), in_vmem, in_vmem],
-        out_specs=[in_vmem] * 4,
+        out_specs=[pl.BlockSpec(memory_space=pl.ANY)] + [in_vmem] * 3,
         scratch_shapes=[
+            pltpu.VMEM((count, rows, width), bf16),
             pltpu.VMEM((count * blocks, width // blocks, width), weight.dtype),
             pltpu.SemaphoreType.DMA((count * blocks,)),
+            pltpu.SemaphoreType.DMA((count,)),
         ],
         compiler_params=params(kernel_memory),
         cost_estimate=brief,
@@ -336,6 +344,26 @@
         compiler_params=params(kernel_memory),
         cost_estimate=brief,
     )(*grads, *normed)
+
+
+def softmax_factors_kernel(_, here, there, weights, scale, out):
+    count = here.shape[0]
+    shards = [[r[n, k : k + 1, :] for k in range(4)] for r in (here, there) for n in range(count)]
+    largest = shards[0][0]
+    for shard in shards[1:]:
+        largest = jnp.maximum(largest, shard[0])
+    by = [jnp.exp(shard[0] - largest) for shard in shards]
+    summed = sum(shard[1] * b for shard, b in zip(shards, by))
+    hit_logit = sum(shard[2] for shard in shards)
+    weighted = sum(shard[3] * b for shard, b in zip(shards, by))
+    per_row = weights[...] / summed
+    hit_grad = weights[...] * (jnp.exp(hit_logit - largest) / summed - 1.0)
+    out[0:1, :] = hit_grad
+    out[1:2, :] = per_row * weighted + hit_grad * hit_logit
+    out[2:3, :] = hit_grad * scale[...]
+    for n in range(count):
+        out[4 + n : 5 + n, :] = per_row * by[n]
+        out[4 + count + n : 5 + count + n, :] = per_row * by[n] * scale[...]
 
 
 def input_grad_kernel(features, places, side, own, in_scale, grad_mixed, dots, *refs):
@@ -417,27 +445,30 @@
         (far,) = held_columns(places, low, [weight_far], f32)
         ends = lax.ppermute(far, "tensor", [(0, 1), (3, 2)])
         middle = lax.ppermute(far, "tensor", [(1, 2), (2, 1)])
-        mixed_squares = spread(jnp.sum(mixed * mixed, axis=1))
+        low_chips = [low, flip(low, "head", n_head, 2)]
         cross, near = stream_columns(places, low, unembed_weight, [2, 1], piece, 4, f32)
         wanted = (target_ids[0] - d * vocab_part)[:, None]
-        ends, middle, mixed_squares, cross, near, low, wanted = lax.optimization_barrier(
-            (ends, middle, mixed_squares, cross, near, low, wanted)
-        )
-        mixed_scale = lax.rsqrt(sum(mixed_squares) / features + epsilon)[:, None]
-        normed_out = (gained * mixed_scale).astype(bf16)
-        normed_heads = [normed_out] + [
-            flip(normed_out, "head", n_head, m) for m in range(1, n_head)
-        ]
+        squares = jnp.sum(mixed * mixed, axis=1)
+        squares = jnp.stack([squares, flip(squares, "tensor", n_tensor, 1)])
+        ends, middle, low_chips, cross, near, squares, wanted = lax.optimization_barrier(
+            (ends, middle, low_chips, cross, near, squares, wanted)
+        )
+        low_cores = flip(jnp.stack(low_chips), "head", n_head, 1)
+        squares_there = flip(squares, "tensor", n_tensor, 2)
         cross = flip(cross + ends, "tensor", n_tensor, 2)
         near = flip(near, "tensor", n_tensor, 1)
         chosen = lax.broadcasted_iota(jnp.int32, (1, vocab_part), 1) == wanted
         (target_rows,) = stream_rows(
             places, [chosen.astype(bf16)], unembed_weight, [None], 16, 8
         )
-        (last,) = stream_columns(places, low, unembed_weight, [0], piece, 4, f32)
-        cross, near, normed_heads, target_rows, last = lax.optimization_barrier(
-            (cross, near, normed_heads, target_rows, last)
-        )
+        (last,) = stream_columns(places, low_chips[0], unembed_weight, [0], piece, 4, f32)
+        cross, near, low_cores, squares_there, target_rows, last = lax.optimization_barrier(
+            (cross, near, low_cores, squares_there, target_rows, last)
+        )
+        low_heads = [low_chips[0], low_cores[0], low_chips[1], low_cores[1]]
+        squares = squares[0] + squares[1] + squares_there[0] + squares_there[1]
+        scale_row = lax.rsqrt(squares / features + epsilon)
+        mixed_scale = scale_row[:, None]
         logits = (last + middle + cross + near) * mixed_scale
     with jax.named_scope("softmax"):
         hits = (lax.broadcasted_iota(jnp.int32, (1, piece), 1) + t * piece) == wanted
@@ -455,31 +486,20 @@
     with jax.named_scope("grad_normed"):
         cross = flip(shifted_low, "tensor", n_tensor, 2)
         near = flip(shifted_low, "tensor", n_tensor, 1)
-        there = swap(stats)
         products = stream_rows(places, [shifted_low], unembed_weight, [0], 4, 4)
+        stats, products = lax.optimization_barrier((stats, products))
+        stats = spread(stats)
         weight_sent = [chunk_of(combine_whole, r, width) for r in (3, 2, 1)]
         weight_far = chunk_of(unembed_whole, 3, piece)
-        cross, near, there, products, value, weight_sent, weight_far = lax.optimization_barrier(
-            (cross, near, there, products, shifted_low, weight_sent, weight_far)
+        cross, near, stats, products, value, weight_sent, weight_far = lax.optimization_barrier(
+            (cross, near, stats, products, shifted_low, weight_sent, weight_far)
         )
         ends = lax.ppermute(cross, "tensor", [(2, 3), (1, 0)])
         middle = lax.ppermute(value, "tensor", [(1, 2), (2, 1)])
-        pair_top = jnp.maximum(top, there[0])
-        here_by, there_by = jnp.exp(top - pair_top), jnp.exp(there[0] - pair_top)
-        stats = spread(
-            jnp.stack(
-                [
-                    top,
-                    pair_top,
-                    stats[1] * here_by + there[1] * there_by,
-                    stats[2] + there[2],
-                    stats[3] * here_by + there[3] * there_by,
-                ]
-            )
-        )
-        stats, near, cross = lax.optimization_barrier((stats, near, cross))
+        stats = jnp.stack(stats)
+        there = swap(stats)
         products += stream_rows(places, [near, cross], unembed_weight, [1, 2], 4, 8)
-        ends, middle, products = lax.optimization_barrier((ends, middle, products))
+        ends, middle, there, products = lax.optimization_barrier((ends, middle, there, products))
         products += whole_call(
             held_between_kernel,
             places,
@@ -488,14 +508,15 @@
         )
         far = jnp.where((t == 0) | (t == n_tensor - 1), ends, middle)
         shifted_parts = [shifted_low, near, cross, far]
-        largest = jnp.max(jnp.stack([s[1] for s in stats]), axis=0)
-        by = [jnp.exp(s[1] - largest) for s in stats]
-        summed = sum(s[2] * b for s, b in zip(stats, by))
-        hit_logit = sum(s[3] for s in stats)
-        per_row = row_weights / summed
-        hit_grad = row_weights * (jnp.exp(hit_logit - largest) / summed - 1.0)
-        grad_dots = per_row * sum(s[4] * b for s, b in zip(stats, by)) + hit_grad * hit_logit
-        factors = [per_row * jnp.exp(s[0] - largest) for s in stats]
+        (row_factors,) = whole_call(
+            softmax_factors_kernel,
+            places,
+            [stats, there, row_weights[None, :], scale_row[None, :]],
+            [shaped(4 + 2 * n_tensor, rows, f32)],
+        )
+        hit_grad, grad_dots, hit_scaled = row_factors[0], row_factors[1], row_factors[2]
+        factors = [row_factors[4 + r] for r in range(n_tensor)]
+        factors_scaled = [row_factors[4 + n_tensor + r] for r in range(n_tensor)]
         grad_part = hit_grad[:, None] * target_rows
         for r, product in enumerate(products):
             grad_part = grad_part + factors[r][:, None] * product
@@ -505,8 +526,8 @@
             [
                 jnp.where(
                     (ids + (t ^ r) * piece) == wanted,
-                    hit_grad[:, None],
-                    e.astype(f32) * factors[r][:, None],
+                    hit_scaled[:, None],
+                    e.astype(f32) * factors_scaled[r][:, None],
                 ).astype(bf16)
                 for r, e in enumerate(shifted_parts)
             ]
@@ -531,12 +552,17 @@
             lane == 0, dots_high, jnp.where(lane == 1, dots - dots_high, 0.0)
         ).astype(bf16)
     with jax.named_scope("joined_grad"):
-        sent = held_columns(places, grad_low, weight_sent, bf16, extra)
+        heads_near = flip(grad_slices[1], "head", n_head, 1)
+        sent = held_columns(places, grad_low, weight_sent[:1], bf16, extra)
+        heads_near, grad_low = lax.optimization_barrier((heads_near, grad_low))
+        sent += held_columns(places, grad_low, weight_sent[1:], bf16, extra)
         came = [flip(c, "tensor", n_tensor, r) for r, c in zip((3, 2, 1), sent)]
-        heads_given = [flip(grad_slices[m], "head", n_head, m) for m in range(1, n_head)]
+        heads_given = [heads_near] + [
+            flip(grad_slices[m], "head", n_head, m) for m in range(2, n_head)
+        ]
         (side,) = stream_columns(places, grad_low, weight_block, [0], width, 2, f32)
         combine_grad = combine(places, own, parts, grad_scaled)[None]
-        unembed_grad = head_sum([grad_slices[0]] + heads_given, normed_heads, 2)
+        unembed_grad = head_sum([grad_slices[0]] + heads_given, low_heads, 2)
         unembed_grad = unembed_grad.reshape(1, 1, piece, width)
         came, side, combine_grad, unembed_grad = lax.optimization_barrier(
             (came, side, combine_grad, unembed_grad)

time: 204 us -> 194 us (0.951)
  other arithmetic: 13.2 us -> 7.67 us
  waiting for transfers between devices: 63.9 us -> 60 us
  Pallas kernels: 59.4 us -> 62.1 us
  starting transfers between devices: 50.9 us -> 48.7 us
    ppermute x26 -> x24, waiting for transfers between devices: 54.6 us -> 49.2 us  [flip(): return lax.ppermute(value, axis, [(i, i ^ mask) for i in range(size)])]
    ppermute x26 -> x24, starting transfers between devices: 31.2 us -> 29.2 us  [flip(): return lax.ppermute(value, axis, [(i, i ^ mask) for i in range(size)])]
    pallas_call x4 -> x6, Pallas kernels: 7.97 us -> 9.96 us  [whole_call(): pl.pallas_call(kernel, out_shape=outs, in_specs=[in_smem] + [in_vmem] * l...]
  transfers between devices with their start and end apart: 38 -> 36, of which waited for: 15 -> 15; matrix products, arithmetic and copies ran while one was open for 11% -> 8% of each run, Pallas kernels for 25% -> 27%
where the time goes in v4:
time: 194 us
  Pallas kernels  62.1 us (32%)
  waiting for transfers between devices  60 us (31%)
  starting transfers between devices  48.7 us (25%)
  local copies, waits for them, and re-layouts  13.8 us (7%)
  other arithmetic  7.67 us (4%)
    ppermute x24, waiting for transfers between devices, flip(): return lax.ppermute(value, axis, [(i, i ^ mask) for i in range(size)])  49.2 us
    ppermute x24, starting transfers between devices, flip(): return lax.ppermute(value, axis, [(i, i ^ mask) for i in range(size)])  29.2 us
    pallas_call x6, Pallas kernels, stream(): pl.pallas_call(functools.partial(kernel, chunks, blocks), out_shape=outs,...  28.4 us
    dynamic_slice x2, local copies, waits for them, and re-layouts, chunk_of(): return lax.dynamic_slice_in_dim(weight, (t ^ r) * size, size, 0)  10.7 us
    pallas_call x1, Pallas kernels, combine(): pl.pallas_call(combine_kernel, out_shape=shaped(count * width, grad.shape...  9.98 us
    pallas_call x6, Pallas kernels, whole_call(): pl.pallas_call(kernel, out_shape=outs, in_specs=[in_smem] + [in_vmem] * l...  9.96 us
    ppermute x6, waiting for transfers between devices, swap(): return lax.ppermute(value, 'dp', [(0, 1), (1, 0)])  7.74 us
    pallas_call x1, Pallas kernels, head_sum(): pl.pallas_call(head_sum_kernel, out_shape=shaped(size, width, f32), grid=...  6.72 us
  transfers between devices with their start and end apart: 36, of which 15 were waited for; matrix products, arithmetic and copies ran while one was open for 8% of the time, Pallas kernels for 27%

profile of v4, /device:TPU:0, one launch (start us, length us, event | category | flops | bytes accessed | tf_op | source)
XLA Modules:
  0.0 193.6 jit_solution(13017393540387275594)
XLA Ops:
  0.6 1.0 bitcast_select_fusion
  1.6 3.0 %collective-permute-start.3 = (bf16[48,1280]{1,0:T(8,128)(2,1)S(1)}, bf16[48,1280]{1,0:T(8,128)(2,1)S(1)}, u32[]{:S(2)}, u32[]{:S(2)}) collective-permute-start(bf16[48,1280]{1,0:T(8,128)(2,1)S(1)} %get-tuple-element.184), channel_id=1, source_target_pairs={{0,1},{1,0},{2,3},{3,2},{4,5},{5,4},{6,7},{7,6},{8,9},{9,8},{10,11... | collective-permute-start | bytes 368648 | tf_op jit(solution)/shard_map/inputs/ppermute | solution.py:40
  4.7 3.6 %collective-permute-start.2 = (bf16[48,1280]{1,0:T(8,128)(2,1)S(1)}, bf16[48,1280]{1,0:T(8,128)(2,1)S(1)}, u32[]{:S(2)}, u32[]{:S(2)}) collective-permute-start(bf16[48,1280]{1,0:T(8,128)(2,1)S(1)} %get-tuple-element.81.kept), channel_id=1, source_target_pairs={{0,6},{2,4},{4,2},{6,0},{1,7},{3,5},{5,3},{7,1},{8,14},{10,12},{12... | collective-permute-start | bytes 368648 | tf_op jit(solution)/shard_map/inputs/ppermute | solution.py:36
  8.3 0.8 collective-permute-start
  9.3 3.5 %collective-permute-done.2.refs_2_ = bf16[48,1280]{1,0:T(8,128)(2,1)S(1)} collective-permute-done((bf16[48,1280]{1,0:T(8,128)(2,1)S(1)}, bf16[48,1280]{1,0:T(8,128)(2,1)S(1)}, u32[]{:S(2)}, u32[]{:S(2)}) %collective-permute-start.2) | collective-permute-done | bytes 122912 | tf_op jit(solution)/shard_map/inputs/ppermute | solution.py:36
  12.8 5.5 %collective-permute-done.1.refs_1_ = bf16[48,1280]{1,0:T(8,128)(2,1)S(1)} collective-permute-done((bf16[48,1280]{1,0:T(8,128)(2,1)S(1)}, bf16[48,1280]{1,0:T(8,128)(2,1)S(1)}, u32[]{:S(2)}, u32[]{:S(2)}) %collective-permute-start.1) | collective-permute-done | bytes 122912 | tf_op jit(solution)/shard_map/inputs/ppermute | solution.py:36
  18.4 2.7 %collective-permute-start.6 = (bf16[48,1280]{1,0:T(8,128)(2,1)S(1)}, bf16[48,1280]{1,0:T(8,128)(2,1)S(1)}, u32[]{:S(2)}, u32[]{:S(2)}) collective-permute-start(bf16[48,1280]{1,0:T(8,128)(2,1)S(1)} %collective-permute-done.3.given), channel_id=1, source_target_pairs={{0,6},{2,4},{4,2},{6,0},{1,7},{3,5},{5,3},{7,1},{8,14},{10,12},{12... | collective-permute-start | bytes 368648 | tf_op jit(solution)/shard_map/inputs/ppermute | solution.py:36
  21.1 1.7 collective-permute-start.4
  22.7 2.5 %inputs.1 = (bf16[96,1280]{1,0:T(8,128)(2,1)S(1)}, f32[96,1280]{1,0:T(8,128)S(1)}, f32[96,1]{1,0:T(8,128)S(1)}) custom-call(s32[1]{0:T(128)} %bitcast.places._, bf16[48,1280]{1,0:T(8,128)(2,1)S(1)} %get-tuple-element.81.kept, bf16[48,1280]{1,0:T(8,128)(2,1)S(1)} %collective-permute-done.3.given, bf16[5120,1280]{1,0:T(8,128)(2,1)} %bitcast.80), custom_call_target="tpu_custom_call" | custom-call | tf_op jit(solution)/shard_map/inputs/pallas_call | solution.py:109
  25.2 1.2 collective-permute-done.6.refs_5_
  26.4 4.2 %collective-permute-done.5.refs_4_ = bf16[48,1280]{1,0:T(8,128)(2,1)S(1)} collective-permute-done((bf16[48,1280]{1,0:T(8,128)(2,1)S(1)}, bf16[48,1280]{1,0:T(8,128)(2,1)S(1)}, u32[]{:S(2)}, u32[]{:S(2)}) %collective-permute-start.5) | collective-permute-done | bytes 122912 | tf_op jit(solution)/shard_map/inputs/ppermute | solution.py:36
  30.6 4.6 %projection.1 = (bf16[3,96,1280]{2,1,0:T(8,128)(2,1)}, f32[96,1280]{1,0:T(8,128)S(1)}, bf16[96,1280]{1,0:T(8,128)(2,1)S(1)}, f32[96,1]{1,0:T(8,128)S(1)}) custom-call(s32[1]{0:T(128)} %bitcast.places._, bf16[48,1280]{1,0:T(8,128)(2,1)S(1)} %collective-permute-done.refs_0_, bf16[48,1280]{1,0:T(8,128)(2,1)S(1)} %collective-permute-done.1.refs_1_, ...), custom_call_target="tpu_custom_call" | custom-call | tf_op jit(solution)/shard_map/projection/pallas_call | solution.py:166
  35.2 0.6 collective-permute-start.8
  35.7 2.8 %constant_dynamic-slice_fusion.refs_0_.right = bf16[2048,1280]{1,0:T(8,128)(2,1)S(1)} fusion(bf16[8192,1280]{1,0:T(8,128)(2,1)} %refs_2_.1, s32[]{:T(128)S(6)} %select_n.102), kind=kLoop, calls=%fused_computation.56 | loop fusion | bytes 10485764 | tf_op jit(solution)/shard_map/projection/dynamic_slice | solution.py:413
  38.6 3.9 %collective-permute-done.8 = bf16[96,1280]{1,0:T(8,128)(2,1)S(1)} collective-permute-done((bf16[96,1280]{1,0:T(8,128)(2,1)S(1)}, bf16[96,1280]{1,0:T(8,128)(2,1)S(1)}, u32[]{:S(2)}, u32[]{:S(2)}) %collective-permute-start.8) | collective-permute-done | bytes 245792 | tf_op jit(solution)/shard_map/projection/ppermute | solution.py:40
  42.8 1.7 logits.4
  44.5 1.6 collective-permute-start.10
  46.1 2.6 %collective-permute-start.9 = (f32[96,2048]{1,0:T(8,128)S(1)}, f32[96,2048]{1,0:T(8,128)S(1)}, u32[]{:S(2)}, u32[]{:S(2)}) collective-permute-start(f32[96,2048]{1,0:T(8,128)S(1)} %logits.4), channel_id=1, source_target_pairs={{0,2},{6,4},{1,3},{7,5},{8,10},{14,12},{9,11},{15,13},{16,18},{22,... | collective-permute-start | bytes 2359304 | tf_op jit(solution)/shard_map/logits/ppermute | solution.py:446
  48.7 1.6 collective-permute-start.11
  50.4 5.6 %logits.5 = (f32[96,2048]{1,0:T(8,128)S(1)}, f32[96,2048]{1,0:T(8,128)S(1)}) custom-call(s32[1]{0:T(128)} %bitcast.places._, bf16[96,1280]{1,0:T(8,128)(2,1)S(1)} %multiply_convert_fusion.1.left.refs_4_, bf16[8192,1280]{1,0:T(8,128)(2,1)} %refs_2_.1), custom_call_target="tpu_custom_call" | custom-call | tf_op jit(solution)/shard_map/logits/pallas_call | solution.py:259
  56.0 7.4 %collective-permute-done.12 = f32[96]{0:T(128)S(1)} collective-permute-done((f32[96]{0:T(128)S(1)}, f32[96]{0:T(128)S(1)}, u32[]{:S(2)}, u32[]{:S(2)}) %collective-permute-start.12) | collective-permute-done | bytes 416 | tf_op jit(solution)/shard_map/logits/ppermute | solution.py:36
  63.4 2.9 %collective-permute-start.16 = (f32[2,96]{1,0:T(2,128)S(1)}, f32[2,96]{1,0:T(2,128)S(1)}, u32[]{:S(2)}, u32[]{:S(2)}) collective-permute-start(f32[2,96]{1,0:T(2,128)S(1)} %pad_maximum_fusion.4), channel_id=1, source_target_pairs={{0,4},{2,6},{4,0},{6,2},{1,5},{3,7},{5,1},{7,3},{8,12},{10,14},{12... | collective-permute-start | bytes 2312 | tf_op jit(solution)/shard_map/logits/ppermute | solution.py:36
  66.7 2.5 %collective-permute-start.14 = (f32[96,2048]{1,0:T(8,128)S(1)}, f32[96,2048]{1,0:T(8,128)S(1)}, u32[]{:S(2)}, u32[]{:S(2)}) collective-permute-start(f32[96,2048]{1,0:T(8,128)S(1)} %get-tuple-element.104), channel_id=1, source_target_pairs={{0,2},{2,0},{4,6},{6,4},{1,3},{3,1},{5,7},{7,5},{8,10},{10,8},{12,... | collective-permute-start | bytes 2359304 | tf_op jit(solution)/shard_map/logits/ppermute | solution.py:36
  69.2 0.3 fusion.refs_0_
  69.6 3.5 %logits.7 = f32[96,2048]{1,0:T(8,128)S(1)} custom-call(s32[1]{0:T(128)} %bitcast.places._, bf16[96,1280]{1,0:T(8,128)(2,1)S(1)} %multiply_convert_fusion.1.left.refs_4_, bf16[8192,1280]{1,0:T(8,128)(2,1)} %refs_2_.1), custom_call_target="tpu_custom_call" | custom-call | tf_op jit(solution)/shard_map/logits/pallas_call | solution.py:259
  73.1 7.7 %logits.6 = f32[96,1280]{1,0:T(8,128)S(1)} custom-call(s32[1]{0:T(128)} %bitcast.places._, bf16[96,8192]{1,0:T(8,128)(2,1)S(1)} %fusion.refs_0_, bf16[8192,1280]{1,0:T(8,128)(2,1)} %refs_2_.1), custom_call_target="tpu_custom_call" | custom-call | tf_op jit(solution)/shard_map/logits/pallas_call | solution.py:259
  80.8 23.1 %collective-permute-done.13 = f32[96,2048]{1,0:T(8,128)S(1)} collective-permute-done((f32[96,2048]{1,0:T(8,128)S(1)}, f32[96,2048]{1,0:T(8,128)S(1)}, u32[]{:S(2)}, u32[]{:S(2)}) %collective-permute-start.13) | collective-permute-done | bytes 786464 | tf_op jit(solution)/shard_map/logits/ppermute | solution.py:36
  104.0 1.5 fusion.16
  105.6 0.5 fusion.5
  106.1 2.4 %collective-permute-start.17 = (bf16[96,2048]{1,0:T(8,128)(2,1)S(1)}, bf16[96,2048]{1,0:T(8,128)(2,1)}, u32[]{:S(2)}, u32[]{:S(2)}) collective-permute-start(bf16[96,2048]{1,0:T(8,128)(2,1)S(1)} %get-tuple-element.120.refs_0_), channel_id=1, source_target_pairs={{0,4},{2,6},{4,0},{6,2},{1,5},{3,7},{5,1},{7,3},{8,12},{10,14},{12... | collective-permute-start | bytes 1179656 | tf_op jit(solution)/shard_map/grad_normed/ppermute | solution.py:36
  108.5 2.9 %grad_normed.4 = f32[96,1280]{1,0:T(8,128)S(1)} custom-call(s32[1]{0:T(128)} %bitcast.places._, bf16[96,2048]{1,0:T(8,128)(2,1)S(1)} %get-tuple-element.120.refs_0_, bf16[8192,1280]{1,0:T(8,128)(2,1)} %refs_2_.1), custom_call_target="tpu_custom_call" | custom-call | tf_op jit(solution)/shard_map/grad_normed/pallas_call | solution.py:259
  111.4 2.1 %collective-permute-start.21 = (f32[4,96]{1,0:T(4,128)S(1)}, f32[4,96]{1,0:T(4,128)S(1)}, u32[]{:S(2)}, u32[]{:S(2)}) collective-permute-start(f32[4,96]{1,0:T(4,128)S(1)} %pad_maximum_fusion.3), channel_id=1, source_target_pairs={{0,6},{2,4},{4,2},{6,0},{1,7},{3,5},{5,3},{7,1},{8,14},{10,12},{12... | collective-permute-start | bytes 4616 | tf_op jit(solution)/shard_map/grad_normed/ppermute | solution.py:36
  113.5 2.4 %collective-permute-start.19 = (f32[4,96]{1,0:T(4,128)S(1)}, f32[4,96]{1,0:T(4,128)S(1)}, u32[]{:S(2)}, u32[]{:S(2)}) collective-permute-start(f32[4,96]{1,0:T(4,128)S(1)} %pad_maximum_fusion.3), channel_id=1, source_target_pairs={{0,2},{2,0},{4,6},{6,4},{1,3},{3,1},{5,7},{7,5},{8,10},{10,8},{12,... | collective-permute-start | bytes 4616 | tf_op jit(solution)/shard_map/grad_normed/ppermute | solution.py:36
  115.9 7.9 %dynamic-slice_bitcast_fusion = (bf16[1280,1280]{1,0:T(8,128)(2,1)}, bf16[1280,1280]{1,0:T(8,128)(2,1)}, bf16[1280,1280]{1,0:T(8,128)(2,1)}) fusion(bf16[1,5120,1280]{2,1,0:T(8,128)(2,1)} %param.9, s32[]{:T(128)S(6)} %select_n.107, s32[]{:T(128)S(6)} %select_n.105, s32[]{:T(128)S(6)} %select_n.106), kind=kLoop, calls=%fused_computation | loop fusion | bytes 19660812 | tf_op jit(solution)/shard_map/grad_normed/dynamic_slice | solution.py:413
  123.8 1.9 collective-permute-done.21
  125.6 1.0 collective-permute-done.20
  126.7 0.8 copy-done.4
  127.4 1.4 collective-permute-start.23
  128.8 1.5 collective-permute-start.22
  130.4 0.6 collective-permute-start.24
  131.1 1.1 copy-done.5
  132.2 5.9 %grad_normed.5 = (f32[96,1280]{1,0:T(8,128)S(1)}, f32[96,1280]{1,0:T(8,128)S(1)}) custom-call(s32[1]{0:T(128)} %bitcast.places._, bf16[96,2048]{1,0:T(8,128)(2,1)S(1)} %copy-done.5, bf16[96,2048]{1,0:T(8,128)(2,1)} %collective-permute-done.17.refs_1_, bf16[8192,1280]{1,0:T(8,128)(2,1)} %refs_2_.1), custom_call_target="tpu_custom_call" | custom-call | tf_op jit(solution)/shard_map/grad_normed/pallas_call | solution.py:259
  138.1 1.9 %collective-permute-done.22.outer = bf16[96,2048]{1,0:T(8,128)(2,1)} collective-permute-done((bf16[96,2048]{1,0:T(8,128)(2,1)}, bf16[96,2048]{1,0:T(8,128)(2,1)}, u32[]{:S(2)}, u32[]{:S(2)}) %collective-permute-start.22) | collective-permute-done | bytes 393248 | tf_op jit(solution)/shard_map/grad_normed/ppermute | solution.py:497
  140.1 2.1 %grad_normed.7 = f32[96,1280]{1,0:T(8,128)S(1)} custom-call(s32[1]{0:T(128)} %bitcast.places._, bf16[96,2048]{1,0:T(8,128)(2,1)} %collective-permute-done.22.outer, bf16[96,2048]{1,0:T(8,128)(2,1)} %collective-permute-done.23.inner, bf16[2048,1280]{1,0:T(8,128)(2,1)S(1)} %bitcast.75), custom_call_target="tpu_custom_call" | custom-call | tf_op jit(solution)/shard_map/grad_normed/pallas_call | solution.py:61
  142.5 0.6 collective-permute-start.25
  143.1 1.9 fusion.9
  145.2 1.0 dynamic-slice_bitcast_fusion.3
  146.2 2.5 %collective-permute-done.25 = bf16[96,1280]{1,0:T(8,128)(2,1)S(1)} collective-permute-done((bf16[96,1280]{1,0:T(8,128)(2,1)S(1)}, bf16[96,1280]{1,0:T(8,128)(2,1)S(1)}, u32[]{:S(2)}, u32[]{:S(2)}) %collective-permute-start.25) | collective-permute-done | bytes 245792 | tf_op jit(solution)/shard_map/grad_normed/ppermute | solution.py:40
  149.3 1.9 joined_grad.5
  151.2 2.0 %collective-permute-start.26 = (bf16[96,1408]{1,0:T(8,128)(2,1)}, bf16[96,1408]{1,0:T(8,128)(2,1)}, u32[]{:S(2)}, u32[]{:S(2)}) collective-permute-start(bf16[96,1408]{1,0:T(8,128)(2,1)} %joined_grad.5), channel_id=1, source_target_pairs={{0,6},{2,4},{4,2},{6,0},{1,7},{3,5},{5,3},{7,1},{8,14},{10,12},{12... | collective-permute-start | bytes 811016 | tf_op jit(solution)/shard_map/joined_grad/ppermute | solution.py:36
  153.2 1.5 collective-permute-start.30
  154.8 2.8 %joined_grad.6 = (bf16[96,1408]{1,0:T(8,128)(2,1)}, bf16[96,1408]{1,0:T(8,128)(2,1)}) custom-call(s32[1]{0:T(128)} %bitcast.places._, bf16[96,1280]{1,0:T(8,128)(2,1)S(1)} %get-tuple-element.136.left, bf16[1280,1280]{1,0:T(8,128)(2,1)S(1)} %copy-done.2, bf16[1280,1280]{1,0:T(8,128)(2,1)S(1)} %copy-done.1, ...), custom_call_target="tpu_custom_call" | custom-call | tf_op jit(solution)/shard_map/joined_grad/pallas_call | solution.py:61
  157.6 0.7 collective-permute-start.28
  158.3 1.7 collective-permute-start.29
  160.2 10.0 %joined_grad.8 = f32[5120,1280]{1,0:T(8,128)} custom-call(s32[1]{0:T(128)} %bitcast.places._, bf16[96,1280]{1,0:T(8,128)(2,1)S(1)} %get-tuple-element.85.own, bf16[3,96,1280]{2,1,0:T(8,128)(2,1)S(1)} %copy-done.9, bf16[96,1280]{1,0:T(8,128)(2,1)S(1)} %get-tuple-element.159.grad), custom_call_target="tpu_custom_call" | custom-call | tf_op jit(solution)/shard_map/joined_grad/pallas_call | solution.py:305
  170.1 2.9 %joined_grad.7.side = f32[96,1280]{1,0:T(8,128)S(1)} custom-call(s32[1]{0:T(128)} %bitcast.places._, bf16[96,1280]{1,0:T(8,128)(2,1)S(1)} %get-tuple-element.136.left, bf16[5120,1280]{1,0:T(8,128)(2,1)} %bitcast.82), custom_call_target="tpu_custom_call" | custom-call | tf_op jit(solution)/shard_map/joined_grad/pallas_call | solution.py:259
  173.1 6.7 %joined_grad.9 = f32[2048,1280]{1,0:T(8,128)} custom-call(bf16[96,2048]{1,0:T(8,128)(2,1)S(1)} %get-tuple-element.143.refs_0_, bf16[96,2048]{1,0:T(8,128)(2,1)S(1)} %copy-done.11, bf16[96,2048]{1,0:T(8,128)(2,1)} %collective-permute-done.30.refs_2_, bf16[96,2048]{1,0:T(8,128)(2,1)} %collective-permute-done.31.refs_3_, ...), custom_call_target="tpu_custom_call" | custom-call | tf_op jit(solution)/shard_map/joined_grad/pallas_call | solution.py:337
  179.8 1.4 input_grads.1
  181.6 1.3 collective-permute-done.32
  182.9 3.4 %collective-permute-start.33 = (bf16[48,1280]{1,0:T(8,128)(2,1)S(1)}, bf16[48,1280]{1,0:T(8,128)(2,1)S(1)}, u32[]{:S(2)}, u32[]{:S(2)}) collective-permute-start(bf16[48,1280]{1,0:T(8,128)(2,1)S(1)} %get-tuple-element.181), channel_id=1, source_target_pairs={{0,16},{8,24},{16,0},{24,8},{2,18},{10,26},{18,2},{26,10},{4,20},{... | collective-permute-start | bytes 368648 | tf_op jit(solution)/shard_map/input_grads/ppermute | solution.py:581
  186.4 3.9 %collective-permute-start.35 = (bf16[48,1280]{1,0:T(8,128)(2,1)S(1)}, bf16[48,1280]{1,0:T(8,128)(2,1)S(1)}, u32[]{:S(2)}, u32[]{:S(2)}) collective-permute-start(bf16[48,1280]{1,0:T(8,128)(2,1)S(1)} %get-tuple-element.183), channel_id=1, source_target_pairs={{0,17},{8,25},{16,1},{24,9},{2,19},{10,27},{18,3},{26,11},{4,21},{... | collective-permute-start | bytes 368648 | tf_op jit(solution)/shard_map/input_grads/ppermute | solution.py:584
  190.3 1.3 collective-permute-done.34
  191.6 1.1 collective-permute-done.35
  192.7 0.8 fusion.11
  (104 shorter events, 3.3 us)
Async XLA Ops:
  1.6 7.7 %collective-permute-start.3 = (bf16[48,1280]{1,0:T(8,128)(2,1)S(1)}, bf16[48,1280]{1,0:T(8,128)(2,1)S(1)}, u32[]{:S(2)}, u32[]{:S(2)}) collective-permute-start(bf16[48,1280]{1,0:T(8,128)(2,1)S(1)} %get-tuple-element.184), channel_id=1, source_target_pairs={{0,1},{1,0},{2,3},{3,2},{4,5},{5,4},{6,7},{7,6},{8,9},{9,8},{10,11... | collective-permute-start | bytes 368648 | tf_op jit(solution)/shard_map/inputs/ppermute | solution.py:40
  4.7 8.2 %collective-permute-start.2 = (bf16[48,1280]{1,0:T(8,128)(2,1)S(1)}, bf16[48,1280]{1,0:T(8,128)(2,1)S(1)}, u32[]{:S(2)}, u32[]{:S(2)}) collective-permute-start(bf16[48,1280]{1,0:T(8,128)(2,1)S(1)} %get-tuple-element.81.kept), channel_id=1, source_target_pairs={{0,6},{2,4},{4,2},{6,0},{1,7},{3,5},{5,3},{7,1},{8,14},{10,12},{12... | collective-permute-start | bytes 368648 | tf_op jit(solution)/shard_map/inputs/ppermute | solution.py:36
  8.3 10.1 %collective-permute-start.1 = (bf16[48,1280]{1,0:T(8,128)(2,1)S(1)}, bf16[48,1280]{1,0:T(8,128)(2,1)S(1)}, u32[]{:S(2)}, u32[]{:S(2)}) collective-permute-start(bf16[48,1280]{1,0:T(8,128)(2,1)S(1)} %get-tuple-element.81.kept), channel_id=1, source_target_pairs={{0,4},{2,6},{4,0},{6,2},{1,5},{3,7},{5,1},{7,3},{8,12},{10,14},{12... | collective-permute-start | bytes 368648 | tf_op jit(solution)/shard_map/inputs/ppermute | solution.py:36
  8.3 10.1 %collective-permute-start = (bf16[48,1280]{1,0:T(8,128)(2,1)S(1)}, bf16[48,1280]{1,0:T(8,128)(2,1)S(1)}, u32[]{:S(2)}, u32[]{:S(2)}) collective-permute-start(bf16[48,1280]{1,0:T(8,128)(2,1)S(1)} %get-tuple-element.81.kept), channel_id=1, source_target_pairs={{0,2},{2,0},{4,6},{6,4},{1,3},{3,1},{5,7},{7,5},{8,10},{10,8},{12,... | collective-permute-start | bytes 368648 | tf_op jit(solution)/shard_map/inputs/ppermute | solution.py:36
  9.0 16.2 %collective-permute-start.7 = (bf16[48,1280]{1,0:T(8,128)(2,1)}, bf16[48,1280]{1,0:T(8,128)(2,1)S(1)}, u32[]{:S(2)}, u32[]{:S(2)}) collective-permute-start(bf16[48,1280]{1,0:T(8,128)(2,1)} %param.7), channel_id=1, source_target_pairs={{0,1},{1,0},{2,3},{3,2},{4,5},{5,4},{6,7},{7,6},{8,9},{9,8},{10,11... | collective-permute-start | bytes 368648 | tf_op jit(solution)/shard_map/inputs/ppermute | solution.py:40
  18.4 8.1 %collective-permute-start.6 = (bf16[48,1280]{1,0:T(8,128)(2,1)S(1)}, bf16[48,1280]{1,0:T(8,128)(2,1)S(1)}, u32[]{:S(2)}, u32[]{:S(2)}) collective-permute-start(bf16[48,1280]{1,0:T(8,128)(2,1)S(1)} %collective-permute-done.3.given), channel_id=1, source_target_pairs={{0,6},{2,4},{4,2},{6,0},{1,7},{3,5},{5,3},{7,1},{8,14},{10,12},{12... | collective-permute-start | bytes 368648 | tf_op jit(solution)/shard_map/inputs/ppermute | solution.py:36
  21.1 9.5 %collective-permute-start.5 = (bf16[48,1280]{1,0:T(8,128)(2,1)S(1)}, bf16[48,1280]{1,0:T(8,128)(2,1)S(1)}, u32[]{:S(2)}, u32[]{:S(2)}) collective-permute-start(bf16[48,1280]{1,0:T(8,128)(2,1)S(1)} %collective-permute-done.3.given), channel_id=1, source_target_pairs={{0,4},{2,6},{4,0},{6,2},{1,5},{3,7},{5,1},{7,3},{8,12},{10,14},{12... | collective-permute-start | bytes 368648 | tf_op jit(solution)/shard_map/inputs/ppermute | solution.py:36
  21.1 9.5 %collective-permute-start.4 = (bf16[48,1280]{1,0:T(8,128)(2,1)S(1)}, bf16[48,1280]{1,0:T(8,128)(2,1)S(1)}, u32[]{:S(2)}, u32[]{:S(2)}) collective-permute-start(bf16[48,1280]{1,0:T(8,128)(2,1)S(1)} %collective-permute-done.3.given), channel_id=1, source_target_pairs={{0,2},{2,0},{4,6},{6,4},{1,3},{3,1},{5,7},{7,5},{8,10},{10,8},{12,... | collective-permute-start | bytes 368648 | tf_op jit(solution)/shard_map/inputs/ppermute | solution.py:36
  35.1 7.4 %copy-start.17 = (bf16[48,1280]{1,0:T(8,128)(2,1)S(1)}, bf16[48,1280]{1,0:T(8,128)(2,1)}, u32[]{:S(2)}) copy-start(bf16[48,1280]{1,0:T(8,128)(2,1)} %param.7) | copy-start | bytes 368644
  35.2 7.6 %copy-start.18 = (f32[1280]{0:T(1024)S(1)}, f32[1280]{0:T(1024)}, u32[]{:S(2)}) copy-start(f32[1280]{0:T(1024)} %param.10) | copy-start | bytes 15364
  35.2 7.3 %collective-permute-start.8 = (bf16[96,1280]{1,0:T(8,128)(2,1)S(1)}, bf16[96,1280]{1,0:T(8,128)(2,1)S(1)}, u32[]{:S(2)}, u32[]{:S(2)}) collective-permute-start(bf16[96,1280]{1,0:T(8,128)(2,1)S(1)} %get-tuple-element.96), channel_id=1, source_target_pairs={{0,1},{1,0},{2,3},{3,2},{4,5},{5,4},{6,7},{7,6},{8,9},{9,8},{10,11... | collective-permute-start | bytes 737288 | tf_op jit(solution)/shard_map/projection/ppermute | solution.py:40
  38.6 5.9 %copy-start = (bf16[2048,1280]{1,0:T(8,128)(2,1)}, bf16[2048,1280]{1,0:T(8,128)(2,1)S(1)}, u32[]{:S(2)}) copy-start(bf16[2048,1280]{1,0:T(8,128)(2,1)S(1)} %constant_dynamic-slice_fusion.refs_0_.right) | copy-start | bytes 15728644
  42.7 1.8 copy-start.13
  42.8 7.5 %copy-start.19 = (s32[1,96]{1,0:T(1,128)S(1)}, s32[1,96]{1,0:T(1,128)}, u32[]{:S(2)}) copy-start(s32[1,96]{1,0:T(1,128)} %param.12) | copy-start | bytes 1156
  44.5 18.9 %collective-permute-start.10 = (f32[96,2048]{1,0:T(8,128)S(1)}, f32[96,2048]{1,0:T(8,128)}, u32[]{:S(2)}, u32[]{:S(2)}) collective-permute-start(f32[96,2048]{1,0:T(8,128)S(1)} %logits.4), channel_id=1, source_target_pairs={{2,4},{4,2},{3,5},{5,3},{10,12},{12,10},{11,13},{13,11},{18,20},{2... | collective-permute-start | bytes 2359304 | tf_op jit(solution)/shard_map/logits/ppermute | solution.py:447
  46.1 17.3 %collective-permute-start.9 = (f32[96,2048]{1,0:T(8,128)S(1)}, f32[96,2048]{1,0:T(8,128)S(1)}, u32[]{:S(2)}, u32[]{:S(2)}) collective-permute-start(f32[96,2048]{1,0:T(8,128)S(1)} %logits.4), channel_id=1, source_target_pairs={{0,2},{6,4},{1,3},{7,5},{8,10},{14,12},{9,11},{15,13},{16,18},{22,... | collective-permute-start | bytes 2359304 | tf_op jit(solution)/shard_map/logits/ppermute | solution.py:446
  48.7 14.7 %collective-permute-start.11 = (bf16[96,1280]{1,0:T(8,128)(2,1)S(1)}, bf16[96,1280]{1,0:T(8,128)(2,1)S(1)}, u32[]{:S(2)}, u32[]{:S(2)}) collective-permute-start(bf16[96,1280]{1,0:T(8,128)(2,1)S(1)} %multiply_convert_fusion.1.left.refs_4_), channel_id=1, source_target_pairs={{0,16},{8,24},{16,0},{24,8},{1,17},{9,25},{17,1},{25,9},{2,18},{10... | collective-permute-start | bytes 737288 | tf_op jit(solution)/shard_map/logits/ppermute | solution.py:36
  50.3 13.1 %collective-permute-start.12 = (f32[96]{0:T(128)S(1)}, f32[96]{0:T(128)S(1)}, u32[]{:S(2)}, u32[]{:S(2)}) collective-permute-start(f32[96]{0:T(128)S(1)} %get-tuple-element.168), channel_id=1, source_target_pairs={{0,2},{2,0},{4,6},{6,4},{1,3},{3,1},{5,7},{7,5},{8,10},{10,8},{12,... | collective-permute-start | bytes 1160 | tf_op jit(solution)/shard_map/logits/ppermute | solution.py:36
  63.4 9.7 %copy-start.7 = (bf16[96,1280]{1,0:T(8,128)(2,1)}, bf16[96,1280]{1,0:T(8,128)(2,1)S(1)}, u32[]{:S(2)}) copy-start(bf16[96,1280]{1,0:T(8,128)(2,1)S(1)} %collective-permute-done.11.refs_6_) | copy-start | bytes 737284
  63.4 17.3 %collective-permute-start.16 = (f32[2,96]{1,0:T(2,128)S(1)}, f32[2,96]{1,0:T(2,128)S(1)}, u32[]{:S(2)}, u32[]{:S(2)}) collective-permute-start(f32[2,96]{1,0:T(2,128)S(1)} %pad_maximum_fusion.4), channel_id=1, source_target_pairs={{0,4},{2,6},{4,0},{6,2},{1,5},{3,7},{5,1},{7,3},{8,12},{10,14},{12... | collective-permute-start | bytes 2312 | tf_op jit(solution)/shard_map/logits/ppermute | solution.py:36
  66.4 14.4 %collective-permute-start.15 = (bf16[2,96,1280]{2,1,0:T(8,128)(2,1)S(1)}, bf16[2,96,1280]{2,1,0:T(8,128)(2,1)S(1)}, u32[]{:S(2)}, u32[]{:S(2)}) collective-permute-start(bf16[2,96,1280]{2,1,0:T(8,128)(2,1)S(1)} %pad_maximum_fusion.1), channel_id=1, source_target_pairs={{0,8},{8,0},{16,24},{24,16},{1,9},{9,1},{17,25},{25,17},{2,10},{10... | collective-permute-start | bytes 1474568 | tf_op jit(solution)/shard_map/logits/ppermute | solution.py:36
  66.6 37.2 %collective-permute-start.13 = (f32[96,2048]{1,0:T(8,128)S(1)}, f32[96,2048]{1,0:T(8,128)S(1)}, u32[]{:S(2)}, u32[]{:S(2)}) collective-permute-start(f32[96,2048]{1,0:T(8,128)S(1)} %add.164), channel_id=1, source_target_pairs={{0,4},{2,6},{4,0},{6,2},{1,5},{3,7},{5,1},{7,3},{8,12},{10,14},{12... | collective-permute-start | bytes 2359304 | tf_op jit(solution)/shard_map/logits/ppermute | solution.py:36
  66.7 37.3 %collective-permute-start.14 = (f32[96,2048]{1,0:T(8,128)S(1)}, f32[96,2048]{1,0:T(8,128)S(1)}, u32[]{:S(2)}, u32[]{:S(2)}) collective-permute-start(f32[96,2048]{1,0:T(8,128)S(1)} %get-tuple-element.104), channel_id=1, source_target_pairs={{0,2},{2,0},{4,6},{6,4},{1,3},{3,1},{5,7},{7,5},{8,10},{10,8},{12,... | collective-permute-start | bytes 2359304 | tf_op jit(solution)/shard_map/logits/ppermute | solution.py:36
  80.8 23.2 %copy-start.15 = (bf16[2,96,1280]{2,1,0:T(8,128)(2,1)}, bf16[2,96,1280]{2,1,0:T(8,128)(2,1)S(1)}, u32[]{:S(2)}) copy-start(bf16[2,96,1280]{2,1,0:T(8,128)(2,1)S(1)} %collective-permute-done.15) | copy-start | bytes 1474564
  106.0 20.6 %collective-permute-start.18 = (bf16[96,2048]{1,0:T(8,128)(2,1)S(1)}, bf16[96,2048]{1,0:T(8,128)(2,1)S(1)}, u32[]{:S(2)}, u32[]{:S(2)}) collective-permute-start(bf16[96,2048]{1,0:T(8,128)(2,1)S(1)} %get-tuple-element.120.refs_0_), channel_id=1, source_target_pairs={{0,2},{2,0},{4,6},{6,4},{1,3},{3,1},{5,7},{7,5},{8,10},{10,8},{12,... | collective-permute-start | bytes 1179656 | tf_op jit(solution)/shard_map/grad_normed/ppermute | solution.py:36
  106.1 21.3 %collective-permute-start.17 = (bf16[96,2048]{1,0:T(8,128)(2,1)S(1)}, bf16[96,2048]{1,0:T(8,128)(2,1)}, u32[]{:S(2)}, u32[]{:S(2)}) collective-permute-start(bf16[96,2048]{1,0:T(8,128)(2,1)S(1)} %get-tuple-element.120.refs_0_), channel_id=1, source_target_pairs={{0,4},{2,6},{4,0},{6,2},{1,5},{3,7},{5,1},{7,3},{8,12},{10,14},{12... | collective-permute-start | bytes 1179656 | tf_op jit(solution)/shard_map/grad_normed/ppermute | solution.py:36
  111.4 14.2 %collective-permute-start.21 = (f32[4,96]{1,0:T(4,128)S(1)}, f32[4,96]{1,0:T(4,128)S(1)}, u32[]{:S(2)}, u32[]{:S(2)}) collective-permute-start(f32[4,96]{1,0:T(4,128)S(1)} %pad_maximum_fusion.3), channel_id=1, source_target_pairs={{0,6},{2,4},{4,2},{6,0},{1,7},{3,5},{5,3},{7,1},{8,14},{10,12},{12... | collective-permute-start | bytes 4616 | tf_op jit(solution)/shard_map/grad_normed/ppermute | solution.py:36
  113.5 13.2 %collective-permute-start.20 = (f32[4,96]{1,0:T(4,128)S(1)}, f32[4,96]{1,0:T(4,128)S(1)}, u32[]{:S(2)}, u32[]{:S(2)}) collective-permute-start(f32[4,96]{1,0:T(4,128)S(1)} %pad_maximum_fusion.3), channel_id=1, source_target_pairs={{0,4},{2,6},{4,0},{6,2},{1,5},{3,7},{5,1},{7,3},{8,12},{10,14},{12... | collective-permute-start | bytes 4616 | tf_op jit(solution)/shard_map/grad_normed/ppermute | solution.py:36
  113.5 13.2 %collective-permute-start.19 = (f32[4,96]{1,0:T(4,128)S(1)}, f32[4,96]{1,0:T(4,128)S(1)}, u32[]{:S(2)}, u32[]{:S(2)}) collective-permute-start(f32[4,96]{1,0:T(4,128)S(1)} %pad_maximum_fusion.3), channel_id=1, source_target_pairs={{0,2},{2,0},{4,6},{6,4},{1,3},{3,1},{5,7},{7,5},{8,10},{10,8},{12,... | collective-permute-start | bytes 4616 | tf_op jit(solution)/shard_map/grad_normed/ppermute | solution.py:36
  126.7 0.8 copy-start.4
  127.4 10.6 %collective-permute-start.23 = (bf16[96,2048]{1,0:T(8,128)(2,1)S(1)}, bf16[96,2048]{1,0:T(8,128)(2,1)}, u32[]{:S(2)}, u32[]{:S(2)}) collective-permute-start(bf16[96,2048]{1,0:T(8,128)(2,1)S(1)} %get-tuple-element.120.refs_0_), channel_id=1, source_target_pairs={{2,4},{4,2},{3,5},{5,3},{10,12},{12,10},{11,13},{13,11},{18,20},{2... | collective-permute-start | bytes 1179656 | tf_op jit(solution)/shard_map/grad_normed/ppermute | solution.py:498
  128.8 11.2 %collective-permute-start.22 = (bf16[96,2048]{1,0:T(8,128)(2,1)}, bf16[96,2048]{1,0:T(8,128)(2,1)}, u32[]{:S(2)}, u32[]{:S(2)}) collective-permute-start(bf16[96,2048]{1,0:T(8,128)(2,1)} %collective-permute-done.17.refs_1_), channel_id=1, source_target_pairs={{4,6},{2,0},{5,7},{3,1},{12,14},{10,8},{13,15},{11,9},{20,22},{18,... | collective-permute-start | bytes 1179656 | tf_op jit(solution)/shard_map/grad_normed/ppermute | solution.py:497
  130.4 7.6 %collective-permute-start.24 = (f32[4,4,96]{2,1,0:T(4,128)S(1)}, f32[4,4,96]{2,1,0:T(4,128)S(1)}, u32[]{:S(2)}, u32[]{:S(2)}) collective-permute-start(f32[4,4,96]{2,1,0:T(4,128)S(1)} %pad_maximum_fusion.2.here), channel_id=1, source_target_pairs={{0,1},{1,0},{2,3},{3,2},{4,5},{5,4},{6,7},{7,6},{8,9},{9,8},{10,11... | collective-permute-start | bytes 18440 | tf_op jit(solution)/shard_map/grad_normed/ppermute | solution.py:40
  131.0 9.1 %slice-start = ((s8[5242880]{0:T(1024)(128)(4,1)}), s8[1048576]{0:T(1024)(128)(4,1)S(1)}, s32[]{:S(2)}) async-start(s8[5242880]{0:T(1024)(128)(4,1)} %bitcast.74), calls=%async_computation | async-start | bytes 2097152
  131.1 1.1 copy-start.5
  132.2 7.9 %copy-start.12 = (f32[1,96]{1,0:T(1,128)S(1)}, f32[1,96]{1,0:T(1,128)}, u32[]{:S(2)}) copy-start(f32[1,96]{1,0:T(1,128)} %weights.1) | copy-start | bytes 1156
  132.2 7.9 %slice-start.1 = ((s8[5242880]{0:T(1024)(128)(4,1)}), s8[4194304]{0:T(1024)(128)(4,1)S(1)}, s32[]{:S(2)}) async-start(s8[5242880]{0:T(1024)(128)(4,1)} %bitcast.74), calls=%async_computation.1 | async-start | bytes 8388608
  140.1 3.0 %copy-start.6 = (bf16[96,2048]{1,0:T(8,128)(2,1)S(1)}, bf16[96,2048]{1,0:T(8,128)(2,1)}, u32[]{:S(2)}) copy-start(bf16[96,2048]{1,0:T(8,128)(2,1)} %copy-done.4) | copy-start | bytes 1179652
  142.5 6.3 %collective-permute-start.25 = (bf16[96,1280]{1,0:T(8,128)(2,1)S(1)}, bf16[96,1280]{1,0:T(8,128)(2,1)S(1)}, u32[]{:S(2)}, u32[]{:S(2)}) collective-permute-start(bf16[96,1280]{1,0:T(8,128)(2,1)S(1)} %get-tuple-element.163), channel_id=1, source_target_pairs={{0,1},{1,0},{2,3},{3,2},{4,5},{5,4},{6,7},{7,6},{8,9},{9,8},{10,11... | collective-permute-start | bytes 737288 | tf_op jit(solution)/shard_map/grad_normed/ppermute | solution.py:40
  145.0 3.8 %copy-start.14 = (f32[96,1280]{1,0:T(8,128)S(1)}, f32[96,1280]{1,0:T(8,128)}, u32[]{:S(2)}) copy-start(f32[96,1280]{1,0:T(8,128)} %copy-done.13) | copy-start | bytes 1474564
  145.2 4.1 %copy-start.3 = (bf16[1280,1280]{1,0:T(8,128)(2,1)S(1)}, bf16[1280,1280]{1,0:T(8,128)(2,1)}, u32[]{:S(2)}) copy-start(bf16[1280,1280]{1,0:T(8,128)(2,1)} %get-tuple-element.134.refs_0_) | copy-start | bytes 9830404
  148.8 6.0 %copy-start.1 = (bf16[1280,1280]{1,0:T(8,128)(2,1)S(1)}, bf16[1280,1280]{1,0:T(8,128)(2,1)}, u32[]{:S(2)}) copy-start(bf16[1280,1280]{1,0:T(8,128)(2,1)} %get-tuple-element.138.refs_1_) | copy-start | bytes 9830404
  148.8 6.0 %copy-start.2 = (bf16[1280,1280]{1,0:T(8,128)(2,1)S(1)}, bf16[1280,1280]{1,0:T(8,128)(2,1)}, u32[]{:S(2)}) copy-start(bf16[1280,1280]{1,0:T(8,128)(2,1)} %get-tuple-element.137.refs_0_) | copy-start | bytes 9830404
  149.2 5.7 %collective-permute-start.27 = (bf16[96,2048]{1,0:T(8,128)(2,1)S(1)}, bf16[96,2048]{1,0:T(8,128)(2,1)S(1)}, u32[]{:S(2)}, u32[]{:S(2)}) collective-permute-start(bf16[96,2048]{1,0:T(8,128)(2,1)S(1)} %get-tuple-element.135), channel_id=1, source_target_pairs={{0,8},{8,0},{16,24},{24,16},{1,9},{9,1},{17,25},{25,17},{2,10},{10... | collective-permute-start | bytes 1179656 | tf_op jit(solution)/shard_map/joined_grad/ppermute | solution.py:36
  151.2 8.8 %copy-start.16 = (bf16[2,96,1280]{2,1,0:T(8,128)(2,1)S(1)}, bf16[2,96,1280]{2,1,0:T(8,128)(2,1)}, u32[]{:S(2)}) copy-start(bf16[2,96,1280]{2,1,0:T(8,128)(2,1)} %copy-done.15) | copy-start | bytes 1474564
  151.2 8.9 %copy-start.9 = (bf16[3,96,1280]{2,1,0:T(8,128)(2,1)S(1)}, bf16[3,96,1280]{2,1,0:T(8,128)(2,1)}, u32[]{:S(2)}) copy-start(bf16[3,96,1280]{2,1,0:T(8,128)(2,1)} %get-tuple-element.141.part) | copy-start | bytes 2211844
  151.2 28.6 %collective-permute-start.26 = (bf16[96,1408]{1,0:T(8,128)(2,1)}, bf16[96,1408]{1,0:T(8,128)(2,1)}, u32[]{:S(2)}, u32[]{:S(2)}) collective-permute-start(bf16[96,1408]{1,0:T(8,128)(2,1)} %joined_grad.5), channel_id=1, source_target_pairs={{0,6},{2,4},{4,2},{6,0},{1,7},{3,5},{5,3},{7,1},{8,14},{10,12},{12... | collective-permute-start | bytes 811016 | tf_op jit(solution)/shard_map/joined_grad/ppermute | solution.py:36
  153.2 19.8 %collective-permute-start.30 = (bf16[96,2048]{1,0:T(8,128)(2,1)}, bf16[96,2048]{1,0:T(8,128)(2,1)}, u32[]{:S(2)}, u32[]{:S(2)}) collective-permute-start(bf16[96,2048]{1,0:T(8,128)(2,1)} %get-tuple-element.145), channel_id=1, source_target_pairs={{0,16},{8,24},{16,0},{24,8},{1,17},{9,25},{17,1},{25,9},{2,18},{10... | collective-permute-start | bytes 1179656 | tf_op jit(solution)/shard_map/joined_grad/ppermute | solution.py:36
  154.7 18.3 %collective-permute-start.31 = (bf16[96,2048]{1,0:T(8,128)(2,1)}, bf16[96,2048]{1,0:T(8,128)(2,1)}, u32[]{:S(2)}, u32[]{:S(2)}) collective-permute-start(bf16[96,2048]{1,0:T(8,128)(2,1)} %get-tuple-element.146), channel_id=1, source_target_pairs={{0,24},{8,16},{16,8},{24,0},{1,25},{9,17},{17,9},{25,1},{2,26},{10... | collective-permute-start | bytes 1179656 | tf_op jit(solution)/shard_map/joined_grad/ppermute | solution.py:36
  154.8 2.8 %copy-start.10 = (bf16[96,2048]{1,0:T(8,128)(2,1)}, bf16[96,2048]{1,0:T(8,128)(2,1)S(1)}, u32[]{:S(2)}) copy-start(bf16[96,2048]{1,0:T(8,128)(2,1)S(1)} %collective-permute-done.27.refs_1_) | copy-start | bytes 1179652
  157.6 22.2 %collective-permute-start.28 = (bf16[96,1408]{1,0:T(8,128)(2,1)}, bf16[96,1408]{1,0:T(8,128)(2,1)}, u32[]{:S(2)}, u32[]{:S(2)}) collective-permute-start(bf16[96,1408]{1,0:T(8,128)(2,1)} %get-tuple-element.139), channel_id=1, source_target_pairs={{0,4},{2,6},{4,0},{6,2},{1,5},{3,7},{5,1},{7,3},{8,12},{10,14},{12... | collective-permute-start | bytes 811016 | tf_op jit(solution)/shard_map/joined_grad/ppermute | solution.py:36
  158.3 21.5 %collective-permute-start.29 = (bf16[96,1408]{1,0:T(8,128)(2,1)}, bf16[96,1408]{1,0:T(8,128)(2,1)}, u32[]{:S(2)}, u32[]{:S(2)}) collective-permute-start(bf16[96,1408]{1,0:T(8,128)(2,1)} %get-tuple-element.140), channel_id=1, source_target_pairs={{0,2},{2,0},{4,6},{6,4},{1,3},{3,1},{5,7},{7,5},{8,10},{10,8},{12,... | collective-permute-start | bytes 811016 | tf_op jit(solution)/shard_map/joined_grad/ppermute | solution.py:36
  170.1 2.9 %copy-start.8 = (bf16[96,1280]{1,0:T(8,128)(2,1)S(1)}, bf16[96,1280]{1,0:T(8,128)(2,1)}, u32[]{:S(2)}) copy-start(bf16[96,1280]{1,0:T(8,128)(2,1)} %copy-done.7) | copy-start | bytes 737284
  170.1 2.9 %copy-start.11 = (bf16[96,2048]{1,0:T(8,128)(2,1)S(1)}, bf16[96,2048]{1,0:T(8,128)(2,1)}, u32[]{:S(2)}) copy-start(bf16[96,2048]{1,0:T(8,128)(2,1)} %copy-done.10) | copy-start | bytes 1179652
  181.3 1.6 collective-permute-start.32
  182.9 7.4 %collective-permute-start.33 = (bf16[48,1280]{1,0:T(8,128)(2,1)S(1)}, bf16[48,1280]{1,0:T(8,128)(2,1)S(1)}, u32[]{:S(2)}, u32[]{:S(2)}) collective-permute-start(bf16[48,1280]{1,0:T(8,128)(2,1)S(1)} %get-tuple-element.181), channel_id=1, source_target_pairs={{0,16},{8,24},{16,0},{24,8},{2,18},{10,26},{18,2},{26,10},{4,20},{... | collective-permute-start | bytes 368648 | tf_op jit(solution)/shard_map/input_grads/ppermute | solution.py:581
  186.3 5.2 %collective-permute-start.34 = (bf16[48,1280]{1,0:T(8,128)(2,1)S(1)}, bf16[48,1280]{1,0:T(8,128)(2,1)S(1)}, u32[]{:S(2)}, u32[]{:S(2)}) collective-permute-start(bf16[48,1280]{1,0:T(8,128)(2,1)S(1)} %get-tuple-element.182), channel_id=1, source_target_pairs={{0,1},{1,0},{2,3},{3,2},{4,5},{5,4},{6,7},{7,6},{8,9},{9,8},{10,11... | collective-permute-start | bytes 368648 | tf_op jit(solution)/shard_map/input_grads/ppermute | solution.py:40
  186.4 6.3 %collective-permute-start.35 = (bf16[48,1280]{1,0:T(8,128)(2,1)S(1)}, bf16[48,1280]{1,0:T(8,128)(2,1)S(1)}, u32[]{:S(2)}, u32[]{:S(2)}) collective-permute-start(bf16[48,1280]{1,0:T(8,128)(2,1)S(1)} %get-tuple-element.183), channel_id=1, source_target_pairs={{0,17},{8,25},{16,1},{24,9},{2,19},{10,27},{18,3},{26,11},{4,21},{... | collective-permute-start | bytes 368648 | tf_op jit(solution)/shard_map/input_grads/ppermute | solution.py:584

commit v5 on v4

--- a/solution.py
+++ b/solution.py
@@ -208,8 +208,15 @@
 
 def held_between_kernel(places, outer, inner, right, out):
     t = tensor_at(places)
-    left = jnp.where((t == 0) | (t == 3), outer[...], inner[...])
-    out[...] = plain_dot(left, right[...])
+    at_end = (t == 0) | (t == 3)
+
+    @pl.when(at_end)
+    def _():
+        out[...] = plain_dot(outer[...], right[...])
+
+    @pl.when(jnp.logical_not(at_end))
+    def _():
+        out[...] = plain_dot(inner[...], right[...])
 
 
 def streamed(places, weight, chunks, blocks, held, done):
@@ -244,11 +251,20 @@
 
 def stream_rows_kernel(chunks, blocks, places, *refs):
     count = len(chunks)
-    lefts, weight, outs, (held, done) = refs[:count], refs[count], refs[count + 1 : -2], refs[-2:]
+    sources, weight, outs = refs[:count], refs[count], refs[count + 1 : 2 * count + 1]
+    held, done, lefts, fetched = refs[2 * count + 1 :]
+    fetches = [
+        pltpu.make_async_copy(source, lefts.at[k], fetched.at[k])
+        for k, source in enumerate(sources)
+    ]
+    for fetch in fetches:
+        fetch.start()
     block = held.shape[1]
     for n, right in streamed(places, weight, chunks, blocks, held, done):
         k, j = n // blocks, n % blocks
-        product = plain_dot(lefts[k][:, j * block : (j + 1) * block], right)
+        if j == 0:
+            fetches[k].wait()
+        product = plain_dot(lefts[k, :, j * block : (j + 1) * block], right)
         if j == 0:
             outs[k][...] = product
         else:
@@ -280,10 +296,23 @@
 
 def stream_rows(places, lefts, weight, chunks, blocks, slots):
     rows, size = lefts[0].shape
+    count = len(chunks)
     outs = [shaped(rows, weight.shape[1], f32) for _ in chunks]
-    return stream(
-        stream_rows_kernel, places, lefts, weight, chunks, size, outs, blocks, slots
-    )
+    anywhere = pl.BlockSpec(memory_space=pl.ANY)
+    return pl.pallas_call(
+        functools.partial(stream_rows_kernel, chunks, blocks),
+        out_shape=outs,
+        in_specs=[in_smem] + [anywhere] * (count + 1),
+        out_specs=[in_vmem] * count,
+        scratch_shapes=[
+            pltpu.VMEM((slots, size // blocks, weight.shape[1]), weight.dtype),
+            pltpu.SemaphoreType.DMA((slots,)),
+            pltpu.VMEM((count, rows, size), bf16),
+            pltpu.SemaphoreType.DMA((count,)),
+        ],
+        compiler_params=params(kernel_memory),
+        cost_estimate=brief,
+    )(places, *lefts, weight)
 
 
 def combine_kernel(places, own, part, grad, out):
@@ -322,28 +351,31 @@
     )(places, own, parts, grad)
 
 
-def head_sum_kernel(*refs):
+def head_sum_kernel(count, *refs):
     out = refs[-1]
-    count = (len(refs) - 1) // 2
     left = jnp.concatenate([r[...] for r in refs[:count]], axis=0)
     right = jnp.concatenate([r[...] for r in refs[count : 2 * count]], axis=0)
     out[...] = contract_rows(left, right)
 
 
-def head_sum(grads, normed, blocks):
+def head_sum(grads, normed, blocks, half, base=None):
     rows, size = grads[0].shape
     width = normed[0].shape[1]
     block = size // blocks
+    start = half * blocks // 2
+    based = [] if base is None else [base]
     return pl.pallas_call(
-        head_sum_kernel,
+        functools.partial(head_sum_kernel, len(grads)),
         out_shape=shaped(size, width, f32),
-        grid=(blocks,),
-        in_specs=[pl.BlockSpec((rows, block), lambda j: (0, j))] * len(grads)
-        + [pl.BlockSpec((rows, width), lambda j: (0, 0))] * len(normed),
-        out_specs=pl.BlockSpec((block, width), lambda j: (j, 0)),
+        grid=(blocks // 2,),
+        in_specs=[pl.BlockSpec((rows, block), lambda j: (0, start + j))] * len(grads)
+        + [pl.BlockSpec((rows, width), lambda j: (0, 0))] * len(normed)
+        + [pl.BlockSpec(memory_space=pl.ANY)] * len(based),
+        out_specs=pl.BlockSpec((block, width), lambda j: (start + j, 0)),
+        input_output_aliases={} if base is None else {2 * len(grads): 0},
         compiler_params=params(kernel_memory),
         cost_estimate=brief,
-    )(*grads, *normed)
+    )(*grads, *normed, *based)
 
 
 def softmax_factors_kernel(_, here, there, weights, scale, out):
@@ -459,11 +491,13 @@
         near = flip(near, "tensor", n_tensor, 1)
         chosen = lax.broadcasted_iota(jnp.int32, (1, vocab_part), 1) == wanted
         (target_rows,) = stream_rows(
-            places, [chosen.astype(bf16)], unembed_weight, [None], 16, 8
+            places, [chosen.astype(bf16)], unembed_weight, [None], 8, 4
         )
         (last,) = stream_columns(places, low_chips[0], unembed_weight, [0], piece, 4, f32)
-        cross, near, low_cores, squares_there, target_rows, last = lax.optimization_barrier(
-            (cross, near, low_cores, squares_there, target_rows, last)
+        cross, near, low_cores, squares_there, target_rows, last, scale_in = (
+            lax.optimization_barrier(
+                (cross, near, low_cores, squares_there, target_rows, last, in_scale[:, 0])
+            )
         )
         low_heads = [low_chips[0], low_cores[0], low_chips[1], low_cores[1]]
         squares = squares[0] + squares[1] + squares_there[0] + squares_there[1]
@@ -486,7 +520,7 @@
     with jax.named_scope("grad_normed"):
         cross = flip(shifted_low, "tensor", n_tensor, 2)
         near = flip(shifted_low, "tensor", n_tensor, 1)
-        products = stream_rows(places, [shifted_low], unembed_weight, [0], 4, 4)
+        products = stream_rows(places, [shifted_low], unembed_weight, [0], 2, 2)
         stats, products = lax.optimization_barrier((stats, products))
         stats = spread(stats)
         weight_sent = [chunk_of(combine_whole, r, width) for r in (3, 2, 1)]
@@ -498,8 +532,10 @@
         middle = lax.ppermute(value, "tensor", [(1, 2), (2, 1)])
         stats = jnp.stack(stats)
         there = swap(stats)
-        products += stream_rows(places, [near, cross], unembed_weight, [1, 2], 4, 8)
-        ends, middle, there, products = lax.optimization_barrier((ends, middle, there, products))
+        products += stream_rows(places, [near, cross], unembed_weight, [1, 2], 2, 4)
+        ends, middle, there, products, wanted = lax.optimization_barrier(
+            (ends, middle, there, products, wanted)
+        )
         products += whole_call(
             held_between_kernel,
             places,
@@ -525,7 +561,7 @@
         grad_stack = jnp.stack(
             [
                 jnp.where(
-                    (ids + (t ^ r) * piece) == wanted,
+                    ids == wanted - (t ^ r) * piece,
                     hit_scaled[:, None],
                     e.astype(f32) * factors_scaled[r][:, None],
                 ).astype(bf16)
@@ -544,7 +580,7 @@
             grad_normed * final_gain[None, :] - mixed_normed * (grad_dots / features)[:, None]
         )
         grad_low = grad_mixed.astype(bf16)
-        grad_scaled = (in_scale * grad_mixed).astype(bf16)
+        grad_scaled = (scale_in[:, None] * grad_mixed).astype(bf16)
         dots = jnp.sum(grad_low.astype(f32) * projected, axis=1, keepdims=True)
         dots_high = lax.reduce_precision(dots, 8, 7)
         lane = lax.broadcasted_iota(jnp.int32, (1, 128), 1)
@@ -562,11 +598,7 @@
         ]
         (side,) = stream_columns(places, grad_low, weight_block, [0], width, 2, f32)
         combine_grad = combine(places, own, parts, grad_scaled)[None]
-        unembed_grad = head_sum([grad_slices[0]] + heads_given, low_heads, 2)
-        unembed_grad = unembed_grad.reshape(1, 1, piece, width)
-        came, side, combine_grad, unembed_grad = lax.optimization_barrier(
-            (came, side, combine_grad, unembed_grad)
-        )
+        came, side, combine_grad = lax.optimization_barrier((came, side, combine_grad))
     with jax.named_scope("input_grads"):
         term, term_low = whole_call(
             functools.partial(input_grad_kernel, features),
@@ -574,19 +606,22 @@
             [side, own, in_scale, grad_mixed, dots] + came,
             [shaped(rows, width, f32), shaped(rows, width, bf16)],
         )
-        pair = flip(term_low, "head", n_head, 1)
-        pair = term_low.astype(f32) + pair.astype(f32)
-        pair_low = pair.astype(bf16)
-        crossed = swap(jnp.where(first, pair_low[half:], term_low[:half]))
-        beside = lax.ppermute(
-            pair_low[:half], ("head", "dp"), [(2 * i, 2 * (i ^ 2)) for i in range(n_head)]
-        )
-        across = lax.ppermute(
-            pair_low[half:], ("head", "dp"), [(2 * i, 2 * (i ^ 2) + 1) for i in range(n_head)]
-        )
-        crossed, beside, across = [v.astype(f32) for v in (crossed, beside, across)]
+        crossed = swap(jnp.where(first, term_low[half:], term_low[:half]))
+        heads = [grad_slices[0]] + heads_given
+        unembed_grad = head_sum(heads, low_heads, 4, 0)
+        crossed, unembed_grad = lax.optimization_barrier((crossed, unembed_grad))
+        crossed = crossed.astype(f32)
         embed_grad = jnp.where(first, crossed, term[half:])[None]
-        trunk_grad = jnp.where(first, pair[:half] + beside, crossed + across)
+        trunk = jnp.where(first, term[:half], crossed)
+        trunk_low = trunk.astype(bf16)
+        core = flip(trunk_low, "head", n_head, 1)
+        core, unembed_grad = lax.optimization_barrier((core, unembed_grad))
+        trunk_low = (trunk_low.astype(f32) + core.astype(f32)).astype(bf16)
+        over = flip(trunk_low, "head", n_head, 2)
+        unembed_grad = head_sum(heads, low_heads, 4, 1, unembed_grad)
+        over, unembed_grad = lax.optimization_barrier((over, unembed_grad))
+        trunk_grad = trunk_low.astype(f32) + over.astype(f32)
+        unembed_grad = unembed_grad.reshape(1, 1, piece, width)
     return (trunk_grad, embed_grad, combine_grad, unembed_grad)
 
 

time: 194 us -> 194 us (level)
  starting transfers between devices: 48.7 us -> 43.9 us
  other arithmetic: 7.67 us -> 9.86 us
    pallas_call x1 -> x5, Pallas kernels: 6.72 us -> 23.3 us  [the longest x3 16.6 us: stream_rows(): pl.pallas_call(functools.partial(stream_rows_kernel, chunks, blocks), out...]
    pallas_call x6 -> x3, Pallas kernels: 28.4 us -> 12 us  [stream(): pl.pallas_call(functools.partial(kernel, chunks, blocks), out_shape=outs,...]
    ppermute x2 -> x0, starting transfers between devices: 7.28 us -> none  [the longest x1 3.88 us: fast_local(): lax.ppermute(pair_low[half:], ('head', 'dp'), [(2 * i, 2 * (i ^ 2) + 1) f...]
    ppermute x24 -> x25, waiting for transfers between devices: 49.2 us -> 51.5 us  [flip(): return lax.ppermute(value, axis, [(i, i ^ mask) for i in range(size)])]
    ppermute x24 -> x25, starting transfers between devices: 29.2 us -> 30.5 us  [flip(): return lax.ppermute(value, axis, [(i, i ^ mask) for i in range(size)])]
  transfers between devices with their start and end apart: 36 -> 35, of which waited for: 15 -> 14; matrix products, arithmetic and copies ran while one was open for 8% -> 9% of each run, Pallas kernels for 27% -> 28%
where the time goes in v5:
time: 194 us; the launch traced here: 193 us
  Pallas kernels  62.8 us (32%)
  waiting for transfers between devices  60.4 us (31%)
  starting transfers between devices  43.9 us (23%)
  local copies, waits for them, and re-layouts  14.9 us (8%)
  other arithmetic  9.86 us (5%)
    ppermute x25, waiting for transfers between devices, flip(): return lax.ppermute(value, axis, [(i, i ^ mask) for i in range(size)])  51.5 us
    ppermute x25, starting transfers between devices, flip(): return lax.ppermute(value, axis, [(i, i ^ mask) for i in range(size)])  30.5 us
    pallas_call x3, Pallas kernels, stream_rows(): pl.pallas_call(functools.partial(stream_rows_kernel, chunks, blocks), out...  16.6 us
    pallas_call x3, Pallas kernels, stream(): pl.pallas_call(functools.partial(kernel, chunks, blocks), out_shape=outs,...  12 us
    dynamic_slice x2, local copies, waits for them, and re-layouts, chunk_of(): return lax.dynamic_slice_in_dim(weight, (t ^ r) * size, size, 0)  10.7 us
    pallas_call x6, Pallas kernels, whole_call(): pl.pallas_call(kernel, out_shape=outs, in_specs=[in_smem] + [in_vmem] * l...  10.5 us
    pallas_call x1, Pallas kernels, combine(): pl.pallas_call(combine_kernel, out_shape=shaped(count * width, grad.shape...  9.94 us
    pallas_call x2, Pallas kernels, head_sum(): pl.pallas_call(functools.partial(head_sum_kernel, len(grads)), out_shape=...  6.72 us
  transfers between devices with their start and end apart: 35, of which 14 were waited for; matrix products, arithmetic and copies ran while one was open for 9% of the time, Pallas kernels for 28%

profile of v5, /device:TPU:0, one launch (start us, length us, event | category | flops | bytes accessed | tf_op | source)
XLA Modules:
  0.0 193.2 jit_solution(4714317079945138233)
XLA Ops:
  0.6 1.0 bitcast_select_fusion
  1.6 3.0 %collective-permute-start.3 = (bf16[48,1280]{1,0:T(8,128)(2,1)S(1)}, bf16[48,1280]{1,0:T(8,128)(2,1)S(1)}, u32[]{:S(2)}, u32[]{:S(2)}) collective-permute-start(bf16[48,1280]{1,0:T(8,128)(2,1)S(1)} %get-tuple-element.193), channel_id=1, source_target_pairs={{0,1},{1,0},{2,3},{3,2},{4,5},{5,4},{6,7},{7,6},{8,9},{9,8},{10,11... | collective-permute-start | bytes 368648 | tf_op jit(solution)/shard_map/inputs/ppermute | solution.py:40
  4.7 3.6 %collective-permute-start.2 = (bf16[48,1280]{1,0:T(8,128)(2,1)S(1)}, bf16[48,1280]{1,0:T(8,128)(2,1)S(1)}, u32[]{:S(2)}, u32[]{:S(2)}) collective-permute-start(bf16[48,1280]{1,0:T(8,128)(2,1)S(1)} %get-tuple-element.88.kept), channel_id=1, source_target_pairs={{0,6},{2,4},{4,2},{6,0},{1,7},{3,5},{5,3},{7,1},{8,14},{10,12},{12... | collective-permute-start | bytes 368648 | tf_op jit(solution)/shard_map/inputs/ppermute | solution.py:36
  8.3 0.8 collective-permute-start
  9.3 3.5 %collective-permute-done.2.refs_2_ = bf16[48,1280]{1,0:T(8,128)(2,1)S(1)} collective-permute-done((bf16[48,1280]{1,0:T(8,128)(2,1)S(1)}, bf16[48,1280]{1,0:T(8,128)(2,1)S(1)}, u32[]{:S(2)}, u32[]{:S(2)}) %collective-permute-start.2) | collective-permute-done | bytes 122912 | tf_op jit(solution)/shard_map/inputs/ppermute | solution.py:36
  12.8 5.5 %collective-permute-done.1.refs_1_ = bf16[48,1280]{1,0:T(8,128)(2,1)S(1)} collective-permute-done((bf16[48,1280]{1,0:T(8,128)(2,1)S(1)}, bf16[48,1280]{1,0:T(8,128)(2,1)S(1)}, u32[]{:S(2)}, u32[]{:S(2)}) %collective-permute-start.1) | collective-permute-done | bytes 122912 | tf_op jit(solution)/shard_map/inputs/ppermute | solution.py:36
  18.4 2.7 %collective-permute-start.6 = (bf16[48,1280]{1,0:T(8,128)(2,1)S(1)}, bf16[48,1280]{1,0:T(8,128)(2,1)S(1)}, u32[]{:S(2)}, u32[]{:S(2)}) collective-permute-start(bf16[48,1280]{1,0:T(8,128)(2,1)S(1)} %collective-permute-done.3.given), channel_id=1, source_target_pairs={{0,6},{2,4},{4,2},{6,0},{1,7},{3,5},{5,3},{7,1},{8,14},{10,12},{12... | collective-permute-start | bytes 368648 | tf_op jit(solution)/shard_map/inputs/ppermute | solution.py:36
  21.1 1.7 collective-permute-start.4
  22.7 2.5 %inputs.1 = (bf16[96,1280]{1,0:T(8,128)(2,1)S(1)}, f32[96,1280]{1,0:T(8,128)S(1)}, f32[96,1]{1,0:T(8,128)S(1)}) custom-call(s32[1]{0:T(128)} %bitcast.places._, bf16[48,1280]{1,0:T(8,128)(2,1)S(1)} %get-tuple-element.88.kept, bf16[48,1280]{1,0:T(8,128)(2,1)S(1)} %collective-permute-done.3.given, bf16[5120,1280]{1,0:T(8,128)(2,1)} %bitcast.88), custom_call_target="tpu_custom_call" | custom-call | tf_op jit(solution)/shard_map/inputs/pallas_call | solution.py:109
  25.2 1.2 collective-permute-done.6.refs_5_
  26.4 4.2 %collective-permute-done.5.refs_4_ = bf16[48,1280]{1,0:T(8,128)(2,1)S(1)} collective-permute-done((bf16[48,1280]{1,0:T(8,128)(2,1)S(1)}, bf16[48,1280]{1,0:T(8,128)(2,1)S(1)}, u32[]{:S(2)}, u32[]{:S(2)}) %collective-permute-start.5) | collective-permute-done | bytes 122912 | tf_op jit(solution)/shard_map/inputs/ppermute | solution.py:36
  30.6 4.6 %projection.1 = (bf16[3,96,1280]{2,1,0:T(8,128)(2,1)}, f32[96,1280]{1,0:T(8,128)S(1)}, bf16[96,1280]{1,0:T(8,128)(2,1)S(1)}, f32[96,1]{1,0:T(8,128)S(1)}) custom-call(s32[1]{0:T(128)} %bitcast.places._, bf16[48,1280]{1,0:T(8,128)(2,1)S(1)} %collective-permute-done.refs_0_, bf16[48,1280]{1,0:T(8,128)(2,1)S(1)} %collective-permute-done.1.refs_1_, ...), custom_call_target="tpu_custom_call" | custom-call | tf_op jit(solution)/shard_map/projection/pallas_call | solution.py:166
  35.8 2.8 %constant_dynamic-slice_fusion.refs_0_.right = bf16[2048,1280]{1,0:T(8,128)(2,1)S(1)} fusion(bf16[8192,1280]{1,0:T(8,128)(2,1)} %refs_2_.1, s32[]{:T(128)S(6)} %select_n.102), kind=kLoop, calls=%fused_computation.57 | loop fusion | bytes 10485764 | tf_op jit(solution)/shard_map/projection/dynamic_slice | solution.py:445
  38.6 3.9 %collective-permute-done.8 = bf16[96,1280]{1,0:T(8,128)(2,1)S(1)} collective-permute-done((bf16[96,1280]{1,0:T(8,128)(2,1)S(1)}, bf16[96,1280]{1,0:T(8,128)(2,1)S(1)}, u32[]{:S(2)}, u32[]{:S(2)}) %collective-permute-start.8) | collective-permute-done | bytes 245792 | tf_op jit(solution)/shard_map/projection/ppermute | solution.py:40
  42.8 1.7 logits.4
  44.5 0.7 collective-permute-start.10
  45.2 4.1 %collective-permute-start.9 = (f32[96,2048]{1,0:T(8,128)S(1)}, f32[96,2048]{1,0:T(8,128)}, u32[]{:S(2)}, u32[]{:S(2)}) collective-permute-start(f32[96,2048]{1,0:T(8,128)S(1)} %logits.4), channel_id=1, source_target_pairs={{0,2},{6,4},{1,3},{7,5},{8,10},{14,12},{9,11},{15,13},{16,18},{22,... | collective-permute-start | bytes 2359304 | tf_op jit(solution)/shard_map/logits/ppermute | solution.py:478
  49.4 1.5 collective-permute-start.11
  51.0 0.7 reduce
  51.6 5.6 %logits.5 = (f32[96,2048]{1,0:T(8,128)S(1)}, f32[96,2048]{1,0:T(8,128)S(1)}) custom-call(s32[1]{0:T(128)} %bitcast.places._, bf16[96,1280]{1,0:T(8,128)(2,1)S(1)} %multiply_convert_fusion.1.left.refs_4_, bf16[8192,1280]{1,0:T(8,128)(2,1)} %refs_2_.1), custom_call_target="tpu_custom_call" | custom-call | tf_op jit(solution)/shard_map/logits/pallas_call | solution.py:275
  57.2 6.2 %collective-permute-done.12 = f32[96]{0:T(128)S(1)} collective-permute-done((f32[96]{0:T(128)S(1)}, f32[96]{0:T(128)S(1)}, u32[]{:S(2)}, u32[]{:S(2)}) %collective-permute-start.12) | collective-permute-done | bytes 416 | tf_op jit(solution)/shard_map/logits/ppermute | solution.py:36
  63.4 3.0 %collective-permute-start.16 = (f32[2,96]{1,0:T(2,128)S(1)}, f32[2,96]{1,0:T(2,128)S(1)}, u32[]{:S(2)}, u32[]{:S(2)}) collective-permute-start(f32[2,96]{1,0:T(2,128)S(1)} %pad_maximum_fusion.4), channel_id=1, source_target_pairs={{0,4},{2,6},{4,0},{6,2},{1,5},{3,7},{5,1},{7,3},{8,12},{10,14},{12... | collective-permute-start | bytes 2312 | tf_op jit(solution)/shard_map/logits/ppermute | solution.py:36
  66.5 1.2 add.126
  67.9 2.5 %collective-permute-start.14 = (f32[96,2048]{1,0:T(8,128)S(1)}, f32[96,2048]{1,0:T(8,128)S(1)}, u32[]{:S(2)}, u32[]{:S(2)}) collective-permute-start(f32[96,2048]{1,0:T(8,128)S(1)} %get-tuple-element.111), channel_id=1, source_target_pairs={{0,2},{2,0},{4,6},{6,4},{1,3},{3,1},{5,7},{7,5},{8,10},{10,8},{12,... | collective-permute-start | bytes 2359304 | tf_op jit(solution)/shard_map/logits/ppermute | solution.py:36
  70.8 3.5 %logits.7 = f32[96,2048]{1,0:T(8,128)S(1)} custom-call(s32[1]{0:T(128)} %bitcast.places._, bf16[96,1280]{1,0:T(8,128)(2,1)S(1)} %multiply_convert_fusion.1.left.refs_4_, bf16[8192,1280]{1,0:T(8,128)(2,1)} %refs_2_.1), custom_call_target="tpu_custom_call" | custom-call | tf_op jit(solution)/shard_map/logits/pallas_call | solution.py:275
  74.3 8.1 %logits.6 = f32[96,1280]{1,0:T(8,128)S(1)} custom-call(s32[1]{0:T(128)} %bitcast.places._, bf16[96,8192]{1,0:T(8,128)(2,1)S(1)} %fusion.refs_0_, bf16[8192,1280]{1,0:T(8,128)(2,1)} %refs_2_.1), custom_call_target="tpu_custom_call" | custom-call | tf_op jit(solution)/shard_map/logits/pallas_call | solution.py:302
  82.4 22.6 %collective-permute-done.13 = f32[96,2048]{1,0:T(8,128)S(1)} collective-permute-done((f32[96,2048]{1,0:T(8,128)S(1)}, f32[96,2048]{1,0:T(8,128)S(1)}, u32[]{:S(2)}, u32[]{:S(2)}) %collective-permute-start.13) | collective-permute-done | bytes 786464 | tf_op jit(solution)/shard_map/logits/ppermute | solution.py:36
  106.3 2.4 %collective-permute-start.17 = (bf16[96,2048]{1,0:T(8,128)(2,1)S(1)}, bf16[96,2048]{1,0:T(8,128)(2,1)}, u32[]{:S(2)}, u32[]{:S(2)}) collective-permute-start(bf16[96,2048]{1,0:T(8,128)(2,1)S(1)} %get-tuple-element.128.refs_0_), channel_id=1, source_target_pairs={{0,4},{2,6},{4,0},{6,2},{1,5},{3,7},{5,1},{7,3},{8,12},{10,14},{12... | collective-permute-start | bytes 1179656 | tf_op jit(solution)/shard_map/grad_normed/ppermute | solution.py:36
  108.7 3.3 %grad_normed.4 = f32[96,1280]{1,0:T(8,128)S(1)} custom-call(s32[1]{0:T(128)} %bitcast.places._, bf16[96,2048]{1,0:T(8,128)(2,1)S(1)} %get-tuple-element.128.refs_0_, bf16[8192,1280]{1,0:T(8,128)(2,1)} %refs_2_.1), custom_call_target="tpu_custom_call" | custom-call | tf_op jit(solution)/shard_map/grad_normed/pallas_call | solution.py:302
  112.0 0.8 copy-done.4
  112.8 2.1 %collective-permute-start.21 = (f32[4,96]{1,0:T(4,128)S(1)}, f32[4,96]{1,0:T(4,128)S(1)}, u32[]{:S(2)}, u32[]{:S(2)}) collective-permute-start(f32[4,96]{1,0:T(4,128)S(1)} %pad_maximum_fusion.3), channel_id=1, source_target_pairs={{0,6},{2,4},{4,2},{6,0},{1,7},{3,5},{5,3},{7,1},{8,14},{10,12},{12... | collective-permute-start | bytes 4616 | tf_op jit(solution)/shard_map/grad_normed/ppermute | solution.py:36
  114.9 2.4 %collective-permute-start.19 = (f32[4,96]{1,0:T(4,128)S(1)}, f32[4,96]{1,0:T(4,128)S(1)}, u32[]{:S(2)}, u32[]{:S(2)}) collective-permute-start(f32[4,96]{1,0:T(4,128)S(1)} %pad_maximum_fusion.3), channel_id=1, source_target_pairs={{0,2},{2,0},{4,6},{6,4},{1,3},{3,1},{5,7},{7,5},{8,10},{10,8},{12,... | collective-permute-start | bytes 4616 | tf_op jit(solution)/shard_map/grad_normed/ppermute | solution.py:36
  117.3 7.9 %dynamic-slice_bitcast_fusion = (bf16[1280,1280]{1,0:T(8,128)(2,1)}, bf16[1280,1280]{1,0:T(8,128)(2,1)}, bf16[1280,1280]{1,0:T(8,128)(2,1)}) fusion(bf16[1,5120,1280]{2,1,0:T(8,128)(2,1)} %param.9, s32[]{:T(128)S(6)} %select_n.107, s32[]{:T(128)S(6)} %select_n.105, s32[]{:T(128)S(6)} %select_n.106), kind=kLoop, calls=%fused_computation | loop fusion | bytes 19660812 | tf_op jit(solution)/shard_map/grad_normed/dynamic_slice | solution.py:445
  125.2 0.6 collective-permute-done.21
  125.8 1.0 collective-permute-done.20
  126.9 0.8 copy-done.6
  127.6 0.7 collective-permute-start.23
  128.3 1.3 collective-permute-start.22
  129.6 0.6 pad_maximum_fusion.2.here
  130.7 0.6 iota_compare_fusion.5
  131.3 1.1 copy-done.7
  132.4 5.2 %grad_normed.5 = (f32[96,1280]{1,0:T(8,128)S(1)}, f32[96,1280]{1,0:T(8,128)S(1)}) custom-call(s32[1]{0:T(128)} %bitcast.places._, bf16[96,2048]{1,0:T(8,128)(2,1)S(1)} %copy-done.7, bf16[96,2048]{1,0:T(8,128)(2,1)} %collective-permute-done.17.refs_1_, bf16[8192,1280]{1,0:T(8,128)(2,1)} %refs_2_.1), custom_call_target="tpu_custom_call" | custom-call | tf_op jit(solution)/shard_map/grad_normed/pallas_call | solution.py:302
  137.6 2.5 %collective-permute-done.22.outer = bf16[96,2048]{1,0:T(8,128)(2,1)} collective-permute-done((bf16[96,2048]{1,0:T(8,128)(2,1)}, bf16[96,2048]{1,0:T(8,128)(2,1)}, u32[]{:S(2)}, u32[]{:S(2)}) %collective-permute-start.22) | collective-permute-done | bytes 393248 | tf_op jit(solution)/shard_map/grad_normed/ppermute | solution.py:531
  140.1 0.7 grad_normed.6
  141.0 2.0 %grad_normed.7 = f32[96,1280]{1,0:T(8,128)S(1)} custom-call(s32[1]{0:T(128)} %bitcast.places._, bf16[96,2048]{1,0:T(8,128)(2,1)} %collective-permute-done.22.outer, bf16[96,2048]{1,0:T(8,128)(2,1)S(1)} %collective-permute-done.23.inner, bf16[2048,1280]{1,0:T(8,128)(2,1)S(1)} %bitcast.83), custom_call_target="tpu_custom_call" | custom-call | tf_op jit(solution)/shard_map/grad_normed/pallas_call | solution.py:61
  143.9 1.9 fusion.10
  146.0 1.0 dynamic-slice_bitcast_fusion.3
  147.0 2.5 %collective-permute-done.25 = bf16[96,1280]{1,0:T(8,128)(2,1)S(1)} collective-permute-done((bf16[96,1280]{1,0:T(8,128)(2,1)S(1)}, bf16[96,1280]{1,0:T(8,128)(2,1)S(1)}, u32[]{:S(2)}, u32[]{:S(2)}) %collective-permute-start.25) | collective-permute-done | bytes 245792 | tf_op jit(solution)/shard_map/grad_normed/ppermute | solution.py:40
  150.2 1.9 joined_grad.4
  152.0 1.8 collective-permute-start.26
  153.8 2.8 %joined_grad.5 = (bf16[96,1408]{1,0:T(8,128)(2,1)}, bf16[96,1408]{1,0:T(8,128)(2,1)}) custom-call(s32[1]{0:T(128)} %bitcast.places._, bf16[96,1280]{1,0:T(8,128)(2,1)S(1)} %get-tuple-element.145.left, bf16[1280,1280]{1,0:T(8,128)(2,1)S(1)} %copy-done.2, bf16[1280,1280]{1,0:T(8,128)(2,1)S(1)} %copy-done.1, ...), custom_call_target="tpu_custom_call" | custom-call | tf_op jit(solution)/shard_map/joined_grad/pallas_call | solution.py:61
  157.2 2.0 %collective-permute-start.29 = (bf16[96,1408]{1,0:T(8,128)(2,1)}, bf16[96,1408]{1,0:T(8,128)(2,1)}, u32[]{:S(2)}, u32[]{:S(2)}) collective-permute-start(bf16[96,1408]{1,0:T(8,128)(2,1)} %get-tuple-element.149), channel_id=1, source_target_pairs={{0,2},{2,0},{4,6},{6,4},{1,3},{3,1},{5,7},{7,5},{8,10},{10,8},{12,... | collective-permute-start | bytes 811016 | tf_op jit(solution)/shard_map/joined_grad/ppermute | solution.py:36
  159.3 1.5 collective-permute-start.31
  160.9 9.9 %joined_grad.7 = f32[5120,1280]{1,0:T(8,128)} custom-call(s32[1]{0:T(128)} %bitcast.places._, bf16[96,1280]{1,0:T(8,128)(2,1)S(1)} %get-tuple-element.92.own, bf16[3,96,1280]{2,1,0:T(8,128)(2,1)S(1)} %copy-done.9, bf16[96,1280]{1,0:T(8,128)(2,1)S(1)} %get-tuple-element.173.grad), custom_call_target="tpu_custom_call" | custom-call | tf_op jit(solution)/shard_map/joined_grad/pallas_call | solution.py:334
  170.8 2.9 %joined_grad.6.side = f32[96,1280]{1,0:T(8,128)S(1)} custom-call(s32[1]{0:T(128)} %bitcast.places._, bf16[96,1280]{1,0:T(8,128)(2,1)S(1)} %get-tuple-element.145.left, bf16[5120,1280]{1,0:T(8,128)(2,1)} %bitcast.90), custom_call_target="tpu_custom_call" | custom-call | tf_op jit(solution)/shard_map/joined_grad/pallas_call | solution.py:275
  173.8 5.1 %collective-permute-done.28.refs_1_ = bf16[96,1408]{1,0:T(8,128)(2,1)} collective-permute-done((bf16[96,1408]{1,0:T(8,128)(2,1)}, bf16[96,1408]{1,0:T(8,128)(2,1)}, u32[]{:S(2)}, u32[]{:S(2)}) %collective-permute-start.28) | collective-permute-done | bytes 270368 | tf_op jit(solution)/shard_map/joined_grad/ppermute | solution.py:36
  178.9 1.4 input_grads.3
  180.3 1.6 collective-permute-start.30
  182.0 3.4 %input_grads.4.refs_8_ = f32[2048,1280]{1,0:T(8,128)} custom-call(bf16[96,2048]{1,0:T(8,128)(2,1)S(1)} %get-tuple-element.158.refs_0_, bf16[96,2048]{1,0:T(8,128)(2,1)S(1)} %collective-permute-done.27.refs_1_, bf16[96,2048]{1,0:T(8,128)(2,1)S(1)} %collective-permute-done.31.refs_2_, bf16[96,2048]{1,0:T(8,128)(2,1)S(1)} %collective-permute-done.32.refs_3_, ...), custom_call_target="tpu_custom_call" | custom-call | tf_op jit(solution)/shard_map/input_grads/pallas_call | solution.py:367
  185.5 1.3 collective-permute-done.33
  186.8 1.6 collective-permute-start.34
  188.4 0.7 fusion.12
  189.1 3.4 %input_grads.5 = f32[2048,1280]{1,0:T(8,128)} custom-call(bf16[96,2048]{1,0:T(8,128)(2,1)S(1)} %get-tuple-element.158.refs_0_, bf16[96,2048]{1,0:T(8,128)(2,1)S(1)} %collective-permute-done.27.refs_1_, bf16[96,2048]{1,0:T(8,128)(2,1)S(1)} %collective-permute-done.31.refs_2_, ...), custom_call_target="tpu_custom_call", output_to_operand_aliasing={{}: (8, {})} | custom-call | tf_op jit(solution)/shard_map/input_grads/pallas_call | solution.py:367
  192.5 0.7 convert_add_fusion
  (124 shorter events, 6.2 us)
Async XLA Ops:
  1.6 7.7 %collective-permute-start.3 = (bf16[48,1280]{1,0:T(8,128)(2,1)S(1)}, bf16[48,1280]{1,0:T(8,128)(2,1)S(1)}, u32[]{:S(2)}, u32[]{:S(2)}) collective-permute-start(bf16[48,1280]{1,0:T(8,128)(2,1)S(1)} %get-tuple-element.193), channel_id=1, source_target_pairs={{0,1},{1,0},{2,3},{3,2},{4,5},{5,4},{6,7},{7,6},{8,9},{9,8},{10,11... | collective-permute-start | bytes 368648 | tf_op jit(solution)/shard_map/inputs/ppermute | solution.py:40
  4.7 8.2 %collective-permute-start.2 = (bf16[48,1280]{1,0:T(8,128)(2,1)S(1)}, bf16[48,1280]{1,0:T(8,128)(2,1)S(1)}, u32[]{:S(2)}, u32[]{:S(2)}) collective-permute-start(bf16[48,1280]{1,0:T(8,128)(2,1)S(1)} %get-tuple-element.88.kept), channel_id=1, source_target_pairs={{0,6},{2,4},{4,2},{6,0},{1,7},{3,5},{5,3},{7,1},{8,14},{10,12},{12... | collective-permute-start | bytes 368648 | tf_op jit(solution)/shard_map/inputs/ppermute | solution.py:36
  8.3 10.1 %collective-permute-start.1 = (bf16[48,1280]{1,0:T(8,128)(2,1)S(1)}, bf16[48,1280]{1,0:T(8,128)(2,1)S(1)}, u32[]{:S(2)}, u32[]{:S(2)}) collective-permute-start(bf16[48,1280]{1,0:T(8,128)(2,1)S(1)} %get-tuple-element.88.kept), channel_id=1, source_target_pairs={{0,4},{2,6},{4,0},{6,2},{1,5},{3,7},{5,1},{7,3},{8,12},{10,14},{12... | collective-permute-start | bytes 368648 | tf_op jit(solution)/shard_map/inputs/ppermute | solution.py:36
  8.3 10.1 %collective-permute-start = (bf16[48,1280]{1,0:T(8,128)(2,1)S(1)}, bf16[48,1280]{1,0:T(8,128)(2,1)S(1)}, u32[]{:S(2)}, u32[]{:S(2)}) collective-permute-start(bf16[48,1280]{1,0:T(8,128)(2,1)S(1)} %get-tuple-element.88.kept), channel_id=1, source_target_pairs={{0,2},{2,0},{4,6},{6,4},{1,3},{3,1},{5,7},{7,5},{8,10},{10,8},{12,... | collective-permute-start | bytes 368648 | tf_op jit(solution)/shard_map/inputs/ppermute | solution.py:36
  9.0 16.2 %collective-permute-start.7 = (bf16[48,1280]{1,0:T(8,128)(2,1)}, bf16[48,1280]{1,0:T(8,128)(2,1)S(1)}, u32[]{:S(2)}, u32[]{:S(2)}) collective-permute-start(bf16[48,1280]{1,0:T(8,128)(2,1)} %param.7), channel_id=1, source_target_pairs={{0,1},{1,0},{2,3},{3,2},{4,5},{5,4},{6,7},{7,6},{8,9},{9,8},{10,11... | collective-permute-start | bytes 368648 | tf_op jit(solution)/shard_map/inputs/ppermute | solution.py:40
  18.4 8.1 %collective-permute-start.6 = (bf16[48,1280]{1,0:T(8,128)(2,1)S(1)}, bf16[48,1280]{1,0:T(8,128)(2,1)S(1)}, u32[]{:S(2)}, u32[]{:S(2)}) collective-permute-start(bf16[48,1280]{1,0:T(8,128)(2,1)S(1)} %collective-permute-done.3.given), channel_id=1, source_target_pairs={{0,6},{2,4},{4,2},{6,0},{1,7},{3,5},{5,3},{7,1},{8,14},{10,12},{12... | collective-permute-start | bytes 368648 | tf_op jit(solution)/shard_map/inputs/ppermute | solution.py:36
  21.1 9.5 %collective-permute-start.5 = (bf16[48,1280]{1,0:T(8,128)(2,1)S(1)}, bf16[48,1280]{1,0:T(8,128)(2,1)S(1)}, u32[]{:S(2)}, u32[]{:S(2)}) collective-permute-start(bf16[48,1280]{1,0:T(8,128)(2,1)S(1)} %collective-permute-done.3.given), channel_id=1, source_target_pairs={{0,4},{2,6},{4,0},{6,2},{1,5},{3,7},{5,1},{7,3},{8,12},{10,14},{12... | collective-permute-start | bytes 368648 | tf_op jit(solution)/shard_map/inputs/ppermute | solution.py:36
  21.1 9.5 %collective-permute-start.4 = (bf16[48,1280]{1,0:T(8,128)(2,1)S(1)}, bf16[48,1280]{1,0:T(8,128)(2,1)S(1)}, u32[]{:S(2)}, u32[]{:S(2)}) collective-permute-start(bf16[48,1280]{1,0:T(8,128)(2,1)S(1)} %collective-permute-done.3.given), channel_id=1, source_target_pairs={{0,2},{2,0},{4,6},{6,4},{1,3},{3,1},{5,7},{7,5},{8,10},{10,8},{12,... | collective-permute-start | bytes 368648 | tf_op jit(solution)/shard_map/inputs/ppermute | solution.py:36
  35.1 15.8 %copy-start.10 = (f32[96,1]{1,0:T(8,128)}, f32[96,1]{1,0:T(8,128)S(1)}, u32[]{:S(2)}) copy-start(f32[96,1]{1,0:T(8,128)S(1)} %get-tuple-element.115.in_scale) | copy-start | bytes 1156
  35.2 7.4 %copy-start.21 = (bf16[48,1280]{1,0:T(8,128)(2,1)S(1)}, bf16[48,1280]{1,0:T(8,128)(2,1)}, u32[]{:S(2)}) copy-start(bf16[48,1280]{1,0:T(8,128)(2,1)} %param.7) | copy-start | bytes 368644
  35.2 7.6 %copy-start.22 = (f32[1280]{0:T(1024)S(1)}, f32[1280]{0:T(1024)}, u32[]{:S(2)}) copy-start(f32[1280]{0:T(1024)} %param.10) | copy-start | bytes 15364
  35.2 7.3 %collective-permute-start.8 = (bf16[96,1280]{1,0:T(8,128)(2,1)S(1)}, bf16[96,1280]{1,0:T(8,128)(2,1)S(1)}, u32[]{:S(2)}, u32[]{:S(2)}) collective-permute-start(bf16[96,1280]{1,0:T(8,128)(2,1)S(1)} %get-tuple-element.103), channel_id=1, source_target_pairs={{0,1},{1,0},{2,3},{3,2},{4,5},{5,4},{6,7},{7,6},{8,9},{9,8},{10,11... | collective-permute-start | bytes 737288 | tf_op jit(solution)/shard_map/projection/ppermute | solution.py:40
  38.6 5.9 %copy-start = (bf16[2048,1280]{1,0:T(8,128)(2,1)}, bf16[2048,1280]{1,0:T(8,128)(2,1)S(1)}, u32[]{:S(2)}) copy-start(bf16[2048,1280]{1,0:T(8,128)(2,1)S(1)} %constant_dynamic-slice_fusion.refs_0_.right) | copy-start | bytes 15728644
  42.7 1.8 copy-start.15
  42.8 8.1 %copy-start.29 = (s32[1,96]{1,0:T(1,128)S(1)}, s32[1,96]{1,0:T(1,128)}, u32[]{:S(2)}) copy-start(s32[1,96]{1,0:T(1,128)} %param.12) | copy-start | bytes 1156
  44.5 18.9 %collective-permute-start.10 = (f32[96,2048]{1,0:T(8,128)S(1)}, f32[96,2048]{1,0:T(8,128)S(1)}, u32[]{:S(2)}, u32[]{:S(2)}) collective-permute-start(f32[96,2048]{1,0:T(8,128)S(1)} %logits.4), channel_id=1, source_target_pairs={{2,4},{4,2},{3,5},{5,3},{10,12},{12,10},{11,13},{13,11},{18,20},{2... | collective-permute-start | bytes 2359304 | tf_op jit(solution)/shard_map/logits/ppermute | solution.py:479
  45.2 18.2 %collective-permute-start.9 = (f32[96,2048]{1,0:T(8,128)S(1)}, f32[96,2048]{1,0:T(8,128)}, u32[]{:S(2)}, u32[]{:S(2)}) collective-permute-start(f32[96,2048]{1,0:T(8,128)S(1)} %logits.4), channel_id=1, source_target_pairs={{0,2},{6,4},{1,3},{7,5},{8,10},{14,12},{9,11},{15,13},{16,18},{22,... | collective-permute-start | bytes 2359304 | tf_op jit(solution)/shard_map/logits/ppermute | solution.py:478
  49.4 14.0 %collective-permute-start.11 = (bf16[96,1280]{1,0:T(8,128)(2,1)S(1)}, bf16[96,1280]{1,0:T(8,128)(2,1)S(1)}, u32[]{:S(2)}, u32[]{:S(2)}) collective-permute-start(bf16[96,1280]{1,0:T(8,128)(2,1)S(1)} %multiply_convert_fusion.1.left.refs_4_), channel_id=1, source_target_pairs={{0,16},{8,24},{16,0},{24,8},{1,17},{9,25},{17,1},{25,9},{2,18},{10... | collective-permute-start | bytes 737288 | tf_op jit(solution)/shard_map/logits/ppermute | solution.py:36
  50.9 54.9 %copy-start.24 = (s32[96,1]{0,1:T(1,128)}, s32[96,1]{0,1:T(1,128)S(1)}, u32[]{:S(2)}) copy-start(s32[96,1]{0,1:T(1,128)S(1)} %subtract_bitcast_fusion.4) | copy-start | bytes 1156
  50.9 12.5 %collective-permute-start.12 = (f32[96]{0:T(128)S(1)}, f32[96]{0:T(128)S(1)}, u32[]{:S(2)}, u32[]{:S(2)}) collective-permute-start(f32[96]{0:T(128)S(1)} %get-tuple-element.182), channel_id=1, source_target_pairs={{0,2},{2,0},{4,6},{6,4},{1,3},{3,1},{5,7},{7,5},{8,10},{10,8},{12,... | collective-permute-start | bytes 1160 | tf_op jit(solution)/shard_map/logits/ppermute | solution.py:36
  63.4 7.4 %copy-start.17 = (f32[96,2048]{1,0:T(8,128)}, f32[96,2048]{1,0:T(8,128)S(1)}, u32[]{:S(2)}) copy-start(f32[96,2048]{1,0:T(8,128)S(1)} %collective-permute-done.10) | copy-start | bytes 2359300
  63.4 18.9 %collective-permute-start.16 = (f32[2,96]{1,0:T(2,128)S(1)}, f32[2,96]{1,0:T(2,128)S(1)}, u32[]{:S(2)}, u32[]{:S(2)}) collective-permute-start(f32[2,96]{1,0:T(2,128)S(1)} %pad_maximum_fusion.4), channel_id=1, source_target_pairs={{0,4},{2,6},{4,0},{6,2},{1,5},{3,7},{5,1},{7,3},{8,12},{10,14},{12... | collective-permute-start | bytes 2312 | tf_op jit(solution)/shard_map/logits/ppermute | solution.py:36
  66.5 15.9 %collective-permute-start.15 = (bf16[2,96,1280]{2,1,0:T(8,128)(2,1)S(1)}, bf16[2,96,1280]{2,1,0:T(8,128)(2,1)S(1)}, u32[]{:S(2)}, u32[]{:S(2)}) collective-permute-start(bf16[2,96,1280]{2,1,0:T(8,128)(2,1)S(1)} %pad_maximum_fusion.1), channel_id=1, source_target_pairs={{0,8},{8,0},{16,24},{24,16},{1,9},{9,1},{17,25},{25,17},{2,10},{10... | collective-permute-start | bytes 1474568 | tf_op jit(solution)/shard_map/logits/ppermute | solution.py:36
  67.8 37.2 %collective-permute-start.13 = (f32[96,2048]{1,0:T(8,128)S(1)}, f32[96,2048]{1,0:T(8,128)S(1)}, u32[]{:S(2)}, u32[]{:S(2)}) collective-permute-start(f32[96,2048]{1,0:T(8,128)S(1)} %add.126), channel_id=1, source_target_pairs={{0,4},{2,6},{4,0},{6,2},{1,5},{3,7},{5,1},{7,3},{8,12},{10,14},{12... | collective-permute-start | bytes 2359304 | tf_op jit(solution)/shard_map/logits/ppermute | solution.py:36
  67.9 37.3 %collective-permute-start.14 = (f32[96,2048]{1,0:T(8,128)S(1)}, f32[96,2048]{1,0:T(8,128)S(1)}, u32[]{:S(2)}, u32[]{:S(2)}) collective-permute-start(f32[96,2048]{1,0:T(8,128)S(1)} %get-tuple-element.111), channel_id=1, source_target_pairs={{0,2},{2,0},{4,6},{6,4},{1,3},{3,1},{5,7},{7,5},{8,10},{10,8},{12,... | collective-permute-start | bytes 2359304 | tf_op jit(solution)/shard_map/logits/ppermute | solution.py:36
  74.3 31.0 %copy-start.18 = (f32[96,2048]{1,0:T(8,128)S(1)}, f32[96,2048]{1,0:T(8,128)}, u32[]{:S(2)}) copy-start(f32[96,2048]{1,0:T(8,128)} %copy-done.17) | copy-start | bytes 2359300
  82.4 22.8 %copy-start.19 = (bf16[2,96,1280]{2,1,0:T(8,128)(2,1)}, bf16[2,96,1280]{2,1,0:T(8,128)(2,1)S(1)}, u32[]{:S(2)}) copy-start(bf16[2,96,1280]{2,1,0:T(8,128)(2,1)S(1)} %collective-permute-done.15) | copy-start | bytes 1474564
  106.2 20.6 %collective-permute-start.18 = (bf16[96,2048]{1,0:T(8,128)(2,1)S(1)}, bf16[96,2048]{1,0:T(8,128)(2,1)S(1)}, u32[]{:S(2)}, u32[]{:S(2)}) collective-permute-start(bf16[96,2048]{1,0:T(8,128)(2,1)S(1)} %get-tuple-element.128.refs_0_), channel_id=1, source_target_pairs={{0,2},{2,0},{4,6},{6,4},{1,3},{3,1},{5,7},{7,5},{8,10},{10,8},{12,... | collective-permute-start | bytes 1179656 | tf_op jit(solution)/shard_map/grad_normed/ppermute | solution.py:36
  106.3 21.3 %collective-permute-start.17 = (bf16[96,2048]{1,0:T(8,128)(2,1)S(1)}, bf16[96,2048]{1,0:T(8,128)(2,1)}, u32[]{:S(2)}, u32[]{:S(2)}) collective-permute-start(bf16[96,2048]{1,0:T(8,128)(2,1)S(1)} %get-tuple-element.128.refs_0_), channel_id=1, source_target_pairs={{0,4},{2,6},{4,0},{6,2},{1,5},{3,7},{5,1},{7,3},{8,12},{10,14},{12... | collective-permute-start | bytes 1179656 | tf_op jit(solution)/shard_map/grad_normed/ppermute | solution.py:36
  112.8 13.0 %collective-permute-start.21 = (f32[4,96]{1,0:T(4,128)S(1)}, f32[4,96]{1,0:T(4,128)S(1)}, u32[]{:S(2)}, u32[]{:S(2)}) collective-permute-start(f32[4,96]{1,0:T(4,128)S(1)} %pad_maximum_fusion.3), channel_id=1, source_target_pairs={{0,6},{2,4},{4,2},{6,0},{1,7},{3,5},{5,3},{7,1},{8,14},{10,12},{12... | collective-permute-start | bytes 4616 | tf_op jit(solution)/shard_map/grad_normed/ppermute | solution.py:36
  114.9 11.9 %collective-permute-start.20 = (f32[4,96]{1,0:T(4,128)S(1)}, f32[4,96]{1,0:T(4,128)S(1)}, u32[]{:S(2)}, u32[]{:S(2)}) collective-permute-start(f32[4,96]{1,0:T(4,128)S(1)} %pad_maximum_fusion.3), channel_id=1, source_target_pairs={{0,4},{2,6},{4,0},{6,2},{1,5},{3,7},{5,1},{7,3},{8,12},{10,14},{12... | collective-permute-start | bytes 4616 | tf_op jit(solution)/shard_map/grad_normed/ppermute | solution.py:36
  114.9 11.9 %collective-permute-start.19 = (f32[4,96]{1,0:T(4,128)S(1)}, f32[4,96]{1,0:T(4,128)S(1)}, u32[]{:S(2)}, u32[]{:S(2)}) collective-permute-start(f32[4,96]{1,0:T(4,128)S(1)} %pad_maximum_fusion.3), channel_id=1, source_target_pairs={{0,2},{2,0},{4,6},{6,4},{1,3},{3,1},{5,7},{7,5},{8,10},{10,8},{12,... | collective-permute-start | bytes 4616 | tf_op jit(solution)/shard_map/grad_normed/ppermute | solution.py:36
  127.6 10.0 %collective-permute-start.23 = (bf16[96,2048]{1,0:T(8,128)(2,1)S(1)}, bf16[96,2048]{1,0:T(8,128)(2,1)S(1)}, u32[]{:S(2)}, u32[]{:S(2)}) collective-permute-start(bf16[96,2048]{1,0:T(8,128)(2,1)S(1)} %get-tuple-element.128.refs_0_), channel_id=1, source_target_pairs={{2,4},{4,2},{3,5},{5,3},{10,12},{12,10},{11,13},{13,11},{18,20},{2... | collective-permute-start | bytes 1179656 | tf_op jit(solution)/shard_map/grad_normed/ppermute | solution.py:532
  128.3 11.8 %collective-permute-start.22 = (bf16[96,2048]{1,0:T(8,128)(2,1)}, bf16[96,2048]{1,0:T(8,128)(2,1)}, u32[]{:S(2)}, u32[]{:S(2)}) collective-permute-start(bf16[96,2048]{1,0:T(8,128)(2,1)} %collective-permute-done.17.refs_1_), channel_id=1, source_target_pairs={{4,6},{2,0},{5,7},{3,1},{12,14},{10,8},{13,15},{11,9},{20,22},{18,... | collective-permute-start | bytes 1179656 | tf_op jit(solution)/shard_map/grad_normed/ppermute | solution.py:531
  130.2 7.4 %collective-permute-start.24 = (f32[4,4,96]{2,1,0:T(4,128)}, f32[4,4,96]{2,1,0:T(4,128)}, u32[]{:S(2)}, u32[]{:S(2)}) collective-permute-start(f32[4,4,96]{2,1,0:T(4,128)} %pad_maximum_fusion.2.here), channel_id=1, source_target_pairs={{0,1},{1,0},{2,3},{3,2},{4,5},{5,4},{6,7},{7,6},{8,9},{9,8},{10,11... | collective-permute-start | bytes 18440 | tf_op jit(solution)/shard_map/grad_normed/ppermute | solution.py:40
  131.3 9.6 %slice-start = ((s8[5242880]{0:T(1024)(128)(4,1)}), s8[1048576]{0:T(1024)(128)(4,1)S(1)}, s32[]{:S(2)}) async-start(s8[5242880]{0:T(1024)(128)(4,1)} %bitcast.82), calls=%async_computation | async-start | bytes 2097152
  131.3 1.1 copy-start.7
  132.4 7.7 %copy-start.13 = (f32[1,96]{1,0:T(1,128)S(1)}, f32[1,96]{1,0:T(1,128)}, u32[]{:S(2)}) copy-start(f32[1,96]{1,0:T(1,128)} %copy-done.12) | copy-start | bytes 1156
  132.4 7.7 %copy-start.14 = (f32[1,96]{1,0:T(1,128)S(1)}, f32[1,96]{1,0:T(1,128)}, u32[]{:S(2)}) copy-start(f32[1,96]{1,0:T(1,128)} %weights.1) | copy-start | bytes 1156
  132.4 8.5 %slice-start.1 = ((s8[5242880]{0:T(1024)(128)(4,1)}), s8[4194304]{0:T(1024)(128)(4,1)S(1)}, s32[]{:S(2)}) async-start(s8[5242880]{0:T(1024)(128)(4,1)} %bitcast.82), calls=%async_computation.1 | async-start | bytes 8388608
  140.9 2.1 %copy-start.5 = (f32[96,1280]{1,0:T(8,128)S(1)}, f32[96,1280]{1,0:T(8,128)}, u32[]{:S(2)}) copy-start(f32[96,1280]{1,0:T(8,128)} %copy-done.4) | copy-start | bytes 1474564
  140.9 2.9 %copy-start.25 = (s32[96,1]{0,1:T(1,128)S(1)}, s32[96,1]{0,1:T(1,128)}, u32[]{:S(2)}) copy-start(s32[96,1]{0,1:T(1,128)} %copy-done.24) | copy-start | bytes 1156
  140.9 2.9 %copy-start.8 = (bf16[96,2048]{1,0:T(8,128)(2,1)S(1)}, bf16[96,2048]{1,0:T(8,128)(2,1)}, u32[]{:S(2)}) copy-start(bf16[96,2048]{1,0:T(8,128)(2,1)} %copy-done.6) | copy-start | bytes 1179652
  143.3 6.3 %collective-permute-start.25 = (bf16[96,1280]{1,0:T(8,128)(2,1)S(1)}, bf16[96,1280]{1,0:T(8,128)(2,1)S(1)}, u32[]{:S(2)}, u32[]{:S(2)}) collective-permute-start(bf16[96,1280]{1,0:T(8,128)(2,1)S(1)} %get-tuple-element.177), channel_id=1, source_target_pairs={{0,1},{1,0},{2,3},{3,2},{4,5},{5,4},{6,7},{7,6},{8,9},{9,8},{10,11... | collective-permute-start | bytes 737288 | tf_op jit(solution)/shard_map/grad_normed/ppermute | solution.py:40
  145.8 3.8 %copy-start.16 = (f32[96,1280]{1,0:T(8,128)S(1)}, f32[96,1280]{1,0:T(8,128)}, u32[]{:S(2)}) copy-start(f32[96,1280]{1,0:T(8,128)} %copy-done.15) | copy-start | bytes 1474564
  145.8 3.8 %copy-start.23 = (f32[1280]{0:T(1024)S(1)}, f32[1280]{0:T(1024)}, u32[]{:S(2)}) copy-start(f32[1280]{0:T(1024)} %param.10) | copy-start | bytes 15364
  145.8 3.8 %copy-start.26 = (f32[96]{0:T(128)S(1)}, f32[96]{0:T(128)}, u32[]{:S(2)}) copy-start(f32[96]{0:T(128)} %reduce) | copy-start | bytes 1156
  146.0 4.0 %copy-start.27 = (pred[128]{0:T(512)(128)(4,1)S(1)}, pred[128]{0:T(512)(128)(4,1)}, u32[]{:S(2)}) copy-start(pred[128]{0:T(512)(128)(4,1)} %get-tuple-element.215) | copy-start | bytes 388
  146.0 4.0 %copy-start.28 = (pred[128]{0:T(512)(128)(4,1)S(1)}, pred[128]{0:T(512)(128)(4,1)}, u32[]{:S(2)}) copy-start(pred[128]{0:T(512)(128)(4,1)} %get-tuple-element.216) | copy-start | bytes 388
  146.0 4.1 %copy-start.3 = (bf16[1280,1280]{1,0:T(8,128)(2,1)S(1)}, bf16[1280,1280]{1,0:T(8,128)(2,1)}, u32[]{:S(2)}) copy-start(bf16[1280,1280]{1,0:T(8,128)(2,1)} %get-tuple-element.143.refs_0_) | copy-start | bytes 9830404
  149.5 4.3 %copy-start.1 = (bf16[1280,1280]{1,0:T(8,128)(2,1)S(1)}, bf16[1280,1280]{1,0:T(8,128)(2,1)}, u32[]{:S(2)}) copy-start(bf16[1280,1280]{1,0:T(8,128)(2,1)} %get-tuple-element.147.refs_1_) | copy-start | bytes 9830404
  149.6 4.3 %copy-start.2 = (bf16[1280,1280]{1,0:T(8,128)(2,1)S(1)}, bf16[1280,1280]{1,0:T(8,128)(2,1)}, u32[]{:S(2)}) copy-start(bf16[1280,1280]{1,0:T(8,128)(2,1)} %get-tuple-element.146.refs_0_) | copy-start | bytes 9830404
  149.9 3.9 %collective-permute-start.27 = (bf16[96,2048]{1,0:T(8,128)(2,1)S(1)}, bf16[96,2048]{1,0:T(8,128)(2,1)S(1)}, u32[]{:S(2)}, u32[]{:S(2)}) collective-permute-start(bf16[96,2048]{1,0:T(8,128)(2,1)S(1)} %get-tuple-element.144), channel_id=1, source_target_pairs={{0,8},{8,0},{16,24},{24,16},{1,9},{9,1},{17,25},{25,17},{2,10},{10... | collective-permute-start | bytes 1179656 | tf_op jit(solution)/shard_map/joined_grad/ppermute | solution.py:36
  152.0 8.9 %copy-start.9 = (bf16[3,96,1280]{2,1,0:T(8,128)(2,1)S(1)}, bf16[3,96,1280]{2,1,0:T(8,128)(2,1)}, u32[]{:S(2)}) copy-start(bf16[3,96,1280]{2,1,0:T(8,128)(2,1)} %get-tuple-element.150.part) | copy-start | bytes 2211844
  152.0 21.7 %collective-permute-start.26 = (bf16[96,1408]{1,0:T(8,128)(2,1)}, bf16[96,1408]{1,0:T(8,128)(2,1)}, u32[]{:S(2)}, u32[]{:S(2)}) collective-permute-start(bf16[96,1408]{1,0:T(8,128)(2,1)} %joined_grad.4), channel_id=1, source_target_pairs={{0,6},{2,4},{4,2},{6,0},{1,7},{3,5},{5,3},{7,1},{8,14},{10,12},{12... | collective-permute-start | bytes 811016 | tf_op jit(solution)/shard_map/joined_grad/ppermute | solution.py:36
  156.6 22.2 %collective-permute-start.28 = (bf16[96,1408]{1,0:T(8,128)(2,1)}, bf16[96,1408]{1,0:T(8,128)(2,1)}, u32[]{:S(2)}, u32[]{:S(2)}) collective-permute-start(bf16[96,1408]{1,0:T(8,128)(2,1)} %get-tuple-element.148), channel_id=1, source_target_pairs={{0,4},{2,6},{4,0},{6,2},{1,5},{3,7},{5,1},{7,3},{8,12},{10,14},{12... | collective-permute-start | bytes 811016 | tf_op jit(solution)/shard_map/joined_grad/ppermute | solution.py:36
  157.2 21.7 %collective-permute-start.29 = (bf16[96,1408]{1,0:T(8,128)(2,1)}, bf16[96,1408]{1,0:T(8,128)(2,1)}, u32[]{:S(2)}, u32[]{:S(2)}) collective-permute-start(bf16[96,1408]{1,0:T(8,128)(2,1)} %get-tuple-element.149), channel_id=1, source_target_pairs={{0,2},{2,0},{4,6},{6,4},{1,3},{3,1},{5,7},{7,5},{8,10},{10,8},{12,... | collective-permute-start | bytes 811016 | tf_op jit(solution)/shard_map/joined_grad/ppermute | solution.py:36
  159.3 22.6 %collective-permute-start.31 = (bf16[96,2048]{1,0:T(8,128)(2,1)}, bf16[96,2048]{1,0:T(8,128)(2,1)S(1)}, u32[]{:S(2)}, u32[]{:S(2)}) collective-permute-start(bf16[96,2048]{1,0:T(8,128)(2,1)} %get-tuple-element.160), channel_id=1, source_target_pairs={{0,16},{8,24},{16,0},{24,8},{1,17},{9,25},{17,1},{25,9},{2,18},{10... | collective-permute-start | bytes 1179656 | tf_op jit(solution)/shard_map/joined_grad/ppermute | solution.py:36
  160.9 21.1 %collective-permute-start.32 = (bf16[96,2048]{1,0:T(8,128)(2,1)}, bf16[96,2048]{1,0:T(8,128)(2,1)S(1)}, u32[]{:S(2)}, u32[]{:S(2)}) collective-permute-start(bf16[96,2048]{1,0:T(8,128)(2,1)} %get-tuple-element.161), channel_id=1, source_target_pairs={{0,24},{8,16},{16,8},{24,0},{1,25},{9,17},{17,9},{25,1},{2,26},{10... | collective-permute-start | bytes 1179656 | tf_op jit(solution)/shard_map/joined_grad/ppermute | solution.py:36
  170.8 8.1 %copy-start.11 = (f32[96,1]{1,0:T(8,128)S(1)}, f32[96,1]{1,0:T(8,128)}, u32[]{:S(2)}) copy-start(f32[96,1]{1,0:T(8,128)} %copy-done.10) | copy-start | bytes 1156
  170.8 11.1 %copy-start.20 = (bf16[2,96,1280]{2,1,0:T(8,128)(2,1)S(1)}, bf16[2,96,1280]{2,1,0:T(8,128)(2,1)}, u32[]{:S(2)}) copy-start(bf16[2,96,1280]{2,1,0:T(8,128)(2,1)} %copy-done.19) | copy-start | bytes 1474564
  180.3 5.0 %collective-permute-start.30 = (bf16[48,1280]{1,0:T(8,128)(2,1)S(1)}, bf16[48,1280]{1,0:T(8,128)(2,1)S(1)}, u32[]{:S(2)}, u32[]{:S(2)}) collective-permute-start(bf16[48,1280]{1,0:T(8,128)(2,1)S(1)} %slice_select_fusion), channel_id=1, source_target_pairs={{0,1},{1,0},{2,3},{3,2},{4,5},{5,4},{6,7},{7,6},{8,9},{9,8},{10,11... | collective-permute-start | bytes 368648 | tf_op jit(solution)/shard_map/input_grads/ppermute | solution.py:40
  185.4 1.4 collective-permute-start.33
  186.8 5.6 %collective-permute-start.34 = (bf16[48,1280]{1,0:T(8,128)(2,1)S(1)}, bf16[48,1280]{1,0:T(8,128)(2,1)S(1)}, u32[]{:S(2)}, u32[]{:S(2)}) collective-permute-start(bf16[48,1280]{1,0:T(8,128)(2,1)S(1)} %add_convert_fusion), channel_id=1, source_target_pairs={{0,16},{8,24},{16,0},{24,8},{1,17},{9,25},{17,1},{25,9},{2,18},{10... | collective-permute-start | bytes 368648 | tf_op jit(solution)/shard_map/input_grads/ppermute | solution.py:36
  (3 other events, 2.1 us)
